TPU v7x, 32 devices: a whole 2x2x4 slice. The times are simulated.
32 devices in a mesh: blocks: 8 (over z, y), rows: 4 (over x, core).
Axes of the slice: x: 2, y: 2, z: 4, core: 2. Of those that a mesh axis runs over, the one named last changes fastest.
Arguments:
- hidden_in: bfloat16 [8, 512, 768], P('blocks', 'rows'), may hold values from -6 to 6
- positions: bfloat16 [8, 3, 512], P('blocks', None, 'rows'), may hold values from -8 to 8
- atom_types: int32 [8, 512], P('blocks', 'rows'), may hold values from 0 to 511
- path_hops: int32 [8, 512, 512], P('blocks', 'rows'), may hold values from 0 to 511
- edge_kinds: int32 [8, 512, 512], P('blocks', 'rows'), may hold values from 0 to 1535
- mol_lengths: int32 [8, 16], P('blocks'), may hold values from 1 to 96, 512 in all within a row
- qkv_weight: bfloat16 [768, 2304], replicated, may hold values from -0.21875 to 0.21875
- out_weight: bfloat16 [768, 768], replicated, may hold values from -0.625 to 0.625
- attn_gain: float32 [768], replicated, may hold values from 0.5 to 1.5
- ffn_gain: float32 [768], replicated, may hold values from 0.5 to 1.5
- up_weight: bfloat16 [768, 768], replicated, may hold values from -0.21875 to 0.21875
- down_weight: bfloat16 [768, 768], replicated, may hold values from -0.21875 to 0.21875
- kernel_means: float32 [128], replicated, may hold values from 0 to 10
- kernel_widths: float32 [128], replicated, may hold values from 0.5 to 3
- kernel_inner: bfloat16 [128, 128], replicated, may hold values from -2 to 2
- kernel_outer: bfloat16 [128, 32], replicated, may hold values from -0.5 to 0.5
- hop_table: bfloat16 [32, 512], replicated, may hold values from -3 to 3
- edge_table: bfloat16 [32, 1536], replicated, may hold values from -3 to 3
- atom_scale: float32 [512], replicated, may hold values from 0.3 to 0.7
- atom_shift: float32 [512], replicated, may hold values from -0.5 to 0.5
- out_grad: bfloat16 [8, 512, 768], P('blocks', 'rows'), may hold values from -6 to 6
Outputs:
- layer_out: bfloat16 [8, 512, 768], P('blocks', 'rows')
- grad_in: float32 [8, 512, 768], P('blocks', 'rows')
- grad_qkv: float32 [768, 2304], replicated
- grad_out_weight: float32 [768, 768], replicated
- grad_attn_gain: float32 [768], replicated
- grad_ffn_gain: float32 [768], replicated
- grad_up: float32 [768, 768], replicated
- grad_down: float32 [768, 768], replicated
- grad_means: float32 [128], replicated
- grad_widths: float32 [128], replicated
- grad_inner: float32 [128, 128], replicated
- grad_outer: float32 [128, 32], replicated
- grad_hops: float32 [32, 512], replicated
- grad_edges: float32 [32, 1536], replicated
- grad_atom_scale: float32 [512], replicated
- grad_atom_shift: float32 [512], replicated
Inputs may be any that keep to these rules, and one draw needn't show every extreme that they name: `mol_lengths`: each block's 16 molecule lengths sum to 512; the largest of every block is exactly 96.
All inputs are finite; a program needn't handle non-finite values.
Results may differ from a plain program's by a relative error of at most 0.01225.
The roundings to bfloat16 on the way count: a program that leaves them out, or rounds other values in their place, can miss the bound.
Values may be sent and summed in bfloat16 or wider, within the bound.
A program may use at most 192 MiB of HBM per device.

v0:
```python
import jax
import jax.numpy as jnp
from jax import lax
from jax.sharding import PartitionSpec as P

MOST = 96


EPS = 1e-05
NEG = -1000000000.0
SQRT_TWO_PI = 2.5066282746310002
CONTRACT_FIRST = (((0,), (0,)), ((), ()))
CONTRACT_LAST = (((1,), (1,)), ((), ()))


def with_halo(value, sides, width):
    for axis, dim in sides:
        devices, length = (lax.axis_size(axis), value.shape[dim])
        up = [(i, (i + 1) % devices) for i in range(devices - 1)]
        down = [(j, i) for i, j in up]
        last = lax.slice_in_dim(value, length - width, length, axis=dim)
        initial = lax.slice_in_dim(value, 0, width, axis=dim)
        before = lax.ppermute(last, axis, up)
        after = lax.ppermute(initial, axis, down)
        value = jnp.concatenate([before, value, after], axis=dim)
    return value


def passed_along(value, axis, steps):
    count = lax.axis_size(axis)
    initial, last = (max(0, -steps), min(count, count - steps))
    return lax.ppermute(value, axis, [(source, source + steps) for source in range(initial, last)])


def layer_norm(values, gain):
    centre = jnp.mean(values, axis=-1, keepdims=True)
    shifted = values - centre
    spread = jnp.mean(shifted * shifted, axis=-1, keepdims=True)
    return shifted * lax.rsqrt(spread + EPS) * gain


def gaussian(offset, kernel_means, kernel_widths):
    scaled = (offset[None] - kernel_means[:, None, None]) / kernel_widths[:, None, None]
    return jnp.exp(-0.5 * scaled * scaled) / (SQRT_TWO_PI * kernel_widths[:, None, None])


def pair_geometry(pos_query, pos_key, type_query, type_key):
    between = pos_query[:, :, None] - pos_key[:, None, :]
    distance = jnp.sqrt(jnp.sum(between * between, axis=0))
    offset = (
        (type_query[0][:, None] + type_key[0][None, :]) * distance
        + type_query[1][:, None]
        + type_key[1][None, :]
    )
    return (distance, offset)


def bias_from_features(features, hop_rows, edge_rows, bias_params):
    kernel_inner, kernel_outer, hop_table, edge_table = bias_params[2:]
    flat = features.reshape(features.shape[0], -1).astype(jnp.bfloat16)
    pre_act = lax.dot_general(
        kernel_inner, flat, CONTRACT_FIRST, preferred_element_type=jnp.float32
    )
    hidden = jax.nn.gelu(pre_act).astype(jnp.bfloat16)
    learned = lax.dot_general(
        kernel_outer, hidden, CONTRACT_FIRST, preferred_element_type=jnp.float32
    )
    table = jnp.take(hop_table, hop_rows.reshape(-1), axis=1).astype(jnp.float32) + jnp.take(
        edge_table, edge_rows.reshape(-1), axis=1
    ).astype(jnp.float32)
    pair_bias = (learned + table).reshape((kernel_outer.shape[1],) + hop_rows.shape)
    return (pair_bias, flat, pre_act, hidden)


def block_scores(block_in, pair_bias, width):
    query_b, keyval_b = (block_in[0], block_in[1])
    heads = pair_bias.shape[0]
    query_rows = query_b.reshape(query_b.shape[0], heads, -1)
    key_rows = keyval_b[:, :width].reshape(keyval_b.shape[0], heads, -1)
    value_rows = keyval_b[:, width:].reshape(keyval_b.shape[0], heads, -1)
    scaling = query_rows.shape[-1] ** (-0.5)
    raw = (
        jnp.einsum("rhe,lhe->hrl", query_rows, key_rows, preferred_element_type=jnp.float32)
        * scaling
    )
    visible = block_in[8][:, None] == block_in[9][None, :]
    scores = jnp.where(visible[None], raw + pair_bias, NEG)
    return (scores, query_rows, key_rows, value_rows, scaling)


def body(
    hidden_in,
    positions,
    atom_types,
    path_hops,
    edge_kinds,
    mol_lengths,
    qkv_weight,
    out_weight,
    attn_gain,
    ffn_gain,
    up_weight,
    down_weight,
    kernel_means,
    kernel_widths,
    kernel_inner,
    kernel_outer,
    hop_table,
    edge_table,
    atom_scale,
    atom_shift,
    out_grad,
):
    f32 = jnp.float32
    b16 = jnp.bfloat16
    block_count, row_count, width = hidden_in.shape
    block_total = row_count * lax.axis_size("rows")
    row_start = lax.axis_index("rows") * row_count
    token_rows = block_count * row_count
    kind_count = atom_scale.shape[0]
    heads = kernel_outer.shape[1]
    margin = MOST - 1
    bias_params = (kernel_means, kernel_widths, kernel_inner, kernel_outer, hop_table, edge_table)
    flat_in = hidden_in.astype(f32).reshape(token_rows, width)
    normed1 = layer_norm(flat_in, attn_gain).astype(b16)
    projected = (
        jnp.dot(normed1, qkv_weight, preferred_element_type=f32)
        .astype(b16)
        .reshape(block_count, row_count, 3 * width)
    )
    query_all = projected[..., :width]
    keyval_own = projected[..., width:]
    one_hot = (
        atom_types.reshape(-1)[:, None] == jnp.arange(kind_count, dtype=jnp.int32)[None, :]
    ).astype(f32)
    type_table = jnp.stack([atom_scale, atom_shift], axis=0)
    type_tokens = lax.dot_general(
        type_table, one_hot, CONTRACT_LAST, precision=lax.Precision.HIGHEST
    )
    type_own = type_tokens.reshape(2, block_count, row_count).transpose(1, 0, 2)
    pos_own = positions.astype(f32)
    ends = jnp.cumsum(mol_lengths, axis=1)

    def molecule_of(index):
        found = jnp.sum((index[None, :, None] >= ends[:, None, :]).astype(jnp.int32), axis=2)
        inside = (index >= 0) & (index < block_total)
        return jnp.where(inside[None, :], found, -1)

    keyval_all = with_halo(keyval_own, (("rows", 1),), margin)
    geometry = jnp.concatenate([pos_own.transpose(0, 2, 1), type_own.transpose(0, 2, 1)], axis=-1)
    geometry_all = with_halo(geometry, (("rows", 1),), margin)
    pos_all = geometry_all[..., :3].transpose(0, 2, 1)
    type_all = geometry_all[..., 3:].transpose(0, 2, 1)
    window_len = row_count + 2 * margin
    key_ids = row_start - margin + jnp.arange(window_len, dtype=jnp.int32)
    padding = ((0, 0), (0, 0), (margin, margin))
    hops_use = lax.dynamic_slice_in_dim(jnp.pad(path_hops, padding), row_start, window_len, 2)
    edges_use = lax.dynamic_slice_in_dim(jnp.pad(edge_kinds, padding), row_start, window_len, 2)
    key_count = key_ids.shape[0]
    mol_keys = molecule_of(key_ids)
    mol_own = molecule_of(row_start + jnp.arange(row_count, dtype=jnp.int32))
    block_inputs = (
        query_all,
        keyval_all,
        pos_own,
        pos_all,
        type_own,
        type_all,
        hops_use,
        edges_use,
        mol_own,
        mol_keys,
    )

    def forward_block(carry, block_in):
        distance, offset = pair_geometry(block_in[2], block_in[3], block_in[4], block_in[5])
        features = gaussian(offset, kernel_means, kernel_widths)
        pair_bias = bias_from_features(features, block_in[6], block_in[7], bias_params)[0]
        scores, query_rows, key_rows, value_rows, scaling = block_scores(block_in, pair_bias, width)
        peak = jnp.max(scores, axis=-1, keepdims=True)
        weights = jnp.exp(scores - peak)
        total = jnp.sum(weights, axis=-1, keepdims=True)
        probs = weights / total
        mixed = jnp.einsum(
            "hrl,lhe->rhe", probs.astype(b16), value_rows, preferred_element_type=f32
        )
        return (carry, (mixed.reshape(row_count, width).astype(b16), peak + jnp.log(total)))

    _, (attended, log_totals) = lax.scan(forward_block, 0, block_inputs)
    attended_flat = attended.reshape(token_rows, width)
    middle = flat_in + jnp.dot(attended_flat, out_weight, preferred_element_type=f32)
    normed2 = layer_norm(middle, ffn_gain).astype(b16)
    pre_ffn = jnp.dot(normed2, up_weight, preferred_element_type=f32)
    act = jax.nn.gelu(pre_ffn).astype(b16)
    result = middle + jnp.dot(act, down_weight, preferred_element_type=f32)
    layer_out = result.astype(b16).reshape(block_count, row_count, width)
    grad_top = out_grad.reshape(token_rows, width)
    grad_down = lax.dot_general(act, grad_top, CONTRACT_FIRST, preferred_element_type=f32)
    grad_act = lax.dot_general(grad_top, down_weight, CONTRACT_LAST, preferred_element_type=f32)
    _, gelu_back = jax.vjp(jax.nn.gelu, pre_ffn)
    grad_pre = gelu_back(grad_act)[0].astype(b16)
    grad_up = lax.dot_general(normed2, grad_pre, CONTRACT_FIRST, preferred_element_type=f32)
    grad_normed2 = lax.dot_general(grad_pre, up_weight, CONTRACT_LAST, preferred_element_type=f32)
    _, norm2_back = jax.vjp(layer_norm, middle, ffn_gain)
    grad_middle_part, grad_ffn_gain = norm2_back(grad_normed2)
    grad_middle = grad_top.astype(f32) + grad_middle_part
    grad_branch = grad_middle.astype(b16)
    grad_out_weight = lax.dot_general(
        attended_flat, grad_branch, CONTRACT_FIRST, preferred_element_type=f32
    )
    grad_attended = lax.dot_general(
        grad_branch, out_weight, CONTRACT_LAST, preferred_element_type=f32
    ).astype(b16)
    grad_attended = grad_attended.reshape(block_count, row_count, width)

    def backward_block(sums, inputs):
        block_in, grad_mixed, log_total = inputs
        distance, offset = pair_geometry(block_in[2], block_in[3], block_in[4], block_in[5])
        features, gauss_back = jax.vjp(gaussian, offset, kernel_means, kernel_widths)
        pair_bias, flat, pre_act, hidden = bias_from_features(
            features, block_in[6], block_in[7], bias_params
        )
        scores, query_rows, key_rows, value_rows, scaling = block_scores(block_in, pair_bias, width)
        probs = jnp.exp(scores - log_total)
        grad_rows = grad_mixed.reshape(row_count, heads, -1)
        grad_probs = jnp.einsum("rhe,lhe->hrl", grad_rows, value_rows, preferred_element_type=f32)
        centre = jnp.sum(probs * grad_probs, axis=-1, keepdims=True)
        grad_scores = probs * (grad_probs - centre)
        grad_low = grad_scores.astype(b16)
        grad_query = (
            jnp.einsum("hrl,lhe->rhe", grad_low, key_rows, preferred_element_type=f32) * scaling
        )
        grad_key = (
            jnp.einsum("hrl,rhe->lhe", grad_low, query_rows, preferred_element_type=f32) * scaling
        )
        grad_value = jnp.einsum(
            "hrl,rhe->lhe", probs.astype(b16), grad_rows, preferred_element_type=f32
        )
        grad_flat = grad_scores.reshape(heads, -1)
        grad_learned = grad_flat.astype(b16)
        grad_outer = lax.dot_general(
            hidden, grad_learned, CONTRACT_LAST, preferred_element_type=f32
        )
        grad_hidden = jnp.dot(kernel_outer, grad_learned, preferred_element_type=f32)
        _, inner_back = jax.vjp(jax.nn.gelu, pre_act)
        grad_inner_pre = inner_back(grad_hidden)[0].astype(b16)
        grad_inner = lax.dot_general(
            flat, grad_inner_pre, CONTRACT_LAST, preferred_element_type=f32
        )
        grad_features = jnp.dot(kernel_inner, grad_inner_pre, preferred_element_type=f32).reshape(
            features.shape
        )
        grad_offset, grad_means, grad_widths = gauss_back(grad_features)
        grad_hops = jax.ops.segment_sum(
            grad_flat.T, block_in[6].reshape(-1), num_segments=hop_table.shape[1]
        ).T
        grad_edges = jax.ops.segment_sum(
            grad_flat.T, block_in[7].reshape(-1), num_segments=edge_table.shape[1]
        ).T
        grad_type_query = jnp.stack(
            [jnp.sum(grad_offset * distance, axis=1), jnp.sum(grad_offset, axis=1)], axis=0
        )
        grad_type_key = jnp.stack(
            [jnp.sum(grad_offset * distance, axis=0), jnp.sum(grad_offset, axis=0)], axis=0
        )
        new_sums = (
            sums[0] + grad_means,
            sums[1] + grad_widths,
            sums[2] + grad_inner,
            sums[3] + grad_outer,
            sums[4] + grad_hops,
            sums[5] + grad_edges,
        )
        grad_keyval = jnp.concatenate(
            [grad_key.reshape(key_count, width), grad_value.reshape(key_count, width)], axis=-1
        )
        return (
            new_sums,
            (grad_query.reshape(row_count, width), grad_keyval, grad_type_query, grad_type_key),
        )

    start_sums = tuple((jnp.zeros(param.shape, f32) for param in bias_params))
    bias_grads, (grad_query_all, grad_keyval_all, grad_type_query, grad_type_key) = lax.scan(
        backward_block, start_sums, (block_inputs, grad_attended, log_totals)
    )
    grad_pack = jnp.concatenate([grad_keyval_all, grad_type_key.transpose(0, 2, 1)], axis=-1)
    from_above = passed_along(grad_pack[:, :margin], "rows", -1)
    from_below = passed_along(grad_pack[:, row_count + margin :], "rows", 1)
    own_pack = grad_pack[:, margin : margin + row_count]
    own_pack = own_pack.at[:, :margin].add(from_below).at[:, row_count - margin :].add(from_above)
    grad_keyval_own = own_pack[..., : 2 * width]
    grad_type_key_own = own_pack[..., 2 * width :].transpose(0, 2, 1)
    grad_proj = jnp.concatenate(
        [grad_query_all.astype(b16), grad_keyval_own.astype(b16)], axis=-1
    ).reshape(token_rows, 3 * width)
    grad_qkv = lax.dot_general(normed1, grad_proj, CONTRACT_FIRST, preferred_element_type=f32)
    grad_normed1 = lax.dot_general(grad_proj, qkv_weight, CONTRACT_LAST, preferred_element_type=f32)
    _, norm1_back = jax.vjp(layer_norm, flat_in, attn_gain)
    grad_in_part, grad_attn_gain = norm1_back(grad_normed1)
    grad_in = (grad_middle + grad_in_part).reshape(block_count, row_count, width)
    grad_types = (grad_type_query + grad_type_key_own).transpose(1, 0, 2).reshape(2, token_rows)
    grad_type_table = jnp.dot(grad_types, one_hot, precision=lax.Precision.HIGHEST)
    local_grads = (
        grad_qkv,
        grad_out_weight,
        grad_attn_gain,
        grad_ffn_gain,
        grad_up,
        grad_down,
        bias_grads[0],
        bias_grads[1],
        bias_grads[2],
        bias_grads[3],
        bias_grads[4],
        bias_grads[5],
        grad_type_table[0],
        grad_type_table[1],
    )
    summed = lax.psum(
        (
            local_grads[0],
            local_grads[1],
            local_grads[2],
            local_grads[3],
            local_grads[4],
            local_grads[5],
            local_grads[6],
            local_grads[7],
            local_grads[8],
            local_grads[9],
            local_grads[10],
            local_grads[11],
            local_grads[12],
            local_grads[13],
        ),
        ("blocks", "rows"),
    )
    return (
        layer_out,
        grad_in,
        summed[0],
        summed[1],
        summed[2],
        summed[3],
        summed[4],
        summed[5],
        summed[6],
        summed[7],
        summed[8],
        summed[9],
        summed[10],
        summed[11],
        summed[12],
        summed[13],
    )


def solution(mesh):
    in_specs = (
        P("blocks", "rows", None),
        P("blocks", None, "rows"),
        P("blocks", "rows"),
        P("blocks", "rows", None),
        P("blocks", "rows", None),
        P("blocks", None),
        P(),
        P(),
        P(),
        P(),
        P(),
        P(),
        P(),
        P(),
        P(),
        P(),
        P(),
        P(),
        P(),
        P(),
        P("blocks", "rows", None),
    )
    out_specs = (
        P("blocks", "rows", None),
        P("blocks", "rows", None),
        P(),
        P(),
        P(),
        P(),
        P(),
        P(),
        P(),
        P(),
        P(),
        P(),
        P(),
        P(),
        P(),
        P(),
    )
    return jax.shard_map(body, mesh=mesh, in_specs=in_specs, out_specs=out_specs, check_vma=False)
```

profile of v0, /device:TPU:0, one launch (start us, length us, event | category | flops | bytes accessed | tf_op | source)
XLA Modules:
  0.0 1299.6 jit_solution(10879485889543498294)
XLA Ops:
  10.3 2.9 collective-permute-start.2
  20.1 5.3 collective-permute-start
  27.7 1.9 pad_dynamic-slice_fusion
  29.7 1.8 reshape.621
  34.7 1.8 reshape.622
  51.2 1.8 slice.170
  55.9 1.8 add.304
  59.1 1.8 add.310
  60.9 1.8 copy.93
  62.7 1.7 copy.88
  64.5 83.4 %gather_fusion.1 = bf16[40704,32]{1,0:T(8,128)(2,1)} fusion(bf16[32,1536]{0,1:T(8,128)(2,1)} %copy.93, s32[40960]{0:T(1024)} %pad_clamp_fusion), kind=kCustom, calls=%fused_computation.1.clone | custom fusion | bytes 5372928 | tf_op jit(solution)/shard_map/while/body/eval_jaxpr/jit(_take)/gather | solution.py:68
  147.9 9.5 copy.94
  157.4 83.3 %gather_fusion = bf16[40704,32]{1,0:T(8,128)(2,1)} fusion(bf16[32,512]{0,1:T(8,128)(2,1)} %copy.91, s32[40960]{0:T(1024)} %pad_clamp_fusion.1), kind=kCustom, calls=%fused_computation.clone | custom fusion | bytes 5372928 | tf_op jit(solution)/shard_map/while/body/eval_jaxpr/jit(_take)/gather | solution.py:68
  240.6 9.5 copy.92
  254.5 1.7 copy.90
  256.2 1.8 sqrt.14
  259.4 1.8 add.307
  261.9 1.8 add.314
  265.7 22.0 %convolution_bitcast_fusion.1 = f32[128,40704]{0,1:T(8,128)} fusion(bf16[128,128]{1,0:T(8,128)(2,1)} %param.43, f32[128]{0:T(128)} %get-tuple-element.296, f32[128]{0:T(128)} %param.42, f32[128]{0:T(128)} %param.41, f32[40704]{0:T(1024)S(1)} %add_add_fusion.3), kind=kOutput, calls=%fused_computation.5 | convolution fusion | flops 1365049344 | bytes 21037568 | tf_op jit(solution)/shard_map/while/body/eval_jaxpr/dot_general | solution.py:61
  287.7 13.9 %fusion = f32[32,40704]{1,0:T(8,128)} fusion(bf16[128,32]{0,1:T(8,128)(2,1)S(1)} %copy-done.63, bf16[40704,32]{0,1:T(8,128)(2,1)S(1)} %copy-done.15, bf16[40704,32]{0,1:T(8,128)(2,1)S(1)} %copy-done.16, pred[40704]{0:T(1024)(128)(4,1)S(1)} %copy-done.38, pred[40704]{0:T(1024)(128)(4,1)S(1)} %copy-done.37, f32[128,40704]{0,1:T(8,128)} %convolution_bitcast_fusion.1), kind=kOutput, calls=%fused_computation.7 | convolution fusion | flops 388153344 | bytes 31350272 | tf_op jit(solution)/shard_map/while/body/eval_jaxpr/dot_general | solution.py:65
  301.6 9.6 reshape.623
  311.2 6.7 copy.95
  320.2 2.1 copy.89
  322.3 2.1 copy.86
  324.4 4.1 fusion.114
  333.0 2.0 fusion.72
  339.9 1.7 copy.96
  341.6 5.2 fusion.18
  346.9 4.0 multiply_reduce_fusion
  352.5 2.3 copy-done.2
  354.8 2.5 convolution_multiply_fusion
  357.3 6.3 copy.97
  363.6 7.2 reshape.629
  370.8 20.3 %fusion.10 = bf16[128,40704]{0,1:T(8,128)(2,1)} fusion(f32[128,40704]{0,1:T(8,128)} %convolution_bitcast_fusion.1, bf16[128,32]{0,1:T(8,128)(2,1)S(1)} %copy-done.64, f32[32,40704]{1,0:T(8,128)} %reshape.629), kind=kOutput, calls=%fused_computation.23 | convolution fusion | flops 438951936 | bytes 36478976 | tf_op jit(solution)/shard_map/while/body/eval_jaxpr/dot_general | solution.py:244
  391.1 12.3 copy.103
  403.4 234.9 %scatter_custom_fusion = f32[512,32]{1,0:T(8,128)} fusion(s32[40704]{0:T(1024)} %reshape.621, f32[40704,32]{1,0:T(8,128)} %copy.103, f32[]{:T(128)} %constant.216.clone.1), kind=kCustom, calls=%fused_computation.141 | custom fusion | flops 1302528 | bytes 66048 | tf_op jit(solution)/shard_map/while/body/eval_jaxpr/scatter-add | solution.py:254
  638.3 235.2 %scatter_custom_fusion.1 = f32[1536,32]{1,0:T(8,128)} fusion(s32[40704]{0:T(1024)} %reshape.622, f32[40704,32]{1,0:T(8,128)} %copy.103, f32[]{:T(128)} %constant.216.clone.1), kind=kCustom, calls=%fused_computation.108 | custom fusion | flops 1302528 | bytes 197120 | tf_op jit(solution)/shard_map/while/body/eval_jaxpr/scatter-add | solution.py:257
  873.6 20.9 %fusion.12 = f32[128,128]{1,0:T(8,128)} fusion(bf16[128,40704]{0,1:T(8,128)(2,1)} %fusion.10, f32[128]{0:T(128)S(1)} %copy-done.61, f32[128]{0:T(128)S(1)} %copy-done.50, f32[128]{0:T(128)S(1)} %copy-done.54, f32[40704]{0:T(1024)} %copy-done.31), kind=kOutput, calls=%fused_computation.30 | convolution fusion | flops 1365049344 | bytes 10650112 | tf_op jit(solution)/shard_map/while/body/eval_jaxpr/dot_general | solution.py:247
  894.5 20.4 %fusion.3 = (f32[128,40704]{0,1:T(8,128)S(1)}, f32[40704,128]{1,0:T(8,128)}) fusion(f32[128]{0:T(128)S(1)} %copy-done.61, f32[128]{0:T(128)S(1)} %copy-done.50, f32[128]{0:T(128)S(1)} %copy-done.54, f32[40704]{0:T(1024)S(1)} %copy-done.32, bf16[128,40704]{0,1:T(8,128)(2,1)} %fusion.10, bf16[128,128]{1,0:T(8,128)(2,1)S(1)} %copy-done.62), kind=kOutput, calls=%fused_computation.16 | convolution fusion | flops 1385889792 | bytes 52298240 | tf_op jit(solution)/shard_map/while/body/eval_jaxpr/dot_general | solution.py:250
  914.9 25.5 %fusion.13 = (f32[128]{0:T(128)}, f32[40704]{0:T(1024)}, f32[128]{0:T(128)}, f32[128]{0:T(128)}) fusion(f32[128,40704]{0,1:T(8,128)S(1)} %get-tuple-element.304, f32[128]{0:T(128)S(1)} %copy-done.50, f32[128]{0:T(128)S(1)} %copy-done.54, f32[40704]{0:T(1024)S(1)} %copy-done.32, f32[128]{0:T(128)S(1)} %copy-done.52, f32[40704,128]{1,0:T(8,128)} %get-tuple-element.305, ...), kind=kLoop, calls=%fused_computation.31 | loop fusion | flops 67690368 | bytes 42010112 | tf_op jit(solution)/shard_map/while/body/eval_jaxpr/transpose(jvp())/reduce_sum | solution.py:43
  940.4 1.8 reduce_sum.269
  943.7 1.7 copy.98
  947.1 1.8 maximum_bitcast_fusion
  951.5 3.0 copy.99
  954.5 2.1 collective-permute-start.4
  956.6 2.9 fusion.116
  959.5 3.0 fusion.106
  962.5 3.0 copy.100
  965.5 3.3 pad_maximum_fusion
  968.8 3.0 copy.101
  973.0 2.6 fusion.38
  975.6 3.9 fusion.32
  979.5 5.2 scatter-add.26
  984.8 3.0 copy.102
  987.8 2.5 slice_add_fusion
  990.3 5.8 scatter-add.27
  997.3 5.3 fusion.64
  1003.9 2.5 fusion.36
  1007.0 13.6 %fusion.25 = f32[128,32]{0,1:T(8,128)} fusion(f32[32,40704]{1,0:T(8,128)} %reshape.629, f32[128,40704]{0,1:T(8,128)} %convolution_bitcast_fusion.1), kind=kOutput, calls=%fused_computation.57 | convolution fusion | flops 381640704 | bytes 26066944 | tf_op jit(solution)/shard_map/while/body/eval_jaxpr/dot_general | solution.py:241
  1024.5 44.6 %all-reduce.2 = (f32[768]{0:T(1024)}, f32[768]{0:T(1024)}, f32[128]{0:T(128)}, f32[128]{0:T(128)}, f32[128,32]{0,1:T(8,128)}, /*index=5*/f32[512]{0:T(512)}, f32[512]{0:T(512)}) all-reduce(f32[768]{0:T(1024)S(1)} %get-tuple-element.255, f32[768]{0:T(1024)S(1)} %copy-done.41, ...), channel_id=1, replica_groups=mesh['blocks'=8,'rows'=4] {'blocks','rows'}, use_global_device_ids=true, to_apply=%region_21.24 | all-reduce | flops 6912 | bytes 55296 | tf_op jit(solution)/shard_map/psum | solution.py:319
  1069.7 2.3 add_bitcast_fusion
  1072.0 204.0 %all-reduce.6.cloned.1.call-done = (f32[768,2304]{1,0:T(8,128)}, f32[768,768]{1,0:T(8,128)}, f32[768,768]{1,0:T(8,128)}, f32[768,768]{1,0:T(8,128)}, f32[128,128...) async-done(((f32[768,2304]{1,0:T(8,128)}, f32[768,768]{1,0:T(8,128)}, f32[768,768]{1,0:T(8,128)}, f32[768,768]{1,0:T(8,128)}, f32[128,128]{1,0:T(8,128)}, ...) | async-done | bytes 14483472 | tf_op jit(solution)/shard_map/psum | solution.py:319
  1277.8 2.1 copy.106
  1279.8 6.6 copy.116
  (225 shorter events, 78.0 us)
Async XLA Ops:
  7.2 9.6 copy-start
  7.2 1268.9 %all-reduce.6.cloned.1.call-start = ((), (), s32[]{:S(2)}) async-start(), calls=%async_computation | async-start | bytes 30539776 | tf_op jit(solution)/shard_map/psum | solution.py:319
  10.3 239.8 %collective-permute-start.2 = (f32[1,95,5]{1,2,0:T(8,128)}, f32[1,95,5]{1,2,0:T(8,128)}, u32[]{:S(2)}, u32[]{:S(2)}) collective-permute-start(f32[1,95,5]{1,2,0:T(8,128)} %get-tuple-element.288), channel_id=1, source_target_pairs={{0,1},{1,2},{2,3},{4,5},{5,6},{6,7},{8,9},{9,10},{10,11},{12,13},{... | collective-permute-start | bytes 5708 | tf_op jit(solution)/shard_map/ppermute | solution.py:23
  13.3 236.9 %collective-permute-start.3 = (f32[1,95,5]{1,2,0:T(8,128)}, f32[1,95,5]{1,2,0:T(8,128)}, u32[]{:S(2)}, u32[]{:S(2)}) collective-permute-start(f32[1,95,5]{1,2,0:T(8,128)} %get-tuple-element.289), channel_id=1, source_target_pairs={{1,0},{2,1},{3,2},{5,4},{6,5},{7,6},{9,8},{10,9},{11,10},{13,12},{... | collective-permute-start | bytes 5708 | tf_op jit(solution)/shard_map/ppermute | solution.py:24
  15.6 4.5 copy-start.39
  16.7 23.5 %copy-start.55 = (f32[128]{0:T(128)}, f32[128]{0:T(128)S(1)}, u32[]{:S(2)}) copy-start(f32[128]{0:T(128)S(1)} %fusion.50) | copy-start | bytes 1540
  16.8 23.5 %copy-start.44 = (f32[128]{0:T(128)}, f32[128]{0:T(128)S(1)}, u32[]{:S(2)}) copy-start(f32[128]{0:T(128)S(1)} %fusion.97) | copy-start | bytes 1540
  20.1 297.8 %collective-permute-start = (bf16[1,95,1536]{2,1,0:T(8,128)(2,1)}, bf16[1,95,1536]{2,1,0:T(8,128)(2,1)}, u32[]{:S(2)}, u32[]{:S(2)}) collective-permute-start(bf16[1,95,1536]{2,1,0:T(8,128)(2,1)} %get-tuple-element.284), channel_id=1, source_target_pairs={{0,1},{1,2},{2,3},{4,5},{5,6},{6,7},{8,9},{9,10},{10,11},{12,13},{... | collective-permute-start | bytes 875528 | tf_op jit(solution)/shard_map/ppermute | solution.py:23
  25.4 292.5 %collective-permute-start.1 = (bf16[1,95,1536]{2,1,0:T(8,128)(2,1)}, bf16[1,95,1536]{2,1,0:T(8,128)(2,1)}, u32[]{:S(2)}, u32[]{:S(2)}) collective-permute-start(bf16[1,95,1536]{2,1,0:T(8,128)(2,1)} %get-tuple-element.285), channel_id=1, source_target_pairs={{1,0},{2,1},{3,2},{5,4},{6,5},{7,6},{9,8},{10,9},{11,10},{13,12},{... | collective-permute-start | bytes 875528 | tf_op jit(solution)/shard_map/ppermute | solution.py:24
  265.7 22.0 %copy-start.15 = (bf16[40704,32]{0,1:T(8,128)(2,1)S(1)}, bf16[40704,32]{0,1:T(8,128)(2,1)}, u32[]{:S(2)}) copy-start(bf16[40704,32]{0,1:T(8,128)(2,1)} %copy.94) | copy-start | bytes 7815172
  265.7 22.0 %copy-start.16 = (bf16[40704,32]{0,1:T(8,128)(2,1)S(1)}, bf16[40704,32]{0,1:T(8,128)(2,1)}, u32[]{:S(2)}) copy-start(bf16[40704,32]{0,1:T(8,128)(2,1)} %copy.92) | copy-start | bytes 7815172
  265.7 22.0 %copy-start.37 = (pred[40704]{0:T(1024)(128)(4,1)S(1)}, pred[40704]{0:T(1024)(128)(4,1)}, u32[]{:S(2)}) copy-start(pred[40704]{0:T(1024)(128)(4,1)} %compare_and_fusion.1) | copy-start | bytes 122116
  265.7 22.0 %copy-start.38 = (pred[40704]{0:T(1024)(128)(4,1)S(1)}, pred[40704]{0:T(1024)(128)(4,1)}, u32[]{:S(2)}) copy-start(pred[40704]{0:T(1024)(128)(4,1)} %compare_and_fusion) | copy-start | bytes 122116
  265.7 22.0 %copy-start.63 = (bf16[128,32]{0,1:T(8,128)(2,1)S(1)}, bf16[128,32]{0,1:T(8,128)(2,1)}, u32[]{:S(2)}) copy-start(bf16[128,32]{0,1:T(8,128)(2,1)} %param.44) | copy-start | bytes 24580
  328.5 2.5 copy-start.1
  330.1 2.5 copy-start.8
  330.1 2.5 copy-start.34
  330.1 2.9 copy-start.25
  331.1 5.7 copy-start.29
  331.1 3.9 copy-start.28
  332.3 4.4 copy-start.4
  332.4 4.4 copy-start.42
  332.6 4.4 copy-start.47
  333.0 5.0 copy-start.12
  335.6 2.4 copy-start.30
  341.6 5.2 copy-start.18
  341.6 5.2 copy-start.24
  341.6 9.3 slice-start
  346.9 4.1 slice-start.1
  350.9 3.9 copy-start.23
  352.5 2.3 copy-start.2
  363.6 7.2 copy-start.64
  391.1 482.4 %copy-start.50 = (f32[128]{0:T(128)S(1)}, f32[128]{0:T(128)}, u32[]{:S(2)}) copy-start(f32[128]{0:T(128)} %param.42) | copy-start | bytes 1540
  391.1 482.4 %copy-start.54 = (f32[128]{0:T(128)S(1)}, f32[128]{0:T(128)}, u32[]{:S(2)}) copy-start(f32[128]{0:T(128)} %param.41) | copy-start | bytes 1540
  391.1 482.4 %copy-start.61 = (f32[128]{0:T(128)S(1)}, f32[128]{0:T(128)}, u32[]{:S(2)}) copy-start(f32[128]{0:T(128)} %get-tuple-element.296) | copy-start | bytes 1540
  873.5 20.9 %copy-start.32 = (f32[40704]{0:T(1024)S(1)}, f32[40704]{0:T(1024)}, u32[]{:S(2)}) copy-start(f32[40704]{0:T(1024)} %copy-done.31) | copy-start | bytes 488452
  873.6 20.9 %copy-start.62 = (bf16[128,128]{1,0:T(8,128)(2,1)S(1)}, bf16[128,128]{1,0:T(8,128)(2,1)}, u32[]{:S(2)}) copy-start(bf16[128,128]{1,0:T(8,128)(2,1)} %param.43) | copy-start | bytes 98308
  894.5 20.4 %copy-start.51 = (f32[128]{0:T(128)S(1)}, f32[128]{0:T(128)}, u32[]{:S(2)}) copy-start(f32[128]{0:T(128)} %get-tuple-element.294) | copy-start | bytes 1540
  894.5 20.4 %copy-start.52 = (f32[128]{0:T(128)S(1)}, f32[128]{0:T(128)}, u32[]{:S(2)}) copy-start(f32[128]{0:T(128)} %get-tuple-element.295) | copy-start | bytes 1540
  947.1 12.4 copy-start.35
  947.1 12.4 copy-start.43
  947.1 12.4 copy-start.48
  954.5 8.1 collective-permute-start.4
  971.7 13.0 %collective-permute-start.5 = (f32[1,95,1538]{2,0,1:T(1,128)}, f32[1,95,1538]{2,0,1:T(1,128)}, u32[]{:S(2)}, u32[]{:S(2)}) collective-permute-start(f32[1,95,1538]{2,0,1:T(1,128)} %copy.101), channel_id=1, source_target_pairs={{1,0},{2,1},{3,2},{5,4},{6,5},{7,6},{9,8},{10,9},{11,10},{13,12},{... | collective-permute-start | bytes 1753328 | tf_op jit(solution)/shard_map/ppermute | solution.py:32
  979.5 17.8 %copy-start.33 = (f32[768]{0:T(1024)S(1)}, f32[768]{0:T(1024)}, u32[]{:S(2)}) copy-start(f32[768]{0:T(1024)} %param.37) | copy-start | bytes 9220
  979.5 17.8 %copy-start.40 = (f32[128]{0:T(128)S(1)}, f32[128]{0:T(128)}, u32[]{:S(2)}) copy-start(f32[128]{0:T(128)} %copy-done.39) | copy-start | bytes 1540
  979.5 17.8 %copy-start.45 = (f32[128]{0:T(128)S(1)}, f32[128]{0:T(128)}, u32[]{:S(2)}) copy-start(f32[128]{0:T(128)} %copy-done.44) | copy-start | bytes 1540
  997.3 5.4 copy-start.13
  1002.6 3.8 copy-start.59
  1002.6 3.8 copy-start.60
  1006.9 13.7 %copy-start.6 = (bf16[1,128,768]{2,1,0:T(8,128)(2,1)S(1)}, bf16[1,128,768]{2,1,0:T(8,128)(2,1)}, u32[]{:S(2)}) copy-start(bf16[1,128,768]{2,1,0:T(8,128)(2,1)} %param.29) | copy-start | bytes 589828
  1006.9 13.7 %copy-start.14 = (bf16[1,128,1536]{1,2,0:T(8,128)(2,1)S(1)}, bf16[1,128,1536]{1,2,0:T(8,128)(2,1)}, u32[]{:S(2)}) copy-start(bf16[1,128,1536]{1,2,0:T(8,128)(2,1)} %copy-done.13) | copy-start | bytes 1179652
  1006.9 13.7 %copy-start.22 = (bf16[32,24,128]{2,1,0:T(8,128)(2,1)S(1)}, bf16[32,24,128]{2,1,0:T(8,128)(2,1)}, u32[]{:S(2)}) copy-start(bf16[32,24,128]{2,1,0:T(8,128)(2,1)} %fusion.32) | copy-start | bytes 589828
  1006.9 15.2 %copy-start.56 = (f32[128]{0:T(128)S(1)}, f32[128]{0:T(128)}, u32[]{:S(2)}) copy-start(f32[128]{0:T(128)} %copy-done.55) | copy-start | bytes 1540
  1006.9 15.2 %copy-start.46 = (f32[128]{0:T(128)S(1)}, f32[128]{0:T(128)}, u32[]{:S(2)}) copy-start(f32[128]{0:T(128)} %copy-done.44) | copy-start | bytes 1540
  1020.6 2.3 copy-start.57
  1020.6 2.3 copy-start.58
  1020.6 2.3 copy-start.65
  1020.6 3.8 copy-start.41
  1022.1 2.4 copy-start.49
  1279.8 6.6 copy-start.21
  1286.4 2.5 copy-start.20
  1286.4 3.9 copy-start.19
  1288.9 2.8 copy-start.36
  (11 other events, 11.3 us)
Sparse Core Ops, SparseCore 0:
  1002.8 273.2 all-reduce.5
where the time goes:
time: 1320 us; the launch traced here: 1300 us
  other arithmetic  543 us (41%)
  local copies, waits for them, and re-layouts  322 us (24%)
  waiting for transfers between devices  204 us (15%)
  matrix products  156 us (12%)
  blocking collectives  44.6 us (3%)
  between operations  15.3 us (1%)
  starting transfers between devices  14.2 us (1%)
    scatter-add x1, other arithmetic, backward_block(): jax.ops.segment_sum(grad_flat.T, block_in[7].reshape(-1), num_segments=ed...  235 us
    scatter-add x1, other arithmetic, backward_block(): jax.ops.segment_sum(grad_flat.T, block_in[6].reshape(-1), num_segments=ho...  235 us
    psum x1, waiting for transfers between devices, body(): lax.psum((local_grads[0], local_grads[1], local_grads[2], local_grads[3],...  204 us
    gather x2, local copies, waits for them, and re-layouts, bias_from_features(): jnp.take(edge_table, edge_rows.reshape(-1), axis=1).astype(jnp.float32)  92.9 us
    gather x2, local copies, waits for them, and re-layouts, bias_from_features(): jnp.take(hop_table, hop_rows.reshape(-1), axis=1).astype(jnp.float32)  92.8 us
    psum x1, blocking collectives, body(): lax.psum((local_grads[0], local_grads[1], local_grads[2], local_grads[3],...  44.6 us
    unnamed x145, local copies, waits for them, and re-layouts  28.5 us
  transfers between devices with their start and end apart: 7, of which 1 were waited for; matrix products, arithmetic and copies ran while one was open for 26% of the time, Pallas kernels for 0%

commit v1 on v0

v1 whole, which is shorter than its diff:
```python
import functools

import jax
import jax.numpy as jnp
from jax import lax
from jax.experimental import pallas as pl
from jax.experimental.pallas import tpu as pltpu
from jax.sharding import PartitionSpec as P

EPS = 1e-05
NEG = -1000000000.0
SQRT_TWO_PI = 2.5066282746310002
SQRT_2_OVER_PI = 0.7978845608028654
CUBIC = 0.044715
LOG2E = 1.4426950408889634
F32 = jnp.float32
B16 = jnp.bfloat16
T = 128
W = 3 * T
D = 768
HEADS = 32
HD = 24
NN = (((1,), (0,)), ((), ()))
NT = (((1,), (1,)), ((), ()))
GROUPS = (
    (0, 1, (0, 1, 2, 3, 4)),
    (0, 2, (5,)),
    (1, 1, (6, 7, 8, 9)),
    (1, 2, (10,)),
    (2, 1, (11, 12, 13, 14, 15)),
)
CHUNK = 8
PAIRS = CHUNK * T


def mm(a, b, dims=NN):
    return lax.dot_general(a, b, dims, preferred_element_type=F32)


def gelu_parts(x):
    x2 = x * x
    t = jnp.tanh(x * (SQRT_2_OVER_PI + (SQRT_2_OVER_PI * CUBIC) * x2))
    half = 0.5 + 0.5 * t
    slope = half + (0.5 * x) * (1.0 - t * t) * (
        SQRT_2_OVER_PI + (3.0 * SQRT_2_OVER_PI * CUBIC) * x2
    )
    return x * half, slope


def normalise(v):
    centre = jnp.mean(v, axis=-1, keepdims=True)
    shifted = v - centre
    spread = jnp.mean(shifted * shifted, axis=-1, keepdims=True)
    rstd = lax.rsqrt(spread + EPS)
    return shifted * rstd, rstd


def norm_back(grad, xhat, rstd, gain):
    g = grad * gain
    return rstd * (
        g
        - jnp.mean(g, axis=-1, keepdims=True)
        - xhat * jnp.mean(g * xhat, axis=-1, keepdims=True)
    )


def down(row):
    return jnp.transpose(jnp.broadcast_to(row, (T, T)))


def compute_kernel(
    lens_ref,
    hid_ref,
    pos_ref,
    types_ref,
    hops_ref,
    edges_ref,
    wqkv_ref,
    wout_ref,
    g1_ref,
    g2_ref,
    wup_ref,
    wdown_ref,
    means_ref,
    widths_ref,
    inner_ref,
    outer_ref,
    hop_tab_ref,
    edge_tab_ref,
    scale_ref,
    shift_ref,
    cot_ref,
    out_ref,
    gmid_ref,
    gn1_ref,
    gqkv_ref,
    gout_ref,
    gg1_ref,
    gg2_ref,
    gup_ref,
    gdown_ref,
    gmw_ref,
    ginner_ref,
    gouter_ref,
    ghop_ref,
    gedge_ref,
    gtype_ref,
    n1t_ref,
    xhat_ref,
    rstd_ref,
    q_ref,
    k_ref,
    v_ref,
    m_ref,
    mb_ref,
    mt_ref,
    off_ref,
    dist_ref,
    hopi_ref,
    edgei_ref,
    cols_ref,
    w1_ref,
    w2_ref,
    innert_ref,
    feat_ref,
    hidden_ref,
    slope_ref,
    bias_ref,
    p_ref,
    mixed_ref,
    gmix_ref,
    gq_ref,
    gk_ref,
    gv_ref,
    goff_ref,
    lhsh_ref,
    lhse_ref,
    rhsh_ref,
    rhse_ref,
    gpre_ref,
):
    row = lax.axis_index("rows")
    rows = lax.axis_size("rows")
    x = hid_ref[...].astype(F32)
    xhat, rstd = normalise(x)
    xhat_ref[...] = xhat
    rstd_ref[...] = rstd
    n1 = (xhat * g1_ref[...]).astype(B16)
    for c in range(D // T):
        for t in range(3):
            n1t_ref[c * T : (c + 1) * T, t * T : (t + 1) * T] = jnp.transpose(
                n1[t * T : (t + 1) * T, c * T : (c + 1) * T]
            )
    q_ref[...] = mm(n1[T : 2 * T], wqkv_ref[:, :D]).astype(B16)
    k_ref[...] = mm(n1, wqkv_ref[:, D : 2 * D]).astype(B16)
    v_ref[...] = mm(n1, wqkv_ref[:, 2 * D :]).astype(B16)

    first = (row - 1) * T
    ids_row = first + lax.broadcasted_iota(jnp.int32, (1, W), 1)
    mol_row = jnp.zeros((1, W), jnp.int32)
    end = jnp.int32(0)
    for m in range(lens_ref.shape[1]):
        end = end + lens_ref[0, m]
        mol_row = mol_row + jnp.where(ids_row >= end, 1, 0)
    mol_row = jnp.where((ids_row >= 0) & (ids_row < rows * T), mol_row, -1).astype(F32)
    mol_own = mol_row[:, T : 2 * T]
    mol_col = down(mol_own)
    scale_col = jnp.concatenate(
        [down(scale_ref[:, c * T : (c + 1) * T]) for c in range(4)], axis=0
    )
    shift_col = jnp.concatenate(
        [down(shift_ref[:, c * T : (c + 1) * T]) for c in range(4)], axis=0
    )
    kinds = lax.broadcasted_iota(jnp.int32, (4 * T, T), 0)
    pos = pos_ref[...].astype(F32)
    sel = [jnp.zeros((T, T), F32) for _ in range(5)]
    own = None
    hop_sel = jnp.zeros((T, T), jnp.int32)
    edge_sel = jnp.zeros((T, T), jnp.int32)
    for t in range(3):
        lanes = slice(t * T, (t + 1) * T)
        mask = mol_col == jnp.broadcast_to(mol_row[:, lanes], (T, T))
        mask_t = down(mol_row[:, lanes]) == jnp.broadcast_to(mol_own, (T, T))
        m_ref[t] = mask.astype(F32)
        mb_ref[t] = mask.astype(F32).astype(B16)
        mt_ref[t] = mask_t.astype(F32).astype(B16)
        hit = kinds == types_ref[:, lanes]
        terms = (
            pos[0:1, lanes],
            pos[1:2, lanes],
            pos[2:3, lanes],
            jnp.sum(jnp.where(hit, scale_col, 0.0), axis=0, keepdims=True),
            jnp.sum(jnp.where(hit, shift_col, 0.0), axis=0, keepdims=True),
        )
        if t == 1:
            own = terms
        sel = [jnp.where(mask, v, s) for v, s in zip(terms, sel)]
        tile = jnp.clip(row + (t - 1), 0, rows - 1)
        at = pl.ds(pl.multiple_of(tile * T, T), T)
        hop_sel = jnp.where(mask, hops_ref[:, at], hop_sel)
        edge_sel = jnp.where(mask, edges_ref[:, at], edge_sel)
    ownc = [down(v) for v in own]
    dx, dy, dz = (ownc[c] - sel[c] for c in range(3))
    dist = jnp.sqrt(dx * dx + dy * dy + dz * dz)
    dist_ref[...] = dist
    off_ref[...] = (ownc[3] + sel[3]) * dist + ownc[4] + sel[4]
    hopi_ref[...] = hop_sel
    edgei_ref[...] = edge_sel

    mean_col = down(means_ref[...])
    inv_col = 1.0 / down(widths_ref[...])
    s_col = inv_col * ((0.5 * LOG2E) ** 0.5)
    cols_ref[0] = s_col
    cols_ref[1] = mean_col * s_col
    cols_ref[2] = jnp.log2(inv_col * (1.0 / SQRT_TWO_PI))
    cols_ref[3] = inv_col * (1.0 / (0.5 * LOG2E) ** 0.5)
    innert_ref[...] = jnp.transpose(inner_ref[...])
    outer_t = outer_ref[...]
    for g in range(4):
        w1_ref[g * HEADS : (g + 1) * HEADS, 0:T] = outer_t
        w1_ref[g * HEADS : (g + 1) * HEADS, T : 2 * T] = hop_tab_ref[:, g * T : (g + 1) * T]
    for g in range(12):
        w2_ref[g * HEADS : (g + 1) * HEADS, :] = edge_tab_ref[:, g * T : (g + 1) * T]

    iota_k = lax.broadcasted_iota(jnp.int32, (T, 2 * T), 0)

    def two(block, s):
        return jnp.concatenate([block[s : s + 1], block[s + 1 : s + 2]], axis=1)

    def wide(a):
        return jnp.concatenate([a, a], axis=1)

    def hot(index):
        return jnp.where(iota_k == (index & (T - 1)), 1.0, 0.0).astype(B16)

    def bias_step(c, _):
        at = pl.ds(pl.multiple_of(c * CHUNK, CHUNK), CHUNK)
        off8 = off_ref[at, :]
        hop8 = hopi_ref[at, :]
        edge8 = edgei_ref[at, :]
        for s in range(0, CHUNK, 2):
            lanes = pl.ds(pl.multiple_of(c * PAIRS + s * T, 2 * T), 2 * T)
            z = two(off8, s) * wide(cols_ref[0]) - wide(cols_ref[1])
            feat = jnp.exp2(wide(cols_ref[2]) - z * z).astype(B16)
            feat_ref[:, lanes] = feat
            pre = mm(innert_ref[...], feat)
            act, slope = gelu_parts(pre)
            hidden = act.astype(B16)
            hidden_ref[:, lanes] = hidden
            slope_ref[:, lanes] = slope
            hop = two(hop8, s)
            edge = two(edge8, s)
            low = mm(w1_ref[...], jnp.concatenate([hidden, hot(hop)], axis=0))
            high = mm(w2_ref[...], hot(edge))
            hop_g = jnp.broadcast_to(hop >> 7, (HEADS, 2 * T))
            edge_g = jnp.broadcast_to(edge >> 7, (HEADS, 2 * T))
            bias = low[0:HEADS]
            for g in range(1, 4):
                bias = jnp.where(hop_g == g, low[g * HEADS : (g + 1) * HEADS], bias)
            more = high[0:HEADS]
            for g in range(1, 12):
                more = jnp.where(edge_g == g, high[g * HEADS : (g + 1) * HEADS], more)
            bias = bias + more
            base = (c * CHUNK + s) * HEADS
            bias_ref[pl.ds(pl.multiple_of(base, HEADS), HEADS), :] = bias[:, :T]
            bias_ref[pl.ds(pl.multiple_of(base + HEADS, HEADS), HEADS), :] = bias[:, T:]
        return 0

    lax.fori_loop(0, T // CHUNK, bias_step, 0)

    scaling = HD ** (-0.5)

    def head_mask(h, tile, tiles):
        lane = lax.broadcasted_iota(jnp.int32, (1, tiles * T), 1) + tile * T
        return ((lane >= h * HD) & (lane < (h + 1) * HD)).astype(F32)

    def spread(low):
        return jnp.concatenate([low * mb_ref[t] for t in range(3)], axis=1)

    def compact(wide_scores):
        return jnp.where(
            m_ref[0] > 0,
            wide_scores[:, :T],
            jnp.where(m_ref[1] > 0, wide_scores[:, T : 2 * T], wide_scores[:, 2 * T :]),
        )

    for half in range(2):
        mixed_half = [None, None, None]
        for tile, tiles, heads in GROUPS:
            lanes = slice(half * W + tile * T, half * W + (tile + tiles) * T)
            masks = [head_mask(h, tile, tiles) for h in heads]
            q = q_ref[:, lanes]
            qm = jnp.concatenate([q * m.astype(B16) for m in masks], axis=0)
            raw = mm(qm, k_ref[:, lanes], NT)
            probs = []
            for a, h in enumerate(heads):
                head = half * 16 + h
                bias = bias_ref[pl.ds(head, T, stride=HEADS), :]
                visible = (m_ref[0] + m_ref[1] + m_ref[2]) > 0
                scores = jnp.where(
                    visible, compact(raw[a * T : (a + 1) * T]) * scaling + bias, NEG
                )
                peak = jnp.max(scores, axis=-1, keepdims=True)
                weights = jnp.exp(scores - peak)
                p = weights / jnp.sum(weights, axis=-1, keepdims=True)
                p_ref[head] = p
                probs.append(spread(p.astype(B16)))
            o = mm(jnp.concatenate(probs, axis=0), v_ref[:, lanes])
            total = o[:T] * masks[0]
            for a in range(1, len(heads)):
                total = total + o[a * T : (a + 1) * T] * masks[a]
            for j in range(tiles):
                part = total[:, j * T : (j + 1) * T]
                before = mixed_half[tile + j]
                mixed_half[tile + j] = part if before is None else before + part
        for j in range(3):
            mixed_ref[:, half * W + j * T : half * W + (j + 1) * T] = mixed_half[j].astype(B16)

    def tr(a):
        return jnp.concatenate(
            [jnp.transpose(a[:, c * T : (c + 1) * T]) for c in range(a.shape[1] // T)], axis=0
        )

    mixed = mixed_ref[...]
    middle = hid_ref[T : 2 * T, :].astype(F32) + mm(mixed, wout_ref[...])
    xhat2, rstd2 = normalise(middle)
    n2 = (xhat2 * g2_ref[...]).astype(B16)
    act, slope = gelu_parts(mm(n2, wup_ref[...]))
    act = act.astype(B16)
    out_ref[...] = (middle + mm(act, wdown_ref[...])).astype(B16)
    cot = cot_ref[...]
    gdown_ref[...] = mm(tr(act), cot)
    grad_pre = (mm(cot, wdown_ref[...], NT) * slope).astype(B16)
    gup_ref[...] = mm(tr(n2), grad_pre)
    gn2 = mm(grad_pre, wup_ref[...], NT)
    gg2_ref[...] = jnp.sum(gn2 * xhat2, axis=0, keepdims=True)
    gmid = cot.astype(F32) + norm_back(gn2, xhat2, rstd2, g2_ref[...])
    gmid_ref[...] = gmid
    branch = gmid.astype(B16)
    gout_ref[...] = mm(tr(mixed), branch)
    gmix_ref[...] = mm(branch, wout_ref[...], NT).astype(B16)

    def spread_t(low):
        return jnp.concatenate([low * mt_ref[t] for t in range(3)], axis=0)

    for half in range(2):
        gq_half = [None, None, None]
        gk_half = [None, None, None]
        gv_half = [None, None, None]

        def put(into, value, tile, tiles):
            for j in range(tiles):
                part = value[:, j * T : (j + 1) * T]
                before = into[tile + j]
                into[tile + j] = part if before is None else before + part

        for tile, tiles, heads in GROUPS:
            lanes = slice(half * W + tile * T, half * W + (tile + tiles) * T)
            masks = [head_mask(h, tile, tiles) for h in heads]
            q = q_ref[:, lanes]
            gm = gmix_ref[:, lanes]
            qm = jnp.concatenate([q * m.astype(B16) for m in masks], axis=0)
            gmm = jnp.concatenate([gm * m.astype(B16) for m in masks], axis=0)
            grad_p = mm(gmm, v_ref[:, lanes], NT)
            wide_g, tall_g, tall_p = [], [], []
            for a, h in enumerate(heads):
                head = half * 16 + h
                p = p_ref[head]
                dp = compact(grad_p[a * T : (a + 1) * T])
                gs = p * (dp - jnp.sum(p * dp, axis=-1, keepdims=True))
                bias_ref[pl.ds(head, T, stride=HEADS), :] = gs
                wide_g.append(spread(gs.astype(B16)))
                tall_g.append(spread_t(jnp.transpose(gs).astype(B16)))
                tall_p.append(spread_t(jnp.transpose(p).astype(B16)))
            o = mm(jnp.concatenate(wide_g, axis=0), k_ref[:, lanes])
            total = o[:T] * masks[0]
            for a in range(1, len(heads)):
                total = total + o[a * T : (a + 1) * T] * masks[a]
            put(gq_half, total, tile, tiles)
            put(gk_half, mm(jnp.concatenate(tall_g, axis=1), qm), tile, tiles)
            put(gv_half, mm(jnp.concatenate(tall_p, axis=1), gmm), tile, tiles)
        for j in range(3):
            lanes = slice(half * W + j * T, half * W + (j + 1) * T)
            gq_ref[:, lanes] = (gq_half[j] * scaling).astype(B16)
            gk_ref[:, lanes] = (gk_half[j] * scaling).astype(B16)
            gv_ref[:, lanes] = gv_half[j].astype(B16)

    n1t = n1t_ref[...]
    gqkv_ref[:, :D] = mm(n1t[:, T : 2 * T], gq_ref[...])
    gqkv_ref[:, D : 2 * D] = mm(n1t, gk_ref[...])
    gqkv_ref[:, 2 * D :] = mm(n1t, gv_ref[...])
    gn1 = mm(gk_ref[...], wqkv_ref[:, D : 2 * D], NT) + mm(gv_ref[...], wqkv_ref[:, 2 * D :], NT)
    gn1_own = gn1[T : 2 * T] + mm(gq_ref[...], wqkv_ref[:, :D], NT)
    gn1_ref[0:T] = gn1[:T]
    gn1_ref[T : 2 * T] = gn1_own
    gn1_ref[2 * T :] = gn1[2 * T :]
    gg1_ref[...] = jnp.sum(gn1_ref[...] * xhat_ref[...], axis=0, keepdims=True)

    gmw_ref[...] = jnp.zeros_like(gmw_ref)
    ginner_ref[...] = jnp.zeros_like(ginner_ref)
    ghop_ref[...] = jnp.zeros_like(ghop_ref)
    gedge_ref[...] = jnp.zeros_like(gedge_ref)

    def back_step(c, _):
        at = pl.ds(pl.multiple_of(c * CHUNK, CHUNK), CHUNK)
        off8 = off_ref[at, :]
        hop8 = hopi_ref[at, :]
        edge8 = edgei_ref[at, :]
        goff = []
        sums = [jnp.zeros((T, T), F32) for _ in range(3)]
        for s in range(0, CHUNK, 2):
            here = slice(s * T, (s + 2) * T)
            lanes = pl.ds(pl.multiple_of(c * PAIRS + s * T, 2 * T), 2 * T)
            base = (c * CHUNK + s) * HEADS
            gs = jnp.concatenate(
                [
                    bias_ref[pl.ds(pl.multiple_of(base, HEADS), HEADS), :],
                    bias_ref[pl.ds(pl.multiple_of(base + HEADS, HEADS), HEADS), :],
                ],
                axis=1,
            )
            hop = two(hop8, s)
            edge = two(edge8, s)
            hop_g = jnp.broadcast_to(hop >> 7, (HEADS, 2 * T))
            edge_g = jnp.broadcast_to(edge >> 7, (HEADS, 2 * T))
            for g in range(4):
                lhsh_ref[g * HEADS : (g + 1) * HEADS, here] = jnp.where(hop_g == g, gs, 0.0).astype(B16)
            for g in range(12):
                lhse_ref[g * HEADS : (g + 1) * HEADS, here] = jnp.where(edge_g == g, gs, 0.0).astype(B16)
            rhsh_ref[0:T, here] = hot(hop)
            rhsh_ref[T : 2 * T, here] = hidden_ref[:, lanes]
            rhse_ref[:, here] = hot(edge)
            grad_hidden = mm(outer_ref[...], gs.astype(B16), (((0,), (0,)), ((), ())))
            gpre = (grad_hidden * slope_ref[:, lanes]).astype(B16)
            gpre_ref[:, here] = gpre
            gfeat = mm(inner_ref[...], gpre)
            z = two(off8, s) * wide(cols_ref[0]) - wide(cols_ref[1])
            a = gfeat * jnp.exp2(wide(cols_ref[2]) - z * z)
            az = a * z
            azz = az * z
            goff.append(jnp.sum(az * wide(cols_ref[3]), axis=0, keepdims=True))
            sums[0] = sums[0] + az[:, :T] + az[:, T:]
            sums[1] = sums[1] + azz[:, :T] + azz[:, T:]
            sums[2] = sums[2] + a[:, :T] + a[:, T:]
        for n in range(3):
            gmw_ref[n] = gmw_ref[n] + sums[n]
        goff_ref[at, :] = jnp.concatenate(
            [-g[:, n * T : (n + 1) * T] for g in goff for n in range(2)], axis=0
        ) * (LOG2E ** 0.0)
        ghop_ref[...] += mm(lhsh_ref[...], rhsh_ref[...], NT)
        gedge_ref[...] += mm(lhse_ref[...], rhse_ref[...], NT)
        ginner_ref[...] += mm(
            feat_ref[:, pl.ds(pl.multiple_of(c * PAIRS, PAIRS), PAIRS)], gpre_ref[...], NT
        )
        return 0

    lax.fori_loop(0, T // CHUNK, back_step, 0)
    gouter_ref[...] = (
        ghop_ref[0:32, T:] + ghop_ref[32:64, T:] + ghop_ref[64:96, T:] + ghop_ref[96:128, T:]
    )

    goff = goff_ref[...]
    gdist = goff * dist_ref[...]
    flat = []
    for value in (gdist, goff):
        query = jnp.sum(jnp.transpose(value), axis=0, keepdims=True)
        parts = [jnp.sum(value * m_ref[t], axis=0, keepdims=True) for t in range(3)]
        parts[1] = parts[1] + query
        flat.append(parts)
    for n in range(2):
        acc = jnp.zeros((4 * T, T), F32)
        for t in range(3):
            hit = kinds == types_ref[:, t * T : (t + 1) * T]
            acc = acc + jnp.where(hit, flat[n][t], 0.0)
        gtype_ref[n : n + 1, :] = jnp.concatenate(
            [
                jnp.sum(jnp.transpose(acc[c * T : (c + 1) * T]), axis=0, keepdims=True)
                for c in range(4)
            ],
            axis=1,
        )


def run_compute(args):
    vm = pltpu.VMEM
    out_shape = [
        jax.ShapeDtypeStruct((T, D), B16),
        jax.ShapeDtypeStruct((T, D), F32),
        jax.ShapeDtypeStruct((W, D), F32),
        jax.ShapeDtypeStruct((D, 3 * D), F32),
        jax.ShapeDtypeStruct((D, D), F32),
        jax.ShapeDtypeStruct((1, D), F32),
        jax.ShapeDtypeStruct((1, D), F32),
        jax.ShapeDtypeStruct((D, D), F32),
        jax.ShapeDtypeStruct((D, D), F32),
        jax.ShapeDtypeStruct((3, T, T), F32),
        jax.ShapeDtypeStruct((T, T), F32),
        jax.ShapeDtypeStruct((HEADS, T), F32),
        jax.ShapeDtypeStruct((T, 2 * T), F32),
        jax.ShapeDtypeStruct((3 * T, T), F32),
        jax.ShapeDtypeStruct((2, 4 * T), F32),
    ]
    scratch = [
        vm((D, W), B16),
        vm((W, D), F32),
        vm((W, 1), F32),
        vm((T, D), B16),
        vm((W, D), B16),
        vm((W, D), B16),
        vm((3, T, T), F32),
        vm((3, T, T), B16),
        vm((3, T, T), B16),
        vm((T, T), F32),
        vm((T, T), F32),
        vm((T, T), jnp.int32),
        vm((T, T), jnp.int32),
        vm((4, T, T), F32),
        vm((T, 2 * T), B16),
        vm((3 * T, T), B16),
        vm((T, T), B16),
        vm((T, T * T), B16),
        vm((T, T * T), B16),
        vm((T, T * T), F32),
        vm((T * HEADS, T), F32),
        vm((HEADS, T, T), F32),
        vm((T, D), B16),
        vm((T, D), B16),
        vm((T, D), B16),
        vm((W, D), B16),
        vm((W, D), B16),
        vm((T, T), F32),
        vm((T, PAIRS), B16),
        vm((3 * T, PAIRS), B16),
        vm((2 * T, PAIRS), B16),
        vm((T, PAIRS), B16),
        vm((T, PAIRS), B16),
    ]
    vspec = pl.BlockSpec(memory_space=pltpu.VMEM)
    sspec = pl.BlockSpec(memory_space=pltpu.SMEM)
    return pl.pallas_call(
        compute_kernel,
        out_shape=out_shape,
        in_specs=[sspec] + [vspec] * (len(args) - 1),
        out_specs=[vspec] * len(out_shape),
        scratch_shapes=scratch,
        compiler_params=pltpu.CompilerParams(vmem_limit_bytes=60 * 1024 * 1024),
        name="layer",
    )(*args)


def body(
    hidden_in,
    positions,
    atom_types,
    path_hops,
    edge_kinds,
    mol_lengths,
    qkv_weight,
    out_weight,
    attn_gain,
    ffn_gain,
    up_weight,
    down_weight,
    kernel_means,
    kernel_widths,
    kernel_inner,
    kernel_outer,
    hop_table,
    edge_table,
    atom_scale,
    atom_shift,
    out_grad,
):
    rows = lax.axis_size("rows")
    up = [(i, i + 1) for i in range(rows - 1)]
    back = [(i + 1, i) for i in range(rows - 1)]

    def window(value, axis):
        return jnp.concatenate(
            [lax.ppermute(value, "rows", up), value, lax.ppermute(value, "rows", back)], axis=axis
        )

    hid_w = window(hidden_in[0], 0)
    pos_w = window(positions[0], 1)
    types_w = window(atom_types, 1)
    (
        out, gmid, gn1, gqkv, gout, gg1, gg2, gup, gdown, gmw, ginner, gouter_t, ghop, gedge, gtype,
    ) = run_compute(
        (
            mol_lengths,
            hid_w,
            pos_w,
            types_w,
            path_hops[0],
            edge_kinds[0],
            qkv_weight,
            out_weight,
            attn_gain[None],
            ffn_gain[None],
            up_weight,
            down_weight,
            kernel_means[None],
            kernel_widths[None],
            kernel_inner,
            kernel_outer.T,
            hop_table,
            edge_table,
            atom_scale[None],
            atom_shift[None],
            out_grad[0],
        )
    )
    from_above = lax.ppermute(gn1[:T], "rows", back)
    from_below = lax.ppermute(gn1[2 * T :], "rows", up)
    gn1_own = gn1[T : 2 * T] + from_above + from_below
    xhat, rstd = normalise(hidden_in[0].astype(F32))
    grad_in = gmid + norm_back(gn1_own, xhat, rstd, attn_gain)
    inv = 1.0 / kernel_widths
    back_scale = (2.0 / LOG2E) ** 0.5
    sums = jnp.sum(gmw, axis=2)
    grad_means = sums[0] * inv * back_scale
    grad_widths = (sums[1] * (back_scale * back_scale) - sums[2]) * inv
    ghop_own = jnp.concatenate([ghop[g * HEADS : (g + 1) * HEADS, :T] for g in range(4)], axis=1)
    gedge_own = jnp.concatenate([gedge[g * HEADS : (g + 1) * HEADS] for g in range(12)], axis=1)
    summed = lax.psum(
        (
            gqkv, gout, gg1[0], gg2[0], gup, gdown, grad_means, grad_widths, ginner, gouter_t.T,
            ghop_own, gedge_own, gtype[0], gtype[1],
        ),
        ("blocks", "rows"),
    )
    return (out[None], grad_in[None]) + tuple(summed)


def solution(mesh):
    split3 = P("blocks", "rows", None)
    in_specs = (
        split3,
        P("blocks", None, "rows"),
        P("blocks", "rows"),
        split3,
        split3,
        P("blocks", None),
    ) + (P(),) * 14 + (split3,)
    out_specs = (split3, split3) + (P(),) * 14
    return jax.shard_map(body, mesh=mesh, in_specs=in_specs, out_specs=out_specs, check_vma=False)
```

time: 1320 us -> 393 us (0.30); the launches traced: 1300 us -> 392 us
  other arithmetic: 543 us -> 9.2 us
  local copies, waits for them, and re-layouts: 322 us -> 27.9 us
  matrix products: 156 us -> 0 us
  Pallas kernels: 0 us -> 64.9 us
    scatter-add x2 -> x0, other arithmetic: 470 us -> none  [the longest x1 235 us: backward_block(): jax.ops.segment_sum(grad_flat.T, block_in[7].reshape(-1), num_segments=ed...]
    gather x4 -> x0, local copies, waits for them, and re-layouts: 186 us -> none  [the longest x2 92.9 us: bias_from_features(): jnp.take(edge_table, edge_rows.reshape(-1), axis=1).astype(jnp.float32)]
    dot_general x26 -> x0, matrix products: 156 us -> none  [the longest x1 22 us: bias_from_features(): lax.dot_general(kernel_inner, flat, CONTRACT_FIRST, preferred_element_typ...]
    pallas_call x0 -> x1, Pallas kernels: none -> 64.9 us  [run_compute(): pl.pallas_call(compute_kernel, out_shape=out_shape, in_specs=[sspec] + [v...]
    reduce_sum x12 -> x4, other arithmetic: 35.3 us -> 1.33 us  [the longest x1 0.89 us: norm_back(): jnp.mean(g, axis=-1, keepdims=True)]
    reshape x5 -> x0, local copies, waits for them, and re-layouts: 27.1 us -> none  [the longest x2 16.3 us: bias_from_features(): (learned + table).reshape((kernel_outer.shape[1],) + hop_rows.shape)]
    slice x14 -> x3, local copies, waits for them, and re-layouts: 20.7 us -> 1.61 us  [the longest x1 0.79 us: body(): ghop[g * HEADS:(g + 1) * HEADS, :T]]
    unnamed x145 -> x48, local copies, waits for them, and re-layouts: 28.5 us -> 23.8 us
  transfers between devices with their start and end apart: 7 -> 9, of which waited for: 1 -> 1; matrix products, arithmetic and copies ran while one was open for 26% -> 3% of each run, Pallas kernels for 0% -> 0%
where the time goes in v1:
time: 393 us; the launch traced here: 392 us
  waiting for transfers between devices  201 us (51%)
  Pallas kernels  64.9 us (17%)
  blocking collectives  53.2 us (14%)
  local copies, waits for them, and re-layouts  27.9 us (7%)
  starting transfers between devices  21.3 us (5%)
  between operations  14.2 us (4%)
  other arithmetic  9.2 us (2%)
    psum x1, waiting for transfers between devices, body(): lax.psum((gqkv, gout, gg1[0], gg2[0], gup, gdown, grad_means, grad_widths...  201 us
    pallas_call x1, Pallas kernels, run_compute(): pl.pallas_call(compute_kernel, out_shape=out_shape, in_specs=[sspec] + [v...  64.9 us
    psum x1, blocking collectives, body(): lax.psum((gqkv, gout, gg1[0], gg2[0], gup, gdown, grad_means, grad_widths...  53.2 us
    unnamed x48, local copies, waits for them, and re-layouts  23.8 us
    ppermute x3, starting transfers between devices, window(): lax.ppermute(value, 'rows', up)  12.4 us
  transfers between devices with their start and end apart: 9, of which 1 were waited for; matrix products, arithmetic and copies ran while one was open for 3% of the time, Pallas kernels for 0%

profile of v1, /device:TPU:0, one launch (start us, length us, event | category | flops | bytes accessed | tf_op | source)
XLA Modules:
  0.0 391.5 jit_solution(11700192712144688297)
XLA Ops:
  7.2 0.0 all-reduce.4.cloned.1.call-start
  7.2 1.3 collective-permute-start.5
  8.5 3.0 collective-permute-start.4
  11.6 1.3 collective-permute-start.1
  12.9 5.1 %collective-permute-start = (bf16[128,768]{1,0:T(8,128)(2,1)}, bf16[128,768]{1,0:T(8,128)(2,1)S(1)}, u32[]{:S(2)}, u32[]{:S(2)}) collective-permute-start(bf16[128,768]{1,0:T(8,128)(2,1)} %bitcast.27), channel_id=1, source_target_pairs={{0,1},{1,2},{2,3},{4,5},{5,6},{6,7},{8,9},{9,10},{10,11},{12,13},{... | collective-permute-start | bytes 589832 | tf_op jit(solution)/shard_map/ppermute | solution.py:580
  18.0 1.3 collective-permute-start.3
  19.3 1.3 broadcast_in_dim.29.g1_ref
  20.6 1.3 broadcast_in_dim.30.g2_ref
  21.8 0.0 collective-permute-done.5
  21.8 4.3 %collective-permute-start.2 = (bf16[3,128]{1,0:T(4,128)(2,1)}, bf16[3,128]{1,0:T(4,128)(2,1)S(1)}, u32[]{:S(2)}, u32[]{:S(2)}) collective-permute-start(bf16[3,128]{1,0:T(4,128)(2,1)} %bitcast.40), channel_id=1, source_target_pairs={{0,1},{1,2},{2,3},{4,5},{5,6},{6,7},{8,9},{9,10},{10,11},{12,13},{... | collective-permute-start | bytes 2312 | tf_op jit(solution)/shard_map/ppermute | solution.py:580
  26.1 0.0 collective-permute-done.4
  26.1 1.2 pad_add_fusion.types_ref
  27.3 0.0 collective-permute-done.3
  27.3 0.0 collective-permute-done.2
  27.3 1.3 pad_maximum_fusion.2.pos_ref
  28.6 0.0 collective-permute-done.1
  28.6 0.0 collective-permute-done
  28.6 1.8 pad_maximum_fusion.hid_ref
  30.4 64.9 %layer.1 = (bf16[128,768]{1,0:T(8,128)(2,1)}, f32[128,768]{1,0:T(8,128)}, f32[384,768]{1,0:T(8,128)}, f32[768,2304]{1,0:T(8,128)}, f32[768,768]{1,0:T(8,128)}, /...) custom-call(s32[1,16]{1,0:T(1,128)} %lens_ref.1, ...), custom_call_target="tpu_custom_call" | custom-call | tf_op jit(solution)/shard_map/layer/pallas_call | solution.py:540
  95.3 0.7 constant_dynamic-update-slice_fusion.11
  96.0 0.7 constant_dynamic-update-slice_fusion.10
  96.7 0.7 constant_dynamic-update-slice_fusion.9
  97.4 0.7 constant_dynamic-update-slice_fusion.8
  98.2 0.7 constant_dynamic-update-slice_fusion.7
  98.9 0.7 constant_dynamic-update-slice_fusion.6
  99.6 0.7 constant_dynamic-update-slice_fusion.5
  100.3 0.7 constant_dynamic-update-slice_fusion.4
  101.0 0.7 constant_dynamic-update-slice_fusion.3
  101.8 0.7 constant_dynamic-update-slice_fusion.2
  102.5 0.7 constant_dynamic-update-slice_fusion.1
  103.2 0.8 fusion.13
  104.0 0.7 pad_maximum_fusion.1
  104.7 0.0 copy-start.8
  104.7 0.0 copy-start.11
  104.7 0.0 all-reduce.4.cloned.1.call-update
  104.7 0.9 copy-done
  105.6 0.1 convert_reduce_fusion
  105.7 0.2 fusion.9
  105.9 0.6 add_rsqrt_fusion
  106.5 0.0 copy-done.12
  106.5 0.1 fusion.12
  106.6 3.7 collective-permute-start.7
  110.3 1.3 collective-permute-start.6
  111.6 0.0 copy-done.14
  111.6 0.0 copy-done.13
  111.6 0.0 copy-done.8
  111.6 0.1 reduce_sum.49
  111.8 0.7 bitcast_multiply_fusion
  112.5 0.8 fusion.14
  113.2 53.2 %all-reduce = (f32[768]{0:T(1024)}, f32[768]{0:T(1024)}, f32[128]{0:T(128)}, f32[128]{0:T(128)}, f32[128,32]{0,1:T(8,128)}, /*index=5*/f32[512]{0:T(512)}, f32[512]{0:T(512)}) all-reduce(f32[768]{0:T(1024)S(1)} %reduce, f32[768]{0:T(1024)S(1)} %reduce.1, f32[128]{0:T(128)S(1)} %fusion.10, ...), channel_id=1, replica_groups=mesh['blocks'=8,'rows'=4] {'blocks','rows'}, use_global_device_ids=true, to_apply=%region_6.0 | all-reduce | flops 6912 | bytes 55296 | tf_op jit(solution)/shard_map/psum | solution.py:625
  166.4 0.0 collective-permute-done.7
  166.4 0.0 collective-permute-done.6
  166.4 0.9 fusion.11
  167.3 1.6 fusion.8
  168.9 200.8 %all-reduce.4.cloned.1.call-done = (f32[768,2304]{1,0:T(8,128)}, f32[768,768]{1,0:T(8,128)}, f32[768,768]{1,0:T(8,128)}, f32[768,768]{1,0:T(8,128)}, f32[128,128...) async-done(((f32[768,2304]{1,0:T(8,128)}, f32[768,768]{1,0:T(8,128)}, f32[768,768]{1,0:T(8,128)}, f32[768,768]{1,0:T(8,128)}, f32[128,128]{1,0:T(8,128)}, ...) | async-done | bytes 14483472 | tf_op jit(solution)/shard_map/psum | solution.py:625
  369.7 6.6 %copy.55 = f32[768,2304]{1,0:T(8,128)} copy(f32[768,2304]{1,0:T(8,128)} %get-tuple-element.78) | data formatting | bytes 14155776
  376.3 1.4 copy.56
  377.7 1.1 copy-done.2
  378.8 1.4 copy.57
  380.2 1.1 copy-done.1
  381.3 1.4 copy.58
  382.7 0.6 copy.59
  383.4 0.6 copy.60
  384.0 0.7 copy.61
  (26 shorter events, 0.1 us)
Async XLA Ops:
  7.2 362.5 %all-reduce.4.cloned.1.call-start = ((), (), s32[]{:S(2)}) async-start(), calls=%async_computation | async-start | bytes 28966912 | tf_op jit(solution)/shard_map/psum | solution.py:625
  7.2 14.6 %collective-permute-start.5 = (s32[1,128]{1,0:T(1,128)}, s32[1,128]{1,0:T(1,128)S(1)}, u32[]{:S(2)}, u32[]{:S(2)}) collective-permute-start(s32[1,128]{1,0:T(1,128)} %param.23), channel_id=1, source_target_pairs={{1,0},{2,1},{3,2},{5,4},{6,5},{7,6},{9,8},{10,9},{11,10},{13,12},{... | collective-permute-start | bytes 1544 | tf_op jit(solution)/shard_map/ppermute | solution.py:580
  8.5 17.6 %collective-permute-start.4 = (s32[1,128]{1,0:T(1,128)}, s32[1,128]{1,0:T(1,128)S(1)}, u32[]{:S(2)}, u32[]{:S(2)}) collective-permute-start(s32[1,128]{1,0:T(1,128)} %param.23), channel_id=1, source_target_pairs={{0,1},{1,2},{2,3},{4,5},{5,6},{6,7},{8,9},{9,10},{10,11},{12,13},{... | collective-permute-start | bytes 1544 | tf_op jit(solution)/shard_map/ppermute | solution.py:580
  11.6 17.0 %collective-permute-start.1 = (bf16[128,768]{1,0:T(8,128)(2,1)}, bf16[128,768]{1,0:T(8,128)(2,1)S(1)}, u32[]{:S(2)}, u32[]{:S(2)}) collective-permute-start(bf16[128,768]{1,0:T(8,128)(2,1)} %bitcast.26), channel_id=1, source_target_pairs={{1,0},{2,1},{3,2},{5,4},{6,5},{7,6},{9,8},{10,9},{11,10},{13,12},{... | collective-permute-start | bytes 589832 | tf_op jit(solution)/shard_map/ppermute | solution.py:580
  12.9 15.7 %collective-permute-start = (bf16[128,768]{1,0:T(8,128)(2,1)}, bf16[128,768]{1,0:T(8,128)(2,1)S(1)}, u32[]{:S(2)}, u32[]{:S(2)}) collective-permute-start(bf16[128,768]{1,0:T(8,128)(2,1)} %bitcast.27), channel_id=1, source_target_pairs={{0,1},{1,2},{2,3},{4,5},{5,6},{6,7},{8,9},{9,10},{10,11},{12,13},{... | collective-permute-start | bytes 589832 | tf_op jit(solution)/shard_map/ppermute | solution.py:580
  18.0 9.3 %collective-permute-start.3 = (bf16[3,128]{1,0:T(4,128)(2,1)}, bf16[3,128]{1,0:T(4,128)(2,1)S(1)}, u32[]{:S(2)}, u32[]{:S(2)}) collective-permute-start(bf16[3,128]{1,0:T(4,128)(2,1)} %bitcast.39), channel_id=1, source_target_pairs={{1,0},{2,1},{3,2},{5,4},{6,5},{7,6},{9,8},{10,9},{11,10},{13,12},{... | collective-permute-start | bytes 2312 | tf_op jit(solution)/shard_map/ppermute | solution.py:580
  21.8 5.5 %collective-permute-start.2 = (bf16[3,128]{1,0:T(4,128)(2,1)}, bf16[3,128]{1,0:T(4,128)(2,1)S(1)}, u32[]{:S(2)}, u32[]{:S(2)}) collective-permute-start(bf16[3,128]{1,0:T(4,128)(2,1)} %bitcast.40), channel_id=1, source_target_pairs={{0,1},{1,2},{2,3},{4,5},{5,6},{6,7},{8,9},{9,10},{10,11},{12,13},{... | collective-permute-start | bytes 2312 | tf_op jit(solution)/shard_map/ppermute | solution.py:580
  104.0 0.7 copy-start.6
  104.7 0.9 copy-start
  104.7 1.9 copy-start.4
  104.7 6.9 %copy-start.14 = (f32[1,768]{1,0:T(1,128)S(1)}, f32[1,768]{1,0:T(1,128)}, u32[]{:S(2)}) copy-start(f32[1,768]{1,0:T(1,128)} %get-tuple-element.36) | copy-start | bytes 9220
  104.7 6.9 %copy-start.13 = (f32[1,768]{1,0:T(1,128)S(1)}, f32[1,768]{1,0:T(1,128)}, u32[]{:S(2)}) copy-start(f32[1,768]{1,0:T(1,128)} %get-tuple-element.37) | copy-start | bytes 9220
  104.7 6.9 %copy-start.8 = (f32[3,128,128]{2,1,0:T(8,128)S(1)}, f32[3,128,128]{2,1,0:T(8,128)}, u32[]{:S(2)}) copy-start(f32[3,128,128]{2,1,0:T(8,128)} %get-tuple-element.40) | copy-start | bytes 589828
  104.7 61.7 %copy-start.11 = (f32[768]{0:T(1024)S(1)}, f32[768]{0:T(1024)}, u32[]{:S(2)}) copy-start(f32[768]{0:T(1024)} %param.29) | copy-start | bytes 9220
  105.6 61.7 %copy-start.5 = (f32[128,768]{1,0:T(8,128)S(1)}, f32[128,768]{1,0:T(8,128)}, u32[]{:S(2)}) copy-start(f32[128,768]{1,0:T(8,128)} %get-tuple-element.32) | copy-start | bytes 1179652
  105.7 0.8 copy-start.12
  106.6 59.8 %collective-permute-start.7 = (f32[128,768]{1,0:T(8,128)S(1)}, f32[128,768]{1,0:T(8,128)S(1)}, u32[]{:S(2)}, u32[]{:S(2)}) collective-permute-start(f32[128,768]{1,0:T(8,128)S(1)} %get-tuple-element.66), channel_id=1, source_target_pairs={{0,1},{1,2},{2,3},{4,5},{5,6},{6,7},{8,9},{9,10},{10,11},{12,13},{... | collective-permute-start | bytes 1179656 | tf_op jit(solution)/shard_map/ppermute | solution.py:614
  110.3 56.2 %collective-permute-start.6 = (f32[128,768]{1,0:T(8,128)S(1)}, f32[128,768]{1,0:T(8,128)S(1)}, u32[]{:S(2)}, u32[]{:S(2)}) collective-permute-start(f32[128,768]{1,0:T(8,128)S(1)} %get-tuple-element.65), channel_id=1, source_target_pairs={{1,0},{2,1},{3,2},{5,4},{6,5},{7,6},{9,8},{10,9},{11,10},{13,12},{... | collective-permute-start | bytes 1179656 | tf_op jit(solution)/shard_map/ppermute | solution.py:613
  369.7 6.6 %copy-start.3 = (f32[768,768]{1,0:T(8,128)S(1)}, f32[768,768]{1,0:T(8,128)}, u32[]{:S(2)}) copy-start(f32[768,768]{1,0:T(8,128)} %get-tuple-element.79) | copy-start | bytes 7077892
  376.3 2.5 copy-start.2
  378.8 2.5 copy-start.1
  381.3 1.4 copy-start.10
  381.3 2.0 copy-start.9
  381.3 2.7 copy-start.7
Sparse Core Ops, SparseCore 0:
  104.9 264.7 all-reduce.3

commit v2 on v1

--- a/solution.py
+++ b/solution.py
@@ -68,11 +68,140 @@
     return jnp.transpose(jnp.broadcast_to(row, (T, T)))
 
 
+def z_split():
+    count = lax.axis_size("blocks") // 2
+    inner = min(count, 4)
+    return inner, count // inner
+
+
+def start_all(copies):
+    for copy in copies:
+        copy.start()
+
+
+class Chain:
+    def __init__(self, place, src, r0, r1, r2, rz, ro, final, out, send, recv, local, swap):
+        c, x, y, z, inner, outer = place
+        self.inner, self.outer = inner, outer
+        self.zi = z % inner
+        row, block = 2 * x + c, 2 * z + y
+        pc = (block, 2 * x + 1 - c)
+        px = (block, 2 * (1 - x) + c)
+        py = (2 * z + 1 - y, row)
+        self.bits = (c, y, x) if swap else (c, x, y)
+        self.partners = (pc, py, px) if swap else (pc, px, py)
+        self.peers = [
+            (2 * (z - self.zi + (self.zi + k) % inner) + y, row) for k in range(1, inner)
+        ]
+        self.far = [
+            (2 * (self.zi + inner * ((z // inner + k) % outer)) + y, row) for k in range(1, outer)
+        ]
+        self.src, self.bufs, self.rz, self.ro = src, (r0, r1, r2), rz, ro
+        self.final, self.out = final, out
+        self.send, self.recv, self.local = send, recv, local
+        self.starts, self.sizes = [0], [src.shape[0]]
+        for bit in self.bits:
+            half = self.sizes[-1] // 2
+            self.starts.append(self.starts[-1] + bit * half)
+            self.sizes.append(half)
+        self.piece = self.sizes[-1] // inner
+        self.mine = self.starts[3] + self.zi * self.piece
+        self.flying = []
+        self.used = 0
+        self.todo = [self.scatter(0), self.scatter(1), self.scatter(2), self.scatter_z]
+        if outer > 1:
+            self.todo += [self.exchange]
+        self.todo += [self.gather_z, self.gather(2), self.gather(1), self.gather(0)]
+        self.left = len(self.todo) + 1
+
+    @staticmethod
+    def at(start, size):
+        return pl.ds(pl.multiple_of(start, 16), size)
+
+    def go(self, src, dst, device):
+        copy = pltpu.make_async_remote_copy(
+            src_ref=src,
+            dst_ref=dst,
+            send_sem=self.send.at[self.used],
+            recv_sem=self.recv.at[self.used],
+            device_id=device,
+            device_id_type=pl.DeviceIdType.MESH,
+        )
+        self.used += 1
+        copy.start()
+        self.flying.append(copy)
+
+    def add(self, start, size, others, into=None):
+        block = 16
+        while block < 128 and size % (2 * block) == 0:
+            block *= 2
+
+        def one(i, _):
+            here = pl.ds(pl.multiple_of(i * block, 16), block)
+            there = self.at(start + i * block, block)
+            total = self.src[there, :].astype(F32)
+            for other in others:
+                total = total + other[here, :].astype(F32)
+            if into is None:
+                self.src[there, :] = total.astype(B16)
+            else:
+                into[here, :] = total.astype(B16)
+            return 0
+
+        lax.fori_loop(0, size // block, one, 0)
+
+    def scatter(self, k):
+        def run():
+            if k > 0:
+                self.add(self.starts[k], self.sizes[k], [self.bufs[k - 1]])
+            half = self.sizes[k + 1]
+            start = self.starts[k] + (1 - self.bits[k]) * half
+            self.go(self.src.at[self.at(start, half)], self.bufs[k], self.partners[k])
+
+        return run
+
+    def scatter_z(self):
+        self.add(self.starts[3], self.sizes[3], [self.bufs[2]])
+        for k, peer in enumerate(self.peers):
+            start = self.starts[3] + ((self.zi + k + 1) % self.inner) * self.piece
+            self.go(self.src.at[self.at(start, self.piece)], self.rz.at[k], peer)
+
+    def exchange(self):
+        self.add(self.mine, self.piece, [self.rz.at[k] for k in range(self.inner - 1)])
+        for k, peer in enumerate(self.far):
+            self.go(self.src.at[self.at(self.mine, self.piece)], self.ro.at[k], peer)
+
+    def gather_z(self):
+        last, count = (self.ro, self.outer) if self.outer > 1 else (self.rz, self.inner)
+        self.add(self.mine, self.piece, [last.at[k] for k in range(count - 1)], self.final)
+        where = self.at(self.mine, self.piece)
+        own = pltpu.make_async_copy(self.final, self.out.at[where], self.local)
+        own.start()
+        self.flying.append(own)
+        for peer in self.peers:
+            self.go(self.final, self.out.at[where], peer)
+
+    def gather(self, k):
+        def run():
+            where = self.at(self.starts[k + 1], self.sizes[k + 1])
+            self.go(self.out.at[where], self.out.at[where], self.partners[k])
+
+        return run
+
+    def step(self):
+        for copy in self.flying:
+            copy.wait()
+        self.flying = []
+        self.left -= 1
+        if self.todo:
+            self.todo.pop(0)()
+
+
 def compute_kernel(
     lens_ref,
-    hid_ref,
+    own_ref,
     pos_ref,
-    types_ref,
+    types_in_ref,
     hops_ref,
     edges_ref,
     wqkv_ref,
@@ -91,69 +220,78 @@
     shift_ref,
     cot_ref,
     out_ref,
-    gmid_ref,
-    gn1_ref,
-    gqkv_ref,
-    gout_ref,
-    gg1_ref,
-    gg2_ref,
-    gup_ref,
-    gdown_ref,
-    gmw_ref,
-    ginner_ref,
-    gouter_ref,
-    ghop_ref,
-    gedge_ref,
-    gtype_ref,
-    n1t_ref,
-    xhat_ref,
-    rstd_ref,
-    q_ref,
-    k_ref,
-    v_ref,
-    m_ref,
-    mb_ref,
-    mt_ref,
-    off_ref,
-    dist_ref,
-    hopi_ref,
-    edgei_ref,
-    cols_ref,
-    w1_ref,
-    w2_ref,
-    innert_ref,
-    feat_ref,
-    hidden_ref,
-    slope_ref,
-    bias_ref,
-    p_ref,
-    mixed_ref,
-    gmix_ref,
-    gq_ref,
-    gk_ref,
-    gv_ref,
-    goff_ref,
-    lhsh_ref,
-    lhse_ref,
-    rhsh_ref,
-    rhse_ref,
-    gpre_ref,
+    gin_ref,
+    *rest,
 ):
+    sums_out, rest = rest[:7], rest[7:]
+    (
+        hid_ref, geo_own_ref, geo_ref, gn1_send_ref, gn1_recv_ref, halo_send, halo_recv,
+        n1t_ref, xhat_ref, rstd_ref, q_ref, k_ref, v_ref, m_ref, mb_ref, mt_ref, off_ref, dist_ref,
+        hopi_ref, edgei_ref, cols_ref, w1_ref, w2_ref, innert_ref, feat_ref, hidden_ref, slope_ref,
+        bias_ref, p_ref, mixed_ref, gmix_ref, gq_ref, gk_ref, gv_ref, goff_ref, lhsh_ref, lhse_ref,
+        rhsh_ref, rhse_ref, gpre_ref, gmid_ref, gmw_ref, ginner_ref, ghop_ref, gedge_ref, gg2_ref, gg1_ref, gn1_ref, n1_ref,
+    ) = rest[:49]
+    rest = rest[49:]
     row = lax.axis_index("rows")
     rows = lax.axis_size("rows")
-    x = hid_ref[...].astype(F32)
-    xhat, rstd = normalise(x)
-    xhat_ref[...] = xhat
-    rstd_ref[...] = rstd
-    n1 = (xhat * g1_ref[...]).astype(B16)
-    for c in range(D // T):
-        for t in range(3):
-            n1t_ref[c * T : (c + 1) * T, t * T : (t + 1) * T] = jnp.transpose(
-                n1[t * T : (t + 1) * T, c * T : (c + 1) * T]
-            )
-    q_ref[...] = mm(n1[T : 2 * T], wqkv_ref[:, :D]).astype(B16)
-    k_ref[...] = mm(n1, wqkv_ref[:, D : 2 * D]).astype(B16)
-    v_ref[...] = mm(n1, wqkv_ref[:, 2 * D :]).astype(B16)
+    block = lax.axis_index("blocks")
+    inner, outer = z_split()
+    place = (row % 2, row // 2, block % 2, block // 2, inner, outer)
+    chains = []
+    for n in range(7):
+        src, r0, r1, r2, rz, ro, final, send, recv, local = rest[10 * n : 10 * n + 10]
+        chains.append(
+            Chain(place, src, r0, r1, r2, rz, ro, final, sums_out[n], send, recv, local, n % 2 == 1)
+        )
+
+    barrier = pltpu.get_barrier_semaphore()
+    others = [(block, (row + k) % rows) for k in range(1, rows)]
+    others += [chains[0].partners[2]] + chains[0].peers + chains[0].far
+    for other in others:
+        pl.semaphore_signal(barrier, inc=1, device_id=other, device_id_type=pl.DeviceIdType.MESH)
+    pl.semaphore_wait(barrier, len(others))
+
+    geo_own_ref[...] = jnp.concatenate(
+        [pos_ref[...].astype(F32), types_in_ref[...].astype(F32), jnp.zeros((4, T), F32)], axis=0
+    )
+    next_row, last_row = (block, (row + 1) % rows), (block, (row + rows - 1) % rows)
+
+    def halo(src, dst, n, device):
+        return pltpu.make_async_remote_copy(
+            src_ref=src,
+            dst_ref=dst,
+            send_sem=halo_send.at[n],
+            recv_sem=halo_recv.at[n],
+            device_id=device,
+            device_id_type=pl.DeviceIdType.MESH,
+        )
+
+    halos = [
+        halo(geo_own_ref, geo_ref.at[0], 0, next_row),
+        halo(geo_own_ref, geo_ref.at[1], 1, last_row),
+        halo(own_ref, hid_ref.at[0], 2, next_row),
+        halo(own_ref, hid_ref.at[1], 3, last_row),
+    ]
+    start_all(halos)
+
+    for copy in halos:
+        copy.wait()
+    geo = jnp.concatenate([geo_ref[0], geo_own_ref[...], geo_ref[1]], axis=1)
+    pos = geo[0:3]
+    types = geo[3:4].astype(jnp.int32)
+    for t, tile_ref in enumerate((hid_ref.at[0], own_ref, hid_ref.at[1])):
+        here = slice(t * T, (t + 1) * T)
+        xhat, rstd = normalise(tile_ref[...].astype(F32))
+        xhat_ref[here, :] = xhat
+        rstd_ref[here, :] = rstd
+        n1_ref[here, :] = (xhat * g1_ref[...]).astype(B16)
+        for c in range(D // T):
+            n1t_ref[c * T : (c + 1) * T, here] = jnp.transpose(n1_ref[here, c * T : (c + 1) * T])
+    for j in range(0, D, 2 * T):
+        here = slice(j, j + 2 * T)
+        q_ref[:, here] = mm(n1_ref[T : 2 * T, :], wqkv_ref[:, here]).astype(B16)
+        k_ref[:, here] = mm(n1_ref[...], wqkv_ref[:, D + j : D + j + 2 * T]).astype(B16)
+        v_ref[:, here] = mm(n1_ref[...], wqkv_ref[:, 2 * D + j : 2 * D + j + 2 * T]).astype(B16)
 
     first = (row - 1) * T
     ids_row = first + lax.broadcasted_iota(jnp.int32, (1, W), 1)
@@ -172,7 +310,6 @@
         [down(shift_ref[:, c * T : (c + 1) * T]) for c in range(4)], axis=0
     )
     kinds = lax.broadcasted_iota(jnp.int32, (4 * T, T), 0)
-    pos = pos_ref[...].astype(F32)
     sel = [jnp.zeros((T, T), F32) for _ in range(5)]
     own = None
     hop_sel = jnp.zeros((T, T), jnp.int32)
@@ -184,7 +321,7 @@
         m_ref[t] = mask.astype(F32)
         mb_ref[t] = mask.astype(F32).astype(B16)
         mt_ref[t] = mask_t.astype(F32).astype(B16)
-        hit = kinds == types_ref[:, lanes]
+        hit = kinds == types[:, lanes]
         terms = (
             pos[0:1, lanes],
             pos[1:2, lanes],
@@ -195,7 +332,7 @@
         if t == 1:
             own = terms
         sel = [jnp.where(mask, v, s) for v, s in zip(terms, sel)]
-        tile = jnp.clip(row + (t - 1), 0, rows - 1)
+        tile = (row + (t - 1 + rows)) % rows
         at = pl.ds(pl.multiple_of(tile * T, T), T)
         hop_sel = jnp.where(mask, hops_ref[:, at], hop_sel)
         edge_sel = jnp.where(mask, edges_ref[:, at], edge_sel)
@@ -284,10 +421,10 @@
             jnp.where(m_ref[1] > 0, wide_scores[:, T : 2 * T], wide_scores[:, 2 * T :]),
         )
 
-    for half in range(2):
+    def attend(half, _):
         mixed_half = [None, None, None]
         for tile, tiles, heads in GROUPS:
-            lanes = slice(half * W + tile * T, half * W + (tile + tiles) * T)
+            lanes = pl.ds(pl.multiple_of(half * W + tile * T, T), tiles * T)
             masks = [head_mask(h, tile, tiles) for h in heads]
             q = q_ref[:, lanes]
             qm = jnp.concatenate([q * m.astype(B16) for m in masks], axis=0)
@@ -314,7 +451,10 @@
                 before = mixed_half[tile + j]
                 mixed_half[tile + j] = part if before is None else before + part
         for j in range(3):
-            mixed_ref[:, half * W + j * T : half * W + (j + 1) * T] = mixed_half[j].astype(B16)
+            mixed_ref[:, pl.ds(pl.multiple_of(half * W + j * T, T), T)] = mixed_half[j].astype(B16)
+        return 0
+
+    lax.fori_loop(0, 2, attend, 0)
 
     def tr(a):
         return jnp.concatenate(
@@ -322,28 +462,38 @@
         )
 
     mixed = mixed_ref[...]
-    middle = hid_ref[T : 2 * T, :].astype(F32) + mm(mixed, wout_ref[...])
+    middle = own_ref[...].astype(F32) + mm(mixed, wout_ref[...])
     xhat2, rstd2 = normalise(middle)
     n2 = (xhat2 * g2_ref[...]).astype(B16)
     act, slope = gelu_parts(mm(n2, wup_ref[...]))
     act = act.astype(B16)
     out_ref[...] = (middle + mm(act, wdown_ref[...])).astype(B16)
     cot = cot_ref[...]
-    gdown_ref[...] = mm(tr(act), cot)
+
+    def fill(n, left, right):
+        for j in range(0, D // T, 2):
+            both = mm(left, right[:, j * T : (j + 2) * T]).astype(B16)
+            chains[n].src[j * D : (j + 1) * D, :] = both[:, :T]
+            chains[n].src[(j + 1) * D : (j + 2) * D, :] = both[:, T:]
+
+    fill(0, tr(act), cot)
+    chains[0].step()
     grad_pre = (mm(cot, wdown_ref[...], NT) * slope).astype(B16)
-    gup_ref[...] = mm(tr(n2), grad_pre)
+    fill(1, tr(n2), grad_pre)
+    chains[1].step()
     gn2 = mm(grad_pre, wup_ref[...], NT)
     gg2_ref[...] = jnp.sum(gn2 * xhat2, axis=0, keepdims=True)
     gmid = cot.astype(F32) + norm_back(gn2, xhat2, rstd2, g2_ref[...])
     gmid_ref[...] = gmid
     branch = gmid.astype(B16)
-    gout_ref[...] = mm(tr(mixed), branch)
+    fill(2, tr(mixed), branch)
+    chains[2].step()
     gmix_ref[...] = mm(branch, wout_ref[...], NT).astype(B16)
 
     def spread_t(low):
         return jnp.concatenate([low * mt_ref[t] for t in range(3)], axis=0)
 
-    for half in range(2):
+    def attend_back(half, _):
         gq_half = [None, None, None]
         gk_half = [None, None, None]
         gv_half = [None, None, None]
@@ -355,7 +505,7 @@
                 into[tile + j] = part if before is None else before + part
 
         for tile, tiles, heads in GROUPS:
-            lanes = slice(half * W + tile * T, half * W + (tile + tiles) * T)
+            lanes = pl.ds(pl.multiple_of(half * W + tile * T, T), tiles * T)
             masks = [head_mask(h, tile, tiles) for h in heads]
             q = q_ref[:, lanes]
             gm = gmix_ref[:, lanes]
@@ -380,21 +530,51 @@
             put(gk_half, mm(jnp.concatenate(tall_g, axis=1), qm), tile, tiles)
             put(gv_half, mm(jnp.concatenate(tall_p, axis=1), gmm), tile, tiles)
         for j in range(3):
-            lanes = slice(half * W + j * T, half * W + (j + 1) * T)
+            lanes = pl.ds(pl.multiple_of(half * W + j * T, T), T)
             gq_ref[:, lanes] = (gq_half[j] * scaling).astype(B16)
             gk_ref[:, lanes] = (gk_half[j] * scaling).astype(B16)
             gv_ref[:, lanes] = gv_half[j].astype(B16)
-
-    n1t = n1t_ref[...]
-    gqkv_ref[:, :D] = mm(n1t[:, T : 2 * T], gq_ref[...])
-    gqkv_ref[:, D : 2 * D] = mm(n1t, gk_ref[...])
-    gqkv_ref[:, 2 * D :] = mm(n1t, gv_ref[...])
-    gn1 = mm(gk_ref[...], wqkv_ref[:, D : 2 * D], NT) + mm(gv_ref[...], wqkv_ref[:, 2 * D :], NT)
-    gn1_own = gn1[T : 2 * T] + mm(gq_ref[...], wqkv_ref[:, :D], NT)
-    gn1_ref[0:T] = gn1[:T]
-    gn1_ref[T : 2 * T] = gn1_own
-    gn1_ref[2 * T :] = gn1[2 * T :]
-    gg1_ref[...] = jnp.sum(gn1_ref[...] * xhat_ref[...], axis=0, keepdims=True)
+        return 0
+
+    lax.fori_loop(0, 2, attend_back, 0)
+
+    for t in range(3 * D // T):
+        part, lane = t // (D // T), (t % (D // T)) * T
+        source = (gq_ref, gk_ref, gv_ref)[part]
+        left = n1t_ref[:, T : 2 * T] if part == 0 else n1t_ref[...]
+        chains[3 + t % 3].src[(t // 3) * D : (t // 3 + 1) * D, :] = mm(
+            left, source[:, lane : lane + T]
+        ).astype(B16)
+    for n in range(3, 6):
+        chains[n].step()
+    for j in range(0, D, 2 * T):
+        here = slice(j, j + 2 * T)
+        part = mm(gk_ref[...], wqkv_ref[here, D : 2 * D], NT) + mm(
+            gv_ref[...], wqkv_ref[here, 2 * D :], NT
+        )
+        gn1_ref[:, here] = part[T : 2 * T] + mm(gq_ref[...], wqkv_ref[here, :D], NT)
+        gn1_send_ref[0, :, here] = part[:T].astype(B16)
+        gn1_send_ref[1, :, here] = part[2 * T :].astype(B16)
+        gg1_ref[:, here] = (
+            jnp.sum(part[:T] * xhat_ref[0:T, here], axis=0, keepdims=True)
+            + jnp.sum(gn1_ref[:, here] * xhat_ref[T : 2 * T, here], axis=0, keepdims=True)
+            + jnp.sum(part[2 * T :] * xhat_ref[2 * T :, here], axis=0, keepdims=True)
+        )
+    back_halos = [
+        halo(gn1_send_ref.at[0], gn1_recv_ref.at[0], 4, last_row),
+        halo(gn1_send_ref.at[1], gn1_recv_ref.at[1], 5, next_row),
+    ]
+    start_all(back_halos)
+    for copy in back_halos:
+        copy.wait()
+    from_next = jnp.where(row < rows - 1, gn1_recv_ref[0].astype(F32), 0.0)
+    from_last = jnp.where(row > 0, gn1_recv_ref[1].astype(F32), 0.0)
+    gin_ref[...] = gmid_ref[...] + norm_back(
+        gn1_ref[...] + from_next + from_last,
+        xhat_ref[T : 2 * T, :],
+        rstd_ref[T : 2 * T, :],
+        g1_ref[...],
+    )
 
     gmw_ref[...] = jnp.zeros_like(gmw_ref)
     ginner_ref[...] = jnp.zeros_like(ginner_ref)
@@ -455,10 +635,6 @@
         return 0
 
     lax.fori_loop(0, T // CHUNK, back_step, 0)
-    gouter_ref[...] = (
-        ghop_ref[0:32, T:] + ghop_ref[32:64, T:] + ghop_ref[64:96, T:] + ghop_ref[96:128, T:]
-    )
-
     goff = goff_ref[...]
     gdist = goff * dist_ref[...]
     flat = []
@@ -467,40 +643,113 @@
         parts = [jnp.sum(value * m_ref[t], axis=0, keepdims=True) for t in range(3)]
         parts[1] = parts[1] + query
         flat.append(parts)
+    gtype = []
     for n in range(2):
         acc = jnp.zeros((4 * T, T), F32)
         for t in range(3):
-            hit = kinds == types_ref[:, t * T : (t + 1) * T]
+            hit = kinds == types[:, t * T : (t + 1) * T]
             acc = acc + jnp.where(hit, flat[n][t], 0.0)
-        gtype_ref[n : n + 1, :] = jnp.concatenate(
-            [
-                jnp.sum(jnp.transpose(acc[c * T : (c + 1) * T]), axis=0, keepdims=True)
-                for c in range(4)
-            ],
-            axis=1,
-        )
+        gtype += [
+            jnp.sum(jnp.transpose(acc[c * T : (c + 1) * T]), axis=0, keepdims=True)
+            for c in range(4)
+        ]
+    inv = 1.0 / widths_ref[...]
+    back_scale = (2.0 / LOG2E) ** 0.5
+    s0, s1, s2 = (jnp.sum(jnp.transpose(gmw_ref[n]), axis=0, keepdims=True) for n in range(3))
+    small = [s0 * inv * back_scale, (s1 * (back_scale * back_scale) - s2) * inv]
+    for gain in (gg1_ref[...], gg2_ref[...]):
+        small += [gain[:, c * T : (c + 1) * T] for c in range(D // T)]
+    small += gtype + [jnp.zeros((10, T), F32)]
+    tail = chains[6].src
+    tail[0:128, :] = ginner_ref[...].astype(B16)
+    tail[128:256, :] = ghop_ref[:, :T].astype(B16)
+    tail[256:640, :] = gedge_ref[...].astype(B16)
+    tail[640:672, :] = (
+        ghop_ref[0:32, T:] + ghop_ref[32:64, T:] + ghop_ref[64:96, T:] + ghop_ref[96:128, T:]
+    ).astype(B16)
+    tail[672:704, :] = jnp.concatenate(small, axis=0).astype(B16)
+    tail[704:, :] = jnp.zeros((tail.shape[0] - 704, T), B16)
+    while any(chain.left for chain in chains):
+        for chain in chains:
+            if chain.left:
+                chain.step()
+
+
+def unpack_kernel(*refs):
+    ins, outs = refs[:7], refs[7:]
+    (gqkv, gout, gg1, gg2, gup, gdown, gmeans, gwidths, ginner, gouter, ghop, gedge, gscale, gshift) = outs
+    gdown[...] = ins[0][...].astype(F32)
+    gup[...] = ins[1][...].astype(F32)
+    gout[...] = ins[2][...].astype(F32)
+    for n in range(3):
+        gqkv[:, n * T : (n + 1) * T] = ins[3 + n][...].astype(F32)
+
+    @pl.when(pl.program_id(0) == 0)
+    def _():
+        tail = ins[6]
+        ginner[...] = tail[0:128, :].astype(F32)
+        for g in range(4):
+            ghop[:, g * T : (g + 1) * T] = tail[128 + 32 * g : 160 + 32 * g, :].astype(F32)
+        for g in range(12):
+            gedge[:, g * T : (g + 1) * T] = tail[256 + 32 * g : 288 + 32 * g, :].astype(F32)
+        gouter[...] = tail[640:672, :].astype(F32)
+        small = tail[672:704, :].astype(F32)
+        gmeans[...] = small[0:1]
+        gwidths[...] = small[1:2]
+        for c in range(D // T):
+            gg1[:, c * T : (c + 1) * T] = small[2 + c : 3 + c]
+            gg2[:, c * T : (c + 1) * T] = small[8 + c : 9 + c]
+        for c in range(4):
+            gscale[:, c * T : (c + 1) * T] = small[14 + c : 15 + c]
+            gshift[:, c * T : (c + 1) * T] = small[18 + c : 19 + c]
+
+
+def run_unpack(sums):
+    def whole(*shape):
+        return pl.BlockSpec(shape, lambda j: (0, 0)), jax.ShapeDtypeStruct(shape, F32)
+
+    def tile(columns):
+        return (
+            pl.BlockSpec((D, columns // 6), lambda j: (0, j)),
+            jax.ShapeDtypeStruct((D, columns), F32),
+        )
+
+    outs = (
+        tile(3 * D), tile(D), whole(1, D), whole(1, D), tile(D), tile(D), whole(1, T), whole(1, T),
+        whole(T, T), whole(HEADS, T), whole(HEADS, 4 * T), whole(HEADS, 12 * T), whole(1, 4 * T),
+        whole(1, 4 * T),
+    )
+    return pl.pallas_call(
+        unpack_kernel,
+        grid=(6,),
+        in_specs=[pl.BlockSpec((D, T), lambda j: (j, 0))] * 6
+        + [pl.BlockSpec(sums[6].shape, lambda j: (0, 0))],
+        out_specs=[o[0] for o in outs],
+        out_shape=[o[1] for o in outs],
+        compiler_params=pltpu.CompilerParams(vmem_limit_bytes=32 * 1024 * 1024),
+        name="unpack",
+    )(*sums)
 
 
 def run_compute(args):
     vm = pltpu.VMEM
-    out_shape = [
-        jax.ShapeDtypeStruct((T, D), B16),
-        jax.ShapeDtypeStruct((T, D), F32),
-        jax.ShapeDtypeStruct((W, D), F32),
-        jax.ShapeDtypeStruct((D, 3 * D), F32),
-        jax.ShapeDtypeStruct((D, D), F32),
-        jax.ShapeDtypeStruct((1, D), F32),
-        jax.ShapeDtypeStruct((1, D), F32),
-        jax.ShapeDtypeStruct((D, D), F32),
-        jax.ShapeDtypeStruct((D, D), F32),
-        jax.ShapeDtypeStruct((3, T, T), F32),
-        jax.ShapeDtypeStruct((T, T), F32),
-        jax.ShapeDtypeStruct((HEADS, T), F32),
-        jax.ShapeDtypeStruct((T, 2 * T), F32),
-        jax.ShapeDtypeStruct((3 * T, T), F32),
-        jax.ShapeDtypeStruct((2, 4 * T), F32),
-    ]
+    inner, outer = z_split()
+    unit = 8 * inner * 16
+
+    def padded(count):
+        return -(-count // unit) * unit
+
+    counts = [padded(6 * D)] * 6 + [padded(704)]
+    out_shape = [jax.ShapeDtypeStruct((T, D), B16), jax.ShapeDtypeStruct((T, D), F32)]
+    out_shape += [jax.ShapeDtypeStruct((count, T), B16) for count in counts]
     scratch = [
+        vm((2, T, D), B16),
+        vm((8, T), F32),
+        vm((2, 8, T), F32),
+        vm((2, T, D), B16),
+        vm((2, T, D), B16),
+        pltpu.SemaphoreType.DMA((6,)),
+        pltpu.SemaphoreType.DMA((6,)),
         vm((D, W), B16),
         vm((W, D), F32),
         vm((W, 1), F32),
@@ -534,16 +783,40 @@
         vm((2 * T, PAIRS), B16),
         vm((T, PAIRS), B16),
         vm((T, PAIRS), B16),
+        vm((T, D), F32),
+        vm((3, T, T), F32),
+        vm((T, T), F32),
+        vm((T, 2 * T), F32),
+        vm((3 * T, T), F32),
+        vm((1, D), F32),
+        vm((1, D), F32),
+        vm((T, D), F32),
+        vm((W, D), B16),
     ]
+    for count in counts:
+        scratch += [
+            vm((count, T), B16),
+            vm((count // 2, T), B16),
+            vm((count // 4, T), B16),
+            vm((count // 8, T), B16),
+            vm((inner - 1, count // (8 * inner), T), B16),
+            vm((max(outer - 1, 1), count // (8 * inner), T), B16),
+            vm((count // (8 * inner), T), B16),
+            pltpu.SemaphoreType.DMA((6 + 2 * (inner - 1) + outer - 1,)),
+            pltpu.SemaphoreType.DMA((6 + 2 * (inner - 1) + outer - 1,)),
+            pltpu.SemaphoreType.DMA,
+        ]
     vspec = pl.BlockSpec(memory_space=pltpu.VMEM)
     sspec = pl.BlockSpec(memory_space=pltpu.SMEM)
     return pl.pallas_call(
         compute_kernel,
         out_shape=out_shape,
         in_specs=[sspec] + [vspec] * (len(args) - 1),
-        out_specs=[vspec] * len(out_shape),
+        out_specs=[vspec] * 2 + [pl.BlockSpec(memory_space=pl.ANY)] * 7,
         scratch_shapes=scratch,
-        compiler_params=pltpu.CompilerParams(vmem_limit_bytes=60 * 1024 * 1024),
+        compiler_params=pltpu.CompilerParams(
+            vmem_limit_bytes=60 * 1024 * 1024, collective_id=0, has_side_effects=True
+        ),
         name="layer",
     )(*args)
 
@@ -571,26 +844,12 @@
     atom_shift,
     out_grad,
 ):
-    rows = lax.axis_size("rows")
-    up = [(i, i + 1) for i in range(rows - 1)]
-    back = [(i + 1, i) for i in range(rows - 1)]
-
-    def window(value, axis):
-        return jnp.concatenate(
-            [lax.ppermute(value, "rows", up), value, lax.ppermute(value, "rows", back)], axis=axis
-        )
-
-    hid_w = window(hidden_in[0], 0)
-    pos_w = window(positions[0], 1)
-    types_w = window(atom_types, 1)
-    (
-        out, gmid, gn1, gqkv, gout, gg1, gg2, gup, gdown, gmw, ginner, gouter_t, ghop, gedge, gtype,
-    ) = run_compute(
+    out, grad_in, *sums = run_compute(
         (
             mol_lengths,
-            hid_w,
-            pos_w,
-            types_w,
+            hidden_in[0],
+            positions[0],
+            atom_types,
             path_hops[0],
             edge_kinds[0],
             qkv_weight,
@@ -610,26 +869,11 @@
             out_grad[0],
         )
     )
-    from_above = lax.ppermute(gn1[:T], "rows", back)
-    from_below = lax.ppermute(gn1[2 * T :], "rows", up)
-    gn1_own = gn1[T : 2 * T] + from_above + from_below
-    xhat, rstd = normalise(hidden_in[0].astype(F32))
-    grad_in = gmid + norm_back(gn1_own, xhat, rstd, attn_gain)
-    inv = 1.0 / kernel_widths
-    back_scale = (2.0 / LOG2E) ** 0.5
-    sums = jnp.sum(gmw, axis=2)
-    grad_means = sums[0] * inv * back_scale
-    grad_widths = (sums[1] * (back_scale * back_scale) - sums[2]) * inv
-    ghop_own = jnp.concatenate([ghop[g * HEADS : (g + 1) * HEADS, :T] for g in range(4)], axis=1)
-    gedge_own = jnp.concatenate([gedge[g * HEADS : (g + 1) * HEADS] for g in range(12)], axis=1)
-    summed = lax.psum(
-        (
-            gqkv, gout, gg1[0], gg2[0], gup, gdown, grad_means, grad_widths, ginner, gouter_t.T,
-            ghop_own, gedge_own, gtype[0], gtype[1],
-        ),
-        ("blocks", "rows"),
-    )
-    return (out[None], grad_in[None]) + tuple(summed)
+    grads = run_unpack(sums)
+    flat = (2, 3, 6, 7, 12, 13)
+    grads = [g[0] if n in flat else g for n, g in enumerate(grads)]
+    grads[9] = grads[9].T
+    return (out[None], grad_in[None]) + tuple(grads)
 
 
 def solution(mesh):

time: 393 us -> 198 us (0.50)
  waiting for transfers between devices: 201 us -> 0 us
  Pallas kernels: 64.9 us -> 183 us
  blocking collectives: 53.2 us -> 0 us
  starting transfers between devices: 21.3 us -> 0 us
  local copies, waits for them, and re-layouts: 27.9 us -> 12.5 us
  between operations: 14.2 us -> 0.68 us
  other arithmetic: 9.2 us -> 1.21 us
    psum x1 -> x0, waiting for transfers between devices: 201 us -> none  [body(): lax.psum((gqkv, gout, gg1[0], gg2[0], gup, gdown, grad_means, grad_widths...]
    pallas_call x1, Pallas kernels: 64.9 us -> 178 us  [run_compute(): pl.pallas_call(compute_kernel, out_shape=out_shape, in_specs=[sspec] + [v...]
    psum x1 -> x0, blocking collectives: 53.2 us -> none  [body(): lax.psum((gqkv, gout, gg1[0], gg2[0], gup, gdown, grad_means, grad_widths...]
    ppermute x8 -> x0, starting transfers between devices: 21.2 us -> none  [the longest x3 12.4 us: window(): lax.ppermute(value, 'rows', up)]
    unnamed x48 -> x20, local copies, waits for them, and re-layouts: 23.8 us -> 9.99 us
    pallas_call x0 -> x1, Pallas kernels: none -> 5.48 us  [run_unpack(): pl.pallas_call(unpack_kernel, grid=(6,), in_specs=[pl.BlockSpec((D, T), l...]
    concatenate x4 -> x0, other arithmetic: 4.96 us -> none  [the longest x3 4.27 us: window(): jnp.concatenate([lax.ppermute(value, 'rows', up), value, lax.ppermute(val...]
  transfers between devices with their start and end apart: 9 -> 0, of which waited for: 1 -> 0; matrix products, arithmetic and copies ran while one was open for 3% -> 0% of each run, Pallas kernels for 0% -> 0%
where the time goes in v2:
time: 198 us
  Pallas kernels  183 us (92%)
  local copies, waits for them, and re-layouts  12.5 us (6%)
    pallas_call x1, Pallas kernels, run_compute(): pl.pallas_call(compute_kernel, out_shape=out_shape, in_specs=[sspec] + [v...  178 us
    unnamed x20, local copies, waits for them, and re-layouts  9.99 us
    pallas_call x1, Pallas kernels, run_unpack(): pl.pallas_call(unpack_kernel, grid=(6,), in_specs=[pl.BlockSpec((D, T), l...  5.48 us

profile of v2, /device:TPU:0, one launch (start us, length us, event | category | flops | bytes accessed | tf_op | source)
XLA Modules:
  0.0 197.9 jit_solution(16643524144878397583)
XLA Ops:
  0.6 1.3 broadcast_in_dim.24.g1_ref
  1.9 1.3 broadcast_in_dim.25.g2_ref
  3.2 178.0 %layer.1 = (bf16[128,768]{1,0:T(8,128)(2,1)}, f32[128,768]{1,0:T(8,128)}, bf16[4608,128]{1,0:T(8,128)(2,1)}, bf16[4608,128]{1,0:T(8,128)(2,1)}, bf16[4608,128]{1...) custom-call(s32[1,16]{1,0:T(1,128)} %lens_ref.1, ...), custom_call_target="tpu_custom_call" | custom-call | tf_op jit(solution)/shard_map/layer/pallas_call | solution.py:811
  181.2 0.0 copy-start
  181.2 1.3 copy-done
  182.5 0.0 copy-start.1
  182.5 1.3 copy-done.1
  183.7 0.0 copy-start.2
  183.7 1.3 copy-done.2
  185.0 0.0 copy-start.3
  185.0 1.3 copy-done.3
  186.3 0.0 copy-start.4
  186.3 1.3 copy-done.4
  187.6 0.0 copy-start.5
  187.6 1.3 copy-done.5
  188.8 0.0 copy-start.6
  188.8 0.9 copy-done.6
  189.8 0.0 copy-start.8
  189.8 0.0 copy-start.7
  189.8 5.5 %unpack.1 = (f32[768,2304]{1,0:T(8,128)}, f32[768,768]{1,0:T(8,128)}, f32[1,768]{1,0:T(1,128)S(1)}, f32[1,768]{1,0:T(1,128)S(1)}, f32[768,768]{1,0:T(8,128)}, /*...) custom-call(bf16[4608,128]{1,0:T(8,128)(2,1)S(1)} %copy-done, ...), custom_call_target="tpu_custom_call" | custom-call | tf_op jit(solution)/shard_map/unpack/pallas_call | solution.py:722
  195.3 0.6 reduce
  195.9 0.6 reduce.1
  196.5 0.0 copy-done.8
  196.5 0.7 copy.39
  197.2 0.0 copy-done.7
  197.2 0.7 copy.40
Async XLA Ops:
  181.2 1.3 copy-start
  182.5 1.3 copy-start.1
  183.7 1.3 copy-start.2
  185.0 1.3 copy-start.3
  186.3 1.3 copy-start.4
  187.6 1.3 copy-start.5
  188.8 0.9 copy-start.6
  189.8 6.7 %copy-start.8 = (bf16[128,768]{1,0:T(8,128)(2,1)S(1)}, bf16[128,768]{1,0:T(8,128)(2,1)}, u32[]{:S(2)}) copy-start(bf16[128,768]{1,0:T(8,128)(2,1)} %get-tuple-element.39) | copy-start | bytes 589828
  189.8 7.4 %copy-start.7 = (f32[128,768]{1,0:T(8,128)S(1)}, f32[128,768]{1,0:T(8,128)}, u32[]{:S(2)}) copy-start(f32[128,768]{1,0:T(8,128)} %get-tuple-element.40) | copy-start | bytes 1179652

commit v3 on v2

--- a/solution.py
+++ b/solution.py
@@ -29,6 +29,9 @@
     (1, 2, (10,)),
     (2, 1, (11, 12, 13, 14, 15)),
 )
+ORDERS = ("cyxz", "cyxz", "cxyz", "cyxz", "cyxz", "cxyz", "cyxz", "cyxz", "cxyz", "cyxz", "cxyz", "cxyz", "cyxz", "cyxz", "cxyz", "cyxz", "cxyz", "cyxz", "cxyz")
+SLOTS = {"att0": (0,), "att1": (1, 2), "att2": (3, 4), "att3": (5, 6), "att4": (7, 8), "att5": (0,), "att6": (2,), "att7": (1,), "att8": (5,), "att9": (3,), "gq1": (8,), "gq3": (4, 0), "gq6": (1,), "gq7": (9,), "gq8": (6, 3, 10), "gn1": (11, 12, 4, 0, 13, 7, 14, 1), "pair0": (2, 15, 16, 6, 3, 5, 17, 8), "pair1": (10,), "pair2": (4, 9), "pair3": (11, 0), "pair4": (7, 12, 1), "pair5": (2,), "pair6": (6, 14, 13, 3), "pair8": (5, 16, 15, 8), "pair9": (9, 4), "pair10": (17, 7, 0), "pair11": (12, 10, 2, 1, 11), "pair12": (13, 14, 6), "pair13": (16, 5, 3), "pair14": (15, 8, 9), "pair15": (4, 0, 7), "small": (17, 12, 2, 6)}
+TAIL = (10, 1, 11, 0, 5, 7, 13, 18, 14, 3, 1, 16, 2, 8, 15, 9, 5, 4, 3, 17, 2, 18, 12, 6, 10, 5, 8, 4, 11, 9, 7, 13, 18, 12, 6, 14, 8, 10, 16, 11, 7, 15, 13, 17, 9, 18, 10, 12, 14, 9, 18, 11, 16, 15, 10, 12, 17, 13, 11, 18, 14, 15, 13, 16, 14, 18, 17, 15, 16, 18, 17)
 CHUNK = 8
 PAIRS = CHUNK * T
 
@@ -39,12 +42,12 @@
 
 def gelu_parts(x):
     x2 = x * x
-    t = jnp.tanh(x * (SQRT_2_OVER_PI + (SQRT_2_OVER_PI * CUBIC) * x2))
-    half = 0.5 + 0.5 * t
-    slope = half + (0.5 * x) * (1.0 - t * t) * (
-        SQRT_2_OVER_PI + (3.0 * SQRT_2_OVER_PI * CUBIC) * x2
-    )
-    return x * half, slope
+    cubic = (SQRT_2_OVER_PI * CUBIC) * x2
+    u = x * (SQRT_2_OVER_PI + cubic)
+    half = 0.5 + 0.5 * jnp.tanh(u)
+    act = x * half
+    slope = half + act * (1.0 - half) * (2.0 * SQRT_2_OVER_PI + 6.0 * cubic)
+    return act, slope
 
 
 def normalise(v):
@@ -80,38 +83,35 @@
 
 
 class Chain:
-    def __init__(self, place, src, r0, r1, r2, rz, ro, final, out, send, recv, local, swap):
+    def __init__(self, place, order, src, bufs, far_buf, final, out, send, recv, local):
         c, x, y, z, inner, outer = place
-        self.inner, self.outer = inner, outer
-        self.zi = z % inner
+        zi = z % inner
         row, block = 2 * x + c, 2 * z + y
-        pc = (block, 2 * x + 1 - c)
-        px = (block, 2 * (1 - x) + c)
-        py = (2 * z + 1 - y, row)
-        self.bits = (c, y, x) if swap else (c, x, y)
-        self.partners = (pc, py, px) if swap else (pc, px, py)
-        self.peers = [
-            (2 * (z - self.zi + (self.zi + k) % inner) + y, row) for k in range(1, inner)
+        axes = {
+            "c": (c, [(block, 2 * x + 1 - c)]),
+            "x": (x, [(block, 2 * (1 - x) + c)]),
+            "y": (y, [(2 * z + 1 - y, row)]),
+            "z": (zi, [(2 * (z - zi + (zi + k) % inner) + y, row) for k in range(1, inner)]),
+        }
+        self.far = [
+            (2 * (zi + inner * ((z // inner + k) % outer)) + y, row) for k in range(1, outer)
         ]
-        self.far = [
-            (2 * (self.zi + inner * ((z // inner + k) % outer)) + y, row) for k in range(1, outer)
-        ]
-        self.src, self.bufs, self.rz, self.ro = src, (r0, r1, r2), rz, ro
-        self.final, self.out = final, out
+        self.src, self.bufs, self.far_buf, self.final, self.out = src, bufs, far_buf, final, out
         self.send, self.recv, self.local = send, recv, local
-        self.starts, self.sizes = [0], [src.shape[0]]
-        for bit in self.bits:
-            half = self.sizes[-1] // 2
-            self.starts.append(self.starts[-1] + bit * half)
-            self.sizes.append(half)
-        self.piece = self.sizes[-1] // inner
-        self.mine = self.starts[3] + self.zi * self.piece
+        self.stages = []
+        start, size = 0, src.shape[0]
+        for name in order:
+            mine, peers = axes[name]
+            size //= len(peers) + 1
+            self.stages.append((mine, peers, start, size))
+            start = start + mine * size
+        self.start, self.size = start, size
         self.flying = []
         self.used = 0
-        self.todo = [self.scatter(0), self.scatter(1), self.scatter(2), self.scatter_z]
+        self.todo = [self.scatter(k) for k in range(4)]
         if outer > 1:
             self.todo += [self.exchange]
-        self.todo += [self.gather_z, self.gather(2), self.gather(1), self.gather(0)]
+        self.todo += [self.finish] + [self.gather(k) for k in (2, 1, 0)]
         self.left = len(self.todo) + 1
 
     @staticmethod
@@ -119,17 +119,21 @@
         return pl.ds(pl.multiple_of(start, 16), size)
 
     def go(self, src, dst, device):
-        copy = pltpu.make_async_remote_copy(
-            src_ref=src,
-            dst_ref=dst,
-            send_sem=self.send.at[self.used],
-            recv_sem=self.recv.at[self.used],
-            device_id=device,
-            device_id_type=pl.DeviceIdType.MESH,
-        )
+        n = self.used
         self.used += 1
-        copy.start()
-        self.flying.append(copy)
+
+        def make():
+            return pltpu.make_async_remote_copy(
+                src_ref=src(),
+                dst_ref=dst(),
+                send_sem=self.send.at[n],
+                recv_sem=self.recv.at[n],
+                device_id=device,
+                device_id_type=pl.DeviceIdType.MESH,
+            )
+
+        make().start()
+        self.flying.append(make)
 
     def add(self, start, size, others, into=None):
         block = 16
@@ -150,47 +154,65 @@
 
         lax.fori_loop(0, size // block, one, 0)
 
+    def take(self, k, into=None):
+        mine, peers, start, size = self.stages[k]
+        self.add(start + mine * size, size, [self.bufs[k].at[i] for i in range(len(peers))], into)
+
     def scatter(self, k):
         def run():
             if k > 0:
-                self.add(self.starts[k], self.sizes[k], [self.bufs[k - 1]])
-            half = self.sizes[k + 1]
-            start = self.starts[k] + (1 - self.bits[k]) * half
-            self.go(self.src.at[self.at(start, half)], self.bufs[k], self.partners[k])
+                self.take(k - 1)
+            mine, peers, start, size = self.stages[k]
+            for i, peer in enumerate(peers):
+                self.go(
+                    lambda i=i: self.src.at[
+                        self.at(start + (mine + i + 1) % (len(peers) + 1) * size, size)
+                    ],
+                    lambda i=i: self.bufs[k].at[i],
+                    peer,
+                )
 
         return run
 
-    def scatter_z(self):
-        self.add(self.starts[3], self.sizes[3], [self.bufs[2]])
-        for k, peer in enumerate(self.peers):
-            start = self.starts[3] + ((self.zi + k + 1) % self.inner) * self.piece
-            self.go(self.src.at[self.at(start, self.piece)], self.rz.at[k], peer)
-
     def exchange(self):
-        self.add(self.mine, self.piece, [self.rz.at[k] for k in range(self.inner - 1)])
-        for k, peer in enumerate(self.far):
-            self.go(self.src.at[self.at(self.mine, self.piece)], self.ro.at[k], peer)
-
-    def gather_z(self):
-        last, count = (self.ro, self.outer) if self.outer > 1 else (self.rz, self.inner)
-        self.add(self.mine, self.piece, [last.at[k] for k in range(count - 1)], self.final)
-        where = self.at(self.mine, self.piece)
-        own = pltpu.make_async_copy(self.final, self.out.at[where], self.local)
-        own.start()
+        self.take(3)
+        for i, peer in enumerate(self.far):
+            self.go(
+                lambda: self.src.at[self.at(self.start, self.size)],
+                lambda i=i: self.far_buf.at[i],
+                peer,
+            )
+
+    def finish(self):
+        if self.far:
+            others = [self.far_buf.at[i] for i in range(len(self.far))]
+            self.add(self.start, self.size, others, self.final)
+        else:
+            self.take(3, self.final)
+
+        def own():
+            return pltpu.make_async_copy(
+                self.final, self.out.at[self.at(self.start, self.size)], self.local
+            )
+
+        own().start()
         self.flying.append(own)
-        for peer in self.peers:
-            self.go(self.final, self.out.at[where], peer)
+        for peer in self.stages[3][1]:
+            self.go(lambda: self.final, lambda: self.out.at[self.at(self.start, self.size)], peer)
 
     def gather(self, k):
         def run():
-            where = self.at(self.starts[k + 1], self.sizes[k + 1])
-            self.go(self.out.at[where], self.out.at[where], self.partners[k])
+            _, _, start, size = self.stages[k + 1]
+            rows = size * (len(self.stages[k + 1][1]) + 1)
+            for peer in self.stages[k][1]:
+                here = lambda: self.out.at[self.at(start, rows)]
+                self.go(here, here, peer)
 
         return run
 
     def step(self):
-        for copy in self.flying:
-            copy.wait()
+        for make in self.flying:
+            make().wait()
         self.flying = []
         self.left -= 1
         if self.todo:
@@ -204,12 +226,12 @@
     types_in_ref,
     hops_ref,
     edges_ref,
-    wqkv_ref,
-    wout_ref,
-    g1_ref,
-    g2_ref,
-    wup_ref,
-    wdown_ref,
+    wqkv_hbm,
+    wout_hbm,
+    gain1_ref,
+    gain2_ref,
+    wup_hbm,
+    wdown_hbm,
     means_ref,
     widths_ref,
     inner_ref,
@@ -229,24 +251,51 @@
         n1t_ref, xhat_ref, rstd_ref, q_ref, k_ref, v_ref, m_ref, mb_ref, mt_ref, off_ref, dist_ref,
         hopi_ref, edgei_ref, cols_ref, w1_ref, w2_ref, innert_ref, feat_ref, hidden_ref, slope_ref,
         bias_ref, p_ref, mixed_ref, gmix_ref, gq_ref, gk_ref, gv_ref, goff_ref, lhsh_ref, lhse_ref,
-        rhsh_ref, rhse_ref, gpre_ref, gmid_ref, gmw_ref, ginner_ref, ghop_ref, gedge_ref, gg2_ref, gg1_ref, gn1_ref, n1_ref,
-    ) = rest[:49]
-    rest = rest[49:]
+        rhsh_ref, rhse_ref, gpre_ref, gmid_ref, gmw_ref, ginner_ref, ghop_ref, gedge_ref, gg2_ref,
+        gg1_ref, gn1_ref, n1_ref, wqkv_ref, wout_ref, wup_ref, wdown_ref, weight_sems, iota_ref, g1_ref, g2_ref,
+    ) = rest[:57]
+    rest = rest[57:]
     row = lax.axis_index("rows")
     rows = lax.axis_size("rows")
     block = lax.axis_index("blocks")
     inner, outer = z_split()
     place = (row % 2, row // 2, block % 2, block // 2, inner, outer)
     chains = []
-    for n in range(7):
-        src, r0, r1, r2, rz, ro, final, send, recv, local = rest[10 * n : 10 * n + 10]
-        chains.append(
-            Chain(place, src, r0, r1, r2, rz, ro, final, sums_out[n], send, recv, local, n % 2 == 1)
-        )
+    for n in range(len(ORDERS)):
+        src, *bufs, far_buf, final, send, recv, local = rest[10 * n : 10 * n + 10]
+        if n < 9:
+            out, third = sums_out[n // 3], n % 3
+        elif n < 18:
+            out, third = sums_out[3 + n % 3], n // 3 - 3
+        else:
+            out, third = sums_out[6], 0
+        out = out.at[pl.ds(third * src.shape[0], src.shape[0])]
+        chains.append(Chain(place, ORDERS[n], src, bufs, far_buf, final, out, send, recv, local))
+
+    def serve(slot):
+        for n in SLOTS.get(slot, ()):
+            chains[n].step()
+
+    loads = [
+        pltpu.make_async_copy(src, dst, weight_sems.at[n])
+        for n, (src, dst) in enumerate(
+            (
+                (wqkv_hbm, wqkv_ref),
+                (wout_hbm, wout_ref),
+                (wup_hbm, wup_ref),
+                (wdown_hbm, wdown_ref),
+            )
+        )
+    ]
+    start_all(loads)
+    for gain, into in ((gain1_ref, g1_ref), (gain2_ref, g2_ref)):
+        for c in range(D // T):
+            into[:, c * T : (c + 1) * T] = gain[c : c + 1, :]
 
     barrier = pltpu.get_barrier_semaphore()
+    z_peers = next(s[1] for s, name in zip(chains[0].stages, ORDERS[0]) if name == "z")
     others = [(block, (row + k) % rows) for k in range(1, rows)]
-    others += [chains[0].partners[2]] + chains[0].peers + chains[0].far
+    others += [(2 * (block // 2) + 1 - block % 2, row)] + z_peers + chains[0].far
     for other in others:
         pl.semaphore_signal(barrier, inc=1, device_id=other, device_id_type=pl.DeviceIdType.MESH)
     pl.semaphore_wait(barrier, len(others))
@@ -274,24 +323,22 @@
     ]
     start_all(halos)
 
-    for copy in halos:
-        copy.wait()
-    geo = jnp.concatenate([geo_ref[0], geo_own_ref[...], geo_ref[1]], axis=1)
-    pos = geo[0:3]
-    types = geo[3:4].astype(jnp.int32)
-    for t, tile_ref in enumerate((hid_ref.at[0], own_ref, hid_ref.at[1])):
-        here = slice(t * T, (t + 1) * T)
-        xhat, rstd = normalise(tile_ref[...].astype(F32))
-        xhat_ref[here, :] = xhat
-        rstd_ref[here, :] = rstd
-        n1_ref[here, :] = (xhat * g1_ref[...]).astype(B16)
-        for c in range(D // T):
-            n1t_ref[c * T : (c + 1) * T, here] = jnp.transpose(n1_ref[here, c * T : (c + 1) * T])
-    for j in range(0, D, 2 * T):
-        here = slice(j, j + 2 * T)
-        q_ref[:, here] = mm(n1_ref[T : 2 * T, :], wqkv_ref[:, here]).astype(B16)
-        k_ref[:, here] = mm(n1_ref[...], wqkv_ref[:, D + j : D + j + 2 * T]).astype(B16)
-        v_ref[:, here] = mm(n1_ref[...], wqkv_ref[:, 2 * D + j : 2 * D + j + 2 * T]).astype(B16)
+    mean_col = down(means_ref[...])
+    inv_col = 1.0 / down(widths_ref[...])
+    s_col = inv_col * ((0.5 * LOG2E) ** 0.5)
+    cols_ref[0] = s_col
+    cols_ref[1] = mean_col * s_col
+    cols_ref[2] = jnp.log2(inv_col * (1.0 / SQRT_TWO_PI))
+    cols_ref[3] = inv_col * (1.0 / (0.5 * LOG2E) ** 0.5)
+    innert_ref[...] = jnp.transpose(inner_ref[...])
+    outer_t = outer_ref[...]
+    for g in range(4):
+        w1_ref[g * HEADS : (g + 1) * HEADS, 0:T] = outer_t
+        w1_ref[g * HEADS : (g + 1) * HEADS, T : 2 * T] = hop_tab_ref[:, g * T : (g + 1) * T]
+    for g in range(12):
+        w2_ref[g * HEADS : (g + 1) * HEADS, :] = edge_tab_ref[:, g * T : (g + 1) * T]
+
+    iota_ref[...] = lax.broadcasted_iota(jnp.int32, (T, 2 * T), 0).astype(F32).astype(B16)
 
     first = (row - 1) * T
     ids_row = first + lax.broadcasted_iota(jnp.int32, (1, W), 1)
@@ -310,6 +357,11 @@
         [down(shift_ref[:, c * T : (c + 1) * T]) for c in range(4)], axis=0
     )
     kinds = lax.broadcasted_iota(jnp.int32, (4 * T, T), 0)
+    for copy in halos[:2]:
+        copy.wait()
+    geo = jnp.concatenate([geo_ref[0], geo_own_ref[...], geo_ref[1]], axis=1)
+    pos = geo[0:3]
+    types = geo[3:4].astype(jnp.int32)
     sel = [jnp.zeros((T, T), F32) for _ in range(5)]
     own = None
     hop_sel = jnp.zeros((T, T), jnp.int32)
@@ -344,31 +396,30 @@
     hopi_ref[...] = hop_sel
     edgei_ref[...] = edge_sel
 
-    mean_col = down(means_ref[...])
-    inv_col = 1.0 / down(widths_ref[...])
-    s_col = inv_col * ((0.5 * LOG2E) ** 0.5)
-    cols_ref[0] = s_col
-    cols_ref[1] = mean_col * s_col
-    cols_ref[2] = jnp.log2(inv_col * (1.0 / SQRT_TWO_PI))
-    cols_ref[3] = inv_col * (1.0 / (0.5 * LOG2E) ** 0.5)
-    innert_ref[...] = jnp.transpose(inner_ref[...])
-    outer_t = outer_ref[...]
-    for g in range(4):
-        w1_ref[g * HEADS : (g + 1) * HEADS, 0:T] = outer_t
-        w1_ref[g * HEADS : (g + 1) * HEADS, T : 2 * T] = hop_tab_ref[:, g * T : (g + 1) * T]
-    for g in range(12):
-        w2_ref[g * HEADS : (g + 1) * HEADS, :] = edge_tab_ref[:, g * T : (g + 1) * T]
-
-    iota_k = lax.broadcasted_iota(jnp.int32, (T, 2 * T), 0)
-
     def two(block, s):
         return jnp.concatenate([block[s : s + 1], block[s + 1 : s + 2]], axis=1)
 
     def wide(a):
         return jnp.concatenate([a, a], axis=1)
 
+    def low16(index):
+        return jnp.broadcast_to(index.astype(F32), (16, 2 * T)).astype(B16)
+
     def hot(index):
-        return jnp.where(iota_k == (index & (T - 1)), 1.0, 0.0).astype(B16)
+        rows16 = jnp.concatenate([low16(index & (T - 1))] * 8, axis=0)
+        return jnp.where(iota_ref[...] == rows16, jnp.ones((), B16), jnp.zeros((), B16))
+
+    def bit_masks(index, bits):
+        wide_index = jnp.broadcast_to(index, (8, 2 * T))
+        return [(wide_index & (1 << b)) != 0 for b in range(bits)]
+
+    def pick(values, masks):
+        for mask in masks:
+            values = [
+                jnp.where(mask, values[i + 1], values[i]) if i + 1 < len(values) else values[i]
+                for i in range(0, len(values), 2)
+            ]
+        return values[0]
 
     def bias_step(c, _):
         at = pl.ds(pl.multiple_of(c * CHUNK, CHUNK), CHUNK)
@@ -389,21 +440,39 @@
             edge = two(edge8, s)
             low = mm(w1_ref[...], jnp.concatenate([hidden, hot(hop)], axis=0))
             high = mm(w2_ref[...], hot(edge))
-            hop_g = jnp.broadcast_to(hop >> 7, (HEADS, 2 * T))
-            edge_g = jnp.broadcast_to(edge >> 7, (HEADS, 2 * T))
-            bias = low[0:HEADS]
-            for g in range(1, 4):
-                bias = jnp.where(hop_g == g, low[g * HEADS : (g + 1) * HEADS], bias)
-            more = high[0:HEADS]
-            for g in range(1, 12):
-                more = jnp.where(edge_g == g, high[g * HEADS : (g + 1) * HEADS], more)
-            bias = bias + more
+            hop_bits = bit_masks(hop >> 7, 2)
+            edge_bits = bit_masks(edge >> 7, 4)
+            bias = jnp.concatenate(
+                [
+                    pick([low[g * HEADS + r : g * HEADS + r + 8] for g in range(4)], hop_bits)
+                    + pick([high[g * HEADS + r : g * HEADS + r + 8] for g in range(12)], edge_bits)
+                    for r in range(0, HEADS, 8)
+                ],
+                axis=0,
+            )
             base = (c * CHUNK + s) * HEADS
             bias_ref[pl.ds(pl.multiple_of(base, HEADS), HEADS), :] = bias[:, :T]
             bias_ref[pl.ds(pl.multiple_of(base + HEADS, HEADS), HEADS), :] = bias[:, T:]
         return 0
 
     lax.fori_loop(0, T // CHUNK, bias_step, 0)
+
+    for copy in halos[2:]:
+        copy.wait()
+    loads[0].wait()
+    for t, tile_ref in enumerate((hid_ref.at[0], own_ref, hid_ref.at[1])):
+        here = slice(t * T, (t + 1) * T)
+        xhat, rstd = normalise(tile_ref[...].astype(F32))
+        xhat_ref[here, :] = xhat
+        rstd_ref[here, :] = rstd
+        n1_ref[here, :] = (xhat * g1_ref[...]).astype(B16)
+        for c in range(D // T):
+            n1t_ref[c * T : (c + 1) * T, here] = jnp.transpose(n1_ref[here, c * T : (c + 1) * T])
+    for j in range(0, D, 2 * T):
+        here = slice(j, j + 2 * T)
+        q_ref[:, here] = mm(n1_ref[T : 2 * T, :], wqkv_ref[:, here]).astype(B16)
+        k_ref[:, here] = mm(n1_ref[...], wqkv_ref[:, D + j : D + j + 2 * T]).astype(B16)
+        v_ref[:, here] = mm(n1_ref[...], wqkv_ref[:, 2 * D + j : 2 * D + j + 2 * T]).astype(B16)
 
     scaling = HD ** (-0.5)
 
@@ -461,6 +530,8 @@
             [jnp.transpose(a[:, c * T : (c + 1) * T]) for c in range(a.shape[1] // T)], axis=0
         )
 
+    for copy in loads[1:]:
+        copy.wait()
     mixed = mixed_ref[...]
     middle = own_ref[...].astype(F32) + mm(mixed, wout_ref[...])
     xhat2, rstd2 = normalise(middle)
@@ -471,29 +542,29 @@
     cot = cot_ref[...]
 
     def fill(n, left, right):
-        for j in range(0, D // T, 2):
-            both = mm(left, right[:, j * T : (j + 2) * T]).astype(B16)
-            chains[n].src[j * D : (j + 1) * D, :] = both[:, :T]
-            chains[n].src[(j + 1) * D : (j + 2) * D, :] = both[:, T:]
+        for j in range(0, D, 2 * T):
+            both = mm(left, right[:, j : j + 2 * T]).astype(B16)
+            chain = chains[3 * n + j // (2 * T)]
+            chain.src[:D, :] = both[:, :T]
+            chain.src[D:, :] = both[:, T:]
+            chain.step()
+            serve(f"f{3 * n + j // (2 * T)}")
 
     fill(0, tr(act), cot)
-    chains[0].step()
     grad_pre = (mm(cot, wdown_ref[...], NT) * slope).astype(B16)
     fill(1, tr(n2), grad_pre)
-    chains[1].step()
     gn2 = mm(grad_pre, wup_ref[...], NT)
     gg2_ref[...] = jnp.sum(gn2 * xhat2, axis=0, keepdims=True)
     gmid = cot.astype(F32) + norm_back(gn2, xhat2, rstd2, g2_ref[...])
     gmid_ref[...] = gmid
     branch = gmid.astype(B16)
     fill(2, tr(mixed), branch)
-    chains[2].step()
     gmix_ref[...] = mm(branch, wout_ref[...], NT).astype(B16)
 
     def spread_t(low):
         return jnp.concatenate([low * mt_ref[t] for t in range(3)], axis=0)
 
-    def attend_back(half, _):
+    for half in range(2):
         gq_half = [None, None, None]
         gk_half = [None, None, None]
         gv_half = [None, None, None]
@@ -504,8 +575,8 @@
                 before = into[tile + j]
                 into[tile + j] = part if before is None else before + part
 
-        for tile, tiles, heads in GROUPS:
-            lanes = pl.ds(pl.multiple_of(half * W + tile * T, T), tiles * T)
+        for group, (tile, tiles, heads) in enumerate(GROUPS):
+            lanes = slice(half * W + tile * T, half * W + (tile + tiles) * T)
             masks = [head_mask(h, tile, tiles) for h in heads]
             q = q_ref[:, lanes]
             gm = gmix_ref[:, lanes]
@@ -529,24 +600,25 @@
             put(gq_half, total, tile, tiles)
             put(gk_half, mm(jnp.concatenate(tall_g, axis=1), qm), tile, tiles)
             put(gv_half, mm(jnp.concatenate(tall_p, axis=1), gmm), tile, tiles)
+            serve(f"att{5 * half + group}")
         for j in range(3):
-            lanes = pl.ds(pl.multiple_of(half * W + j * T, T), T)
+            lanes = slice(half * W + j * T, half * W + (j + 1) * T)
             gq_ref[:, lanes] = (gq_half[j] * scaling).astype(B16)
             gk_ref[:, lanes] = (gk_half[j] * scaling).astype(B16)
             gv_ref[:, lanes] = gv_half[j].astype(B16)
-        return 0
-
-    lax.fori_loop(0, 2, attend_back, 0)
-
-    for t in range(3 * D // T):
-        part, lane = t // (D // T), (t % (D // T)) * T
+
+    for n in range(9):
+        part, tile = n // 3, n % 3
         source = (gq_ref, gk_ref, gv_ref)[part]
         left = n1t_ref[:, T : 2 * T] if part == 0 else n1t_ref[...]
-        chains[3 + t % 3].src[(t // 3) * D : (t // 3 + 1) * D, :] = mm(
-            left, source[:, lane : lane + T]
-        ).astype(B16)
-    for n in range(3, 6):
-        chains[n].step()
+        right = jnp.concatenate(
+            [source[:, tile * T : (tile + 1) * T], source[:, (tile + 3) * T : (tile + 4) * T]], axis=1
+        )
+        both = mm(left, right).astype(B16)
+        chains[9 + n].src[:D, :] = both[:, :T]
+        chains[9 + n].src[D:, :] = both[:, T:]
+        chains[9 + n].step()
+        serve(f"gq{n}")
     for j in range(0, D, 2 * T):
         here = slice(j, j + 2 * T)
         part = mm(gk_ref[...], wqkv_ref[here, D : 2 * D], NT) + mm(
@@ -565,17 +637,7 @@
         halo(gn1_send_ref.at[1], gn1_recv_ref.at[1], 5, next_row),
     ]
     start_all(back_halos)
-    for copy in back_halos:
-        copy.wait()
-    from_next = jnp.where(row < rows - 1, gn1_recv_ref[0].astype(F32), 0.0)
-    from_last = jnp.where(row > 0, gn1_recv_ref[1].astype(F32), 0.0)
-    gin_ref[...] = gmid_ref[...] + norm_back(
-        gn1_ref[...] + from_next + from_last,
-        xhat_ref[T : 2 * T, :],
-        rstd_ref[T : 2 * T, :],
-        g1_ref[...],
-    )
-
+    serve("gn1")
     gmw_ref[...] = jnp.zeros_like(gmw_ref)
     ginner_ref[...] = jnp.zeros_like(ginner_ref)
     ghop_ref[...] = jnp.zeros_like(ghop_ref)
@@ -601,16 +663,20 @@
             )
             hop = two(hop8, s)
             edge = two(edge8, s)
-            hop_g = jnp.broadcast_to(hop >> 7, (HEADS, 2 * T))
-            edge_g = jnp.broadcast_to(edge >> 7, (HEADS, 2 * T))
-            for g in range(4):
-                lhsh_ref[g * HEADS : (g + 1) * HEADS, here] = jnp.where(hop_g == g, gs, 0.0).astype(B16)
-            for g in range(12):
-                lhse_ref[g * HEADS : (g + 1) * HEADS, here] = jnp.where(edge_g == g, gs, 0.0).astype(B16)
+            low_gs = gs.astype(B16)
+            halves = (low_gs[:16], low_gs[16:])
+            for index, count, into in ((hop, 4, lhsh_ref), (edge, 12, lhse_ref)):
+                group16 = low16(index >> 7)
+                for g in range(count):
+                    mask = group16 == jnp.full((), g, B16)
+                    for r in range(2):
+                        into[g * HEADS + 16 * r : g * HEADS + 16 * r + 16, here] = jnp.where(
+                            mask, halves[r], jnp.zeros((), B16)
+                        )
             rhsh_ref[0:T, here] = hot(hop)
             rhsh_ref[T : 2 * T, here] = hidden_ref[:, lanes]
             rhse_ref[:, here] = hot(edge)
-            grad_hidden = mm(outer_ref[...], gs.astype(B16), (((0,), (0,)), ((), ())))
+            grad_hidden = mm(outer_ref[...], low_gs, (((0,), (0,)), ((), ())))
             gpre = (grad_hidden * slope_ref[:, lanes]).astype(B16)
             gpre_ref[:, here] = gpre
             gfeat = mm(inner_ref[...], gpre)
@@ -632,6 +698,9 @@
         ginner_ref[...] += mm(
             feat_ref[:, pl.ds(pl.multiple_of(c * PAIRS, PAIRS), PAIRS)], gpre_ref[...], NT
         )
+        for k in range(T // CHUNK):
+            if f"pair{k}" in SLOTS:
+                pl.when(c == k)(functools.partial(serve, f"pair{k}"))
         return 0
 
     lax.fori_loop(0, T // CHUNK, back_step, 0)
@@ -660,7 +729,7 @@
     for gain in (gg1_ref[...], gg2_ref[...]):
         small += [gain[:, c * T : (c + 1) * T] for c in range(D // T)]
     small += gtype + [jnp.zeros((10, T), F32)]
-    tail = chains[6].src
+    tail = chains[18].src
     tail[0:128, :] = ginner_ref[...].astype(B16)
     tail[128:256, :] = ghop_ref[:, :T].astype(B16)
     tail[256:640, :] = gedge_ref[...].astype(B16)
@@ -669,6 +738,20 @@
     ).astype(B16)
     tail[672:704, :] = jnp.concatenate(small, axis=0).astype(B16)
     tail[704:, :] = jnp.zeros((tail.shape[0] - 704, T), B16)
+    chains[18].step()
+    serve("small")
+    for copy in back_halos:
+        copy.wait()
+    from_next = jnp.where(row < rows - 1, gn1_recv_ref[0].astype(F32), 0.0)
+    from_last = jnp.where(row > 0, gn1_recv_ref[1].astype(F32), 0.0)
+    gin_ref[...] = gmid_ref[...] + norm_back(
+        gn1_ref[...] + from_next + from_last,
+        xhat_ref[T : 2 * T, :],
+        rstd_ref[T : 2 * T, :],
+        g1_ref[...],
+    )
+    for n in TAIL:
+        chains[n].step()
     while any(chain.left for chain in chains):
         for chain in chains:
             if chain.left:
@@ -678,11 +761,13 @@
 def unpack_kernel(*refs):
     ins, outs = refs[:7], refs[7:]
     (gqkv, gout, gg1, gg2, gup, gdown, gmeans, gwidths, ginner, gouter, ghop, gedge, gscale, gshift) = outs
-    gdown[...] = ins[0][...].astype(F32)
-    gup[...] = ins[1][...].astype(F32)
-    gout[...] = ins[2][...].astype(F32)
-    for n in range(3):
-        gqkv[:, n * T : (n + 1) * T] = ins[3 + n][...].astype(F32)
+    for t in range(D // T):
+        here = slice(t * T, (t + 1) * T)
+        gdown[:, here] = ins[0][t].astype(F32)
+        gup[:, here] = ins[1][t].astype(F32)
+        gout[:, here] = ins[2][t].astype(F32)
+        for n in range(3):
+            gqkv[:, (3 * t + n) * T : (3 * t + n + 1) * T] = ins[3 + n][t].astype(F32)
 
     @pl.when(pl.program_id(0) == 0)
     def _():
@@ -696,9 +781,8 @@
         small = tail[672:704, :].astype(F32)
         gmeans[...] = small[0:1]
         gwidths[...] = small[1:2]
-        for c in range(D // T):
-            gg1[:, c * T : (c + 1) * T] = small[2 + c : 3 + c]
-            gg2[:, c * T : (c + 1) * T] = small[8 + c : 9 + c]
+        gg1[...] = small[2:8]
+        gg2[...] = small[8:14]
         for c in range(4):
             gscale[:, c * T : (c + 1) * T] = small[14 + c : 15 + c]
             gshift[:, c * T : (c + 1) * T] = small[18 + c : 19 + c]
@@ -708,27 +792,28 @@
     def whole(*shape):
         return pl.BlockSpec(shape, lambda j: (0, 0)), jax.ShapeDtypeStruct(shape, F32)
 
-    def tile(columns):
+    def rows(columns):
         return (
-            pl.BlockSpec((D, columns // 6), lambda j: (0, j)),
+            pl.BlockSpec((T, columns), lambda j: (j, 0)),
             jax.ShapeDtypeStruct((D, columns), F32),
         )
 
     outs = (
-        tile(3 * D), tile(D), whole(1, D), whole(1, D), tile(D), tile(D), whole(1, T), whole(1, T),
+        rows(3 * D), rows(D), whole(6, T), whole(6, T), rows(D), rows(D), whole(1, T), whole(1, T),
         whole(T, T), whole(HEADS, T), whole(HEADS, 4 * T), whole(HEADS, 12 * T), whole(1, 4 * T),
         whole(1, 4 * T),
     )
+    tiles = [value.reshape(6, D, T) for value in sums[:6]]
     return pl.pallas_call(
         unpack_kernel,
-        grid=(6,),
-        in_specs=[pl.BlockSpec((D, T), lambda j: (j, 0))] * 6
+        grid=(D // T,),
+        in_specs=[pl.BlockSpec((6, T, T), lambda j: (0, j, 0))] * 6
         + [pl.BlockSpec(sums[6].shape, lambda j: (0, 0))],
         out_specs=[o[0] for o in outs],
         out_shape=[o[1] for o in outs],
-        compiler_params=pltpu.CompilerParams(vmem_limit_bytes=32 * 1024 * 1024),
+        compiler_params=pltpu.CompilerParams(vmem_limit_bytes=60 * 1024 * 1024),
         name="unpack",
-    )(*sums)
+    )(*tiles, sums[6])
 
 
 def run_compute(args):
@@ -739,9 +824,10 @@
     def padded(count):
         return -(-count // unit) * unit
 
-    counts = [padded(6 * D)] * 6 + [padded(704)]
+    counts = [padded(2 * D)] * 18 + [padded(704)]
     out_shape = [jax.ShapeDtypeStruct((T, D), B16), jax.ShapeDtypeStruct((T, D), F32)]
-    out_shape += [jax.ShapeDtypeStruct((count, T), B16) for count in counts]
+    out_shape += [jax.ShapeDtypeStruct((3 * counts[0], T), B16)] * 6
+    out_shape += [jax.ShapeDtypeStruct((counts[18], T), B16)]
     scratch = [
         vm((2, T, D), B16),
         vm((8, T), F32),
@@ -792,26 +878,38 @@
         vm((1, D), F32),
         vm((T, D), F32),
         vm((W, D), B16),
+        vm((D, 3 * D), B16),
+        vm((D, D), B16),
+        vm((D, D), B16),
+        vm((D, D), B16),
+        pltpu.SemaphoreType.DMA((4,)),
+        vm((T, 2 * T), B16),
+        vm((1, D), F32),
+        vm((1, D), F32),
     ]
-    for count in counts:
+    for count, order in zip(counts, ORDERS):
+        size = count
+        scratch.append(vm((count, T), B16))
+        for name in order:
+            ways = inner if name == "z" else 2
+            size //= ways
+            scratch.append(vm((ways - 1, size, T), B16))
         scratch += [
-            vm((count, T), B16),
-            vm((count // 2, T), B16),
-            vm((count // 4, T), B16),
-            vm((count // 8, T), B16),
-            vm((inner - 1, count // (8 * inner), T), B16),
-            vm((max(outer - 1, 1), count // (8 * inner), T), B16),
-            vm((count // (8 * inner), T), B16),
+            vm((max(outer - 1, 1), size, T), B16),
+            vm((size, T), B16),
             pltpu.SemaphoreType.DMA((6 + 2 * (inner - 1) + outer - 1,)),
             pltpu.SemaphoreType.DMA((6 + 2 * (inner - 1) + outer - 1,)),
             pltpu.SemaphoreType.DMA,
         ]
     vspec = pl.BlockSpec(memory_space=pltpu.VMEM)
     sspec = pl.BlockSpec(memory_space=pltpu.SMEM)
+    aspec = pl.BlockSpec(memory_space=pl.ANY)
     return pl.pallas_call(
         compute_kernel,
         out_shape=out_shape,
-        in_specs=[sspec] + [vspec] * (len(args) - 1),
+        in_specs=[
+            sspec if n == 0 else aspec if n in (6, 7, 10, 11) else vspec for n in range(len(args))
+        ],
         out_specs=[vspec] * 2 + [pl.BlockSpec(memory_space=pl.ANY)] * 7,
         scratch_shapes=scratch,
         compiler_params=pltpu.CompilerParams(
@@ -854,8 +952,8 @@
             edge_kinds[0],
             qkv_weight,
             out_weight,
-            attn_gain[None],
-            ffn_gain[None],
+            attn_gain.reshape(6, T),
+            ffn_gain.reshape(6, T),
             up_weight,
             down_weight,
             kernel_means[None],
@@ -871,7 +969,7 @@
     )
     grads = run_unpack(sums)
     flat = (2, 3, 6, 7, 12, 13)
-    grads = [g[0] if n in flat else g for n, g in enumerate(grads)]
+    grads = [g.reshape(-1) if n in flat else g for n, g in enumerate(grads)]
     grads[9] = grads[9].T
     return (out[None], grad_in[None]) + tuple(grads)
 

time: 198 us -> 128 us (0.65)
  Pallas kernels: 183 us -> 126 us
  local copies, waits for them, and re-layouts: 12.5 us -> 1.43 us
    pallas_call x2, Pallas kernels: 183 us -> 126 us  [the longest x1 117 us: run_compute(): pl.pallas_call(compute_kernel, out_shape=out_shape, in_specs=[sspec if n...]
    unnamed x20 -> x6, local copies, waits for them, and re-layouts: 9.99 us -> 1.43 us
    broadcast_in_dim x2 -> x0, local copies, waits for them, and re-layouts: 2.53 us -> none  [the longest x1 1.27 us: body(): attn_gain[None]]
where the time goes in v3:
time: 128 us
  Pallas kernels  126 us (98%)
  local copies, waits for them, and re-layouts  1.43 us (1%)
    pallas_call x1, Pallas kernels, run_compute(): pl.pallas_call(compute_kernel, out_shape=out_shape, in_specs=[sspec if n...  117 us
    pallas_call x1, Pallas kernels, run_unpack(): pl.pallas_call(unpack_kernel, grid=(D // T,), in_specs=[pl.BlockSpec((6,...  9.22 us

profile of v3, /device:TPU:0, one launch (start us, length us, event | category | flops | bytes accessed | tf_op | source)
XLA Modules:
  0.0 128.1 jit_solution(12261792508537524078)
XLA Ops:
  0.7 116.8 %layer.1 = (bf16[128,768]{1,0:T(8,128)(2,1)}, f32[128,768]{1,0:T(8,128)}, bf16[4608,128]{1,0:T(8,128)(2,1)}, bf16[4608,128]{1,0:T(8,128)(2,1)}, bf16[4608,128]{1...) custom-call(s32[1,16]{1,0:T(1,128)} %lens_ref.1, ...), custom_call_target="tpu_custom_call" | custom-call | tf_op jit(solution)/shard_map/layer/pallas_call | solution.py:907
  117.4 0.0 copy-start.1
  117.4 0.0 copy-start
  117.4 9.2 %unpack.1 = (f32[768,2304]{1,0:T(8,128)}, f32[768,768]{1,0:T(8,128)}, f32[6,128]{1,0:T(8,128)}, f32[6,128]{1,0:T(8,128)}, f32[768,768]{1,0:T(8,128)}, /*index=5*...) custom-call(bf16[6,768,128]{2,1,0:T(8,128)(2,1)} %bitcast.27, ...), custom_call_target="tpu_custom_call" | custom-call | tf_op jit(solution)/shard_map/unpack/pallas_call | solution.py:807
  126.7 0.0 copy-done.1
  126.7 0.7 copy.39
  127.4 0.0 copy-done
  127.4 0.7 copy.40
Async XLA Ops:
  117.4 9.3 %copy-start.1 = (bf16[128,768]{1,0:T(8,128)(2,1)S(1)}, bf16[128,768]{1,0:T(8,128)(2,1)}, u32[]{:S(2)}) copy-start(bf16[128,768]{1,0:T(8,128)(2,1)} %get-tuple-element.39) | copy-start | bytes 589828
  117.4 9.9 %copy-start = (f32[128,768]{1,0:T(8,128)S(1)}, f32[128,768]{1,0:T(8,128)}, u32[]{:S(2)}) copy-start(f32[128,768]{1,0:T(8,128)} %get-tuple-element.40) | copy-start | bytes 1179652

commit v4 on v3

--- a/solution.py
+++ b/solution.py
@@ -29,9 +29,9 @@
     (1, 2, (10,)),
     (2, 1, (11, 12, 13, 14, 15)),
 )
-ORDERS = ("cyxz", "cyxz", "cxyz", "cyxz", "cyxz", "cxyz", "cyxz", "cyxz", "cxyz", "cyxz", "cxyz", "cxyz", "cyxz", "cyxz", "cxyz", "cyxz", "cxyz", "cyxz", "cxyz")
-SLOTS = {"att0": (0,), "att1": (1, 2), "att2": (3, 4), "att3": (5, 6), "att4": (7, 8), "att5": (0,), "att6": (2,), "att7": (1,), "att8": (5,), "att9": (3,), "gq1": (8,), "gq3": (4, 0), "gq6": (1,), "gq7": (9,), "gq8": (6, 3, 10), "gn1": (11, 12, 4, 0, 13, 7, 14, 1), "pair0": (2, 15, 16, 6, 3, 5, 17, 8), "pair1": (10,), "pair2": (4, 9), "pair3": (11, 0), "pair4": (7, 12, 1), "pair5": (2,), "pair6": (6, 14, 13, 3), "pair8": (5, 16, 15, 8), "pair9": (9, 4), "pair10": (17, 7, 0), "pair11": (12, 10, 2, 1, 11), "pair12": (13, 14, 6), "pair13": (16, 5, 3), "pair14": (15, 8, 9), "pair15": (4, 0, 7), "small": (17, 12, 2, 6)}
-TAIL = (10, 1, 11, 0, 5, 7, 13, 18, 14, 3, 1, 16, 2, 8, 15, 9, 5, 4, 3, 17, 2, 18, 12, 6, 10, 5, 8, 4, 11, 9, 7, 13, 18, 12, 6, 14, 8, 10, 16, 11, 7, 15, 13, 17, 9, 18, 10, 12, 14, 9, 18, 11, 16, 15, 10, 12, 17, 13, 11, 18, 14, 15, 13, 16, 14, 18, 17, 15, 16, 18, 17)
+ORDERS = ("cxyz", "cyxz", "cyzx", "cxyz", "cxyz", "cxyz", "cyxz", "cyxz", "cxyz", "cxyz", "cyxz", "cxyz", "cxyz", "cxyz", "cyxz", "cyxz", "cyxz", "cyxz", ("c", "xyz"))
+SLOTS = {"f4": (0,), "f6": (1,), "f7": (2,), "f8": (3,), "att0": (4,), "att1": (6, 5), "att2": (7, 8), "att3": (0,), "att4": (1,), "att5": (3,), "att6": (2,), "att8": (4, 6), "gq0": (5,), "gq3": (7,), "gq4": (9,), "gq5": (0, 8, 10), "gq6": (2, 11), "gq7": (1, 3, 12), "gn1": (6, 4, 13, 5), "pair0": (7, 17, 8, 0), "pair1": (1, 3, 10, 2), "pair2": (6, 11, 14, 16), "pair3": (15, 4, 5, 9), "pair4": (17, 7, 8, 12), "pair5": (1, 11, 0, 13), "pair6": (3, 10, 6, 2), "pair7": (17, 4, 14, 16), "pair8": (1, 7, 5, 15), "pair9": (11, 6, 8, 12), "pair10": (10, 9, 14, 0), "pair11": (3, 13, 7, 2), "pair12": (11, 17, 16, 4), "pair13": (1, 10, 15, 12), "pair14": (1, 5, 0, 14), "pair15": (3, 6, 13, 8), "small": (17, 3, 9, 7)}
+TAIL = (4, 10, 0, 6, 16, 15, 18, 12, 7, 2, 5, 4, 14, 11, 2, 13, 5, 8, 9, 17, 16, 10, 8, 15, 10, 12, 14, 18, 13, 11, 9, 16, 11, 17, 15, 17, 12, 14, 12, 14, 18, 13, 16, 18, 13, 15, 9, 16, 15, 9)
 CHUNK = 8
 PAIRS = CHUNK * T
 
@@ -75,11 +75,6 @@
     count = lax.axis_size("blocks") // 2
     inner = min(count, 4)
     return inner, count // inner
-
-
-def start_all(copies):
-    for copy in copies:
-        copy.start()
 
 
 class Chain:
@@ -93,6 +88,15 @@
             "y": (y, [(2 * z + 1 - y, row)]),
             "z": (zi, [(2 * (z - zi + (zi + k) % inner) + y, row) for k in range(1, inner)]),
         }
+        chip = (2 * x + y) * inner + zi
+        chips = [(chip + k) % (4 * inner) for k in range(1, 4 * inner)]
+        axes["xyz"] = (
+            chip,
+            [
+                (2 * (z - zi + n % inner) + n // inner % 2, 2 * (n // (2 * inner)) + c)
+                for n in chips
+            ],
+        )
         self.far = [
             (2 * (zi + inner * ((z // inner + k) % outer)) + y, row) for k in range(1, outer)
         ]
@@ -108,10 +112,11 @@
         self.start, self.size = start, size
         self.flying = []
         self.used = 0
-        self.todo = [self.scatter(k) for k in range(4)]
+        last = len(order) - 1
+        self.todo = [self.scatter(k) for k in range(last + 1)]
         if outer > 1:
             self.todo += [self.exchange]
-        self.todo += [self.finish] + [self.gather(k) for k in (2, 1, 0)]
+        self.todo += [self.finish] + [self.gather(k) for k in range(last - 1, -1, -1)]
         self.left = len(self.todo) + 1
 
     @staticmethod
@@ -136,23 +141,25 @@
         self.flying.append(make)
 
     def add(self, start, size, others, into=None):
-        block = 16
-        while block < 128 and size % (2 * block) == 0:
-            block *= 2
+        wide = F32 if len(others) > 1 else B16
+        block = max(n for n in range(16, 257, 16) if size % n == 0)
 
         def one(i, _):
             here = pl.ds(pl.multiple_of(i * block, 16), block)
             there = self.at(start + i * block, block)
-            total = self.src[there, :].astype(F32)
+            total = self.src[there, :].astype(wide)
             for other in others:
-                total = total + other[here, :].astype(F32)
+                total = total + other[here, :].astype(wide)
             if into is None:
                 self.src[there, :] = total.astype(B16)
             else:
                 into[here, :] = total.astype(B16)
             return 0
 
-        lax.fori_loop(0, size // block, one, 0)
+        if size == block:
+            one(0, 0)
+        else:
+            lax.fori_loop(0, size // block, one, 0)
 
     def take(self, k, into=None):
         mine, peers, start, size = self.stages[k]
@@ -175,7 +182,7 @@
         return run
 
     def exchange(self):
-        self.take(3)
+        self.take(-1)
         for i, peer in enumerate(self.far):
             self.go(
                 lambda: self.src.at[self.at(self.start, self.size)],
@@ -188,7 +195,7 @@
             others = [self.far_buf.at[i] for i in range(len(self.far))]
             self.add(self.start, self.size, others, self.final)
         else:
-            self.take(3, self.final)
+            self.take(-1, self.final)
 
         def own():
             return pltpu.make_async_copy(
@@ -197,7 +204,7 @@
 
         own().start()
         self.flying.append(own)
-        for peer in self.stages[3][1]:
+        for peer in self.stages[-1][1]:
             self.go(lambda: self.final, lambda: self.out.at[self.at(self.start, self.size)], peer)
 
     def gather(self, k):
@@ -211,6 +218,8 @@
         return run
 
     def step(self):
+        if not self.left:
+            return
         for make in self.flying:
             make().wait()
         self.flying = []
@@ -219,32 +228,9 @@
             self.todo.pop(0)()
 
 
-def compute_kernel(
-    lens_ref,
-    own_ref,
-    pos_ref,
-    types_in_ref,
-    hops_ref,
-    edges_ref,
-    wqkv_hbm,
-    wout_hbm,
-    gain1_ref,
-    gain2_ref,
-    wup_hbm,
-    wdown_hbm,
-    means_ref,
-    widths_ref,
-    inner_ref,
-    outer_ref,
-    hop_tab_ref,
-    edge_tab_ref,
-    scale_ref,
-    shift_ref,
-    cot_ref,
-    out_ref,
-    gin_ref,
-    *rest,
-):
+def compute_kernel(lens_ref, *rest):
+    inputs, rest = rest[:20], rest[20:]
+    out_hbm, gin_hbm, *rest = rest
     sums_out, rest = rest[:7], rest[7:]
     (
         hid_ref, geo_own_ref, geo_ref, gn1_send_ref, gn1_recv_ref, halo_send, halo_recv,
@@ -252,9 +238,14 @@
         hopi_ref, edgei_ref, cols_ref, w1_ref, w2_ref, innert_ref, feat_ref, hidden_ref, slope_ref,
         bias_ref, p_ref, mixed_ref, gmix_ref, gq_ref, gk_ref, gv_ref, goff_ref, lhsh_ref, lhse_ref,
         rhsh_ref, rhse_ref, gpre_ref, gmid_ref, gmw_ref, ginner_ref, ghop_ref, gedge_ref, gg2_ref,
-        gg1_ref, gn1_ref, n1_ref, wqkv_ref, wout_ref, wup_ref, wdown_ref, weight_sems, iota_ref, g1_ref, g2_ref,
-    ) = rest[:57]
-    rest = rest[57:]
+        gg1_ref, gn1_ref, n1_ref, iota_ref, g1_ref, g2_ref, out_ref, gin_ref, out_sems, load_sems,
+    ) = rest[:56]
+    held, rest = rest[56:76], rest[76:]
+    (
+        own_ref, pos_ref, types_in_ref, hops_ref, edges_ref, wqkv_ref, wout_ref, gain1_ref, gain2_ref, wup_ref,
+        wdown_ref, means_ref, widths_ref, inner_ref, outer_ref, hop_tab_ref, edge_tab_ref, scale_ref, shift_ref,
+        cot_ref,
+    ) = held
     row = lax.axis_index("rows")
     rows = lax.axis_size("rows")
     block = lax.axis_index("blocks")
@@ -262,7 +253,9 @@
     place = (row % 2, row // 2, block % 2, block // 2, inner, outer)
     chains = []
     for n in range(len(ORDERS)):
-        src, *bufs, far_buf, final, send, recv, local = rest[10 * n : 10 * n + 10]
+        count = 6 + len(ORDERS[n])
+        src, *bufs, far_buf, final, send, recv, local = rest[:count]
+        rest = rest[count:]
         if n < 9:
             out, third = sums_out[n // 3], n % 3
         elif n < 18:
@@ -277,32 +270,39 @@
             chains[n].step()
 
     loads = [
-        pltpu.make_async_copy(src, dst, weight_sems.at[n])
-        for n, (src, dst) in enumerate(
-            (
-                (wqkv_hbm, wqkv_ref),
-                (wout_hbm, wout_ref),
-                (wup_hbm, wup_ref),
-                (wdown_hbm, wdown_ref),
-            )
-        )
+        pltpu.make_async_copy(src, dst, load_sems.at[n])
+        for n, (src, dst) in enumerate(zip(inputs, held))
     ]
-    start_all(loads)
-    for gain, into in ((gain1_ref, g1_ref), (gain2_ref, g2_ref)):
-        for c in range(D // T):
-            into[:, c * T : (c + 1) * T] = gain[c : c + 1, :]
+    late = (5, 6, 9, 10, 19)
+    for n in (1, 2, 0):
+        loads[n].start()
+    for n in range(3, 20):
+        if n not in late:
+            loads[n].start()
+    for n in late:
+        loads[n].start()
 
     barrier = pltpu.get_barrier_semaphore()
-    z_peers = next(s[1] for s, name in zip(chains[0].stages, ORDERS[0]) if name == "z")
-    others = [(block, (row + k) % rows) for k in range(1, rows)]
-    others += [(2 * (block // 2) + 1 - block % 2, row)] + z_peers + chains[0].far
+    z_now = block // 2
+    near = [
+        (2 * (z_now - z_now % inner + (z_now + i) % inner) + (block + j) % 2, 2 * ((row // 2 + k) % 2) + row % 2)
+        for i in range(inner)
+        for j in range(2)
+        for k in range(2)
+        if i + j + k > 0
+    ]
+    others = [(block, 2 * (row // 2) + 1 - row % 2), (block, 2 * (1 - row // 2) + 1 - row % 2)]
+    others += near + chains[0].far
     for other in others:
         pl.semaphore_signal(barrier, inc=1, device_id=other, device_id_type=pl.DeviceIdType.MESH)
-    pl.semaphore_wait(barrier, len(others))
-
+    for n in (1, 2):
+        loads[n].wait()
     geo_own_ref[...] = jnp.concatenate(
         [pos_ref[...].astype(F32), types_in_ref[...].astype(F32), jnp.zeros((4, T), F32)], axis=0
     )
+    loads[0].wait()
+    pl.semaphore_wait(barrier, len(others))
+
     next_row, last_row = (block, (row + 1) % rows), (block, (row + rows - 1) % rows)
 
     def halo(src, dst, n, device):
@@ -315,13 +315,47 @@
             device_id_type=pl.DeviceIdType.MESH,
         )
 
-    halos = [
-        halo(geo_own_ref, geo_ref.at[0], 0, next_row),
-        halo(geo_own_ref, geo_ref.at[1], 1, last_row),
-        halo(own_ref, hid_ref.at[0], 2, next_row),
-        halo(own_ref, hid_ref.at[1], 3, last_row),
-    ]
-    start_all(halos)
+    def neighbours(forward, backward, n):
+        to_next = lambda: halo(*forward, n, next_row)
+        to_last = lambda: halo(*backward, n + 1, last_row)
+
+        def start():
+            pl.when(row < rows - 1)(lambda: to_next().start())
+            pl.when(row > 0)(lambda: to_last().start())
+
+        def wait():
+            @pl.when(row < rows - 1)
+            def _():
+                to_next().wait_send()
+                to_last().wait_recv()
+
+            @pl.when(row > 0)
+            def _():
+                to_last().wait_send()
+                to_next().wait_recv()
+
+        return start, wait
+
+    @pl.when(row == 0)
+    def _():
+        geo_ref[0] = jnp.zeros((8, T), F32)
+        hid_ref[0] = jnp.zeros((T, D), B16)
+
+    @pl.when(row == rows - 1)
+    def _():
+        geo_ref[1] = jnp.zeros((8, T), F32)
+        hid_ref[1] = jnp.zeros((T, D), B16)
+
+    geo_start, geo_wait = neighbours((geo_own_ref, geo_ref.at[0]), (geo_own_ref, geo_ref.at[1]), 0)
+    hid_start, hid_wait = neighbours((own_ref, hid_ref.at[0]), (own_ref, hid_ref.at[1]), 2)
+    geo_start()
+    hid_start()
+    for n in range(3, 20):
+        if n not in late:
+            loads[n].wait()
+    for gain, into in ((gain1_ref, g1_ref), (gain2_ref, g2_ref)):
+        for c in range(D // T):
+            into[:, c * T : (c + 1) * T] = gain[c : c + 1, :]
 
     mean_col = down(means_ref[...])
     inv_col = 1.0 / down(widths_ref[...])
@@ -357,8 +391,7 @@
         [down(shift_ref[:, c * T : (c + 1) * T]) for c in range(4)], axis=0
     )
     kinds = lax.broadcasted_iota(jnp.int32, (4 * T, T), 0)
-    for copy in halos[:2]:
-        copy.wait()
+    geo_wait()
     geo = jnp.concatenate([geo_ref[0], geo_own_ref[...], geo_ref[1]], axis=1)
     pos = geo[0:3]
     types = geo[3:4].astype(jnp.int32)
@@ -457,9 +490,8 @@
 
     lax.fori_loop(0, T // CHUNK, bias_step, 0)
 
-    for copy in halos[2:]:
-        copy.wait()
-    loads[0].wait()
+    hid_wait()
+    loads[5].wait()
     for t, tile_ref in enumerate((hid_ref.at[0], own_ref, hid_ref.at[1])):
         here = slice(t * T, (t + 1) * T)
         xhat, rstd = normalise(tile_ref[...].astype(F32))
@@ -530,8 +562,8 @@
             [jnp.transpose(a[:, c * T : (c + 1) * T]) for c in range(a.shape[1] // T)], axis=0
         )
 
-    for copy in loads[1:]:
-        copy.wait()
+    for n in late[1:]:
+        loads[n].wait()
     mixed = mixed_ref[...]
     middle = own_ref[...].astype(F32) + mm(mixed, wout_ref[...])
     xhat2, rstd2 = normalise(middle)
@@ -539,6 +571,8 @@
     act, slope = gelu_parts(mm(n2, wup_ref[...]))
     act = act.astype(B16)
     out_ref[...] = (middle + mm(act, wdown_ref[...])).astype(B16)
+    out_copy = pltpu.make_async_copy(out_ref, out_hbm, out_sems.at[0])
+    out_copy.start()
     cot = cot_ref[...]
 
     def fill(n, left, right):
@@ -632,11 +666,10 @@
             + jnp.sum(gn1_ref[:, here] * xhat_ref[T : 2 * T, here], axis=0, keepdims=True)
             + jnp.sum(part[2 * T :] * xhat_ref[2 * T :, here], axis=0, keepdims=True)
         )
-    back_halos = [
-        halo(gn1_send_ref.at[0], gn1_recv_ref.at[0], 4, last_row),
-        halo(gn1_send_ref.at[1], gn1_recv_ref.at[1], 5, next_row),
-    ]
-    start_all(back_halos)
+    gn1_start, gn1_wait = neighbours(
+        (gn1_send_ref.at[1], gn1_recv_ref.at[1]), (gn1_send_ref.at[0], gn1_recv_ref.at[0]), 4
+    )
+    gn1_start()
     serve("gn1")
     gmw_ref[...] = jnp.zeros_like(gmw_ref)
     ginner_ref[...] = jnp.zeros_like(ginner_ref)
@@ -740,8 +773,7 @@
     tail[704:, :] = jnp.zeros((tail.shape[0] - 704, T), B16)
     chains[18].step()
     serve("small")
-    for copy in back_halos:
-        copy.wait()
+    gn1_wait()
     from_next = jnp.where(row < rows - 1, gn1_recv_ref[0].astype(F32), 0.0)
     from_last = jnp.where(row > 0, gn1_recv_ref[1].astype(F32), 0.0)
     gin_ref[...] = gmid_ref[...] + norm_back(
@@ -750,12 +782,16 @@
         rstd_ref[T : 2 * T, :],
         g1_ref[...],
     )
+    gin_copy = pltpu.make_async_copy(gin_ref, gin_hbm, out_sems.at[1])
+    gin_copy.start()
     for n in TAIL:
         chains[n].step()
     while any(chain.left for chain in chains):
         for chain in chains:
             if chain.left:
                 chain.step()
+    out_copy.wait()
+    gin_copy.wait()
 
 
 def unpack_kernel(*refs):
@@ -792,9 +828,11 @@
     def whole(*shape):
         return pl.BlockSpec(shape, lambda j: (0, 0)), jax.ShapeDtypeStruct(shape, F32)
 
+    step = 384
+
     def rows(columns):
         return (
-            pl.BlockSpec((T, columns), lambda j: (j, 0)),
+            pl.BlockSpec((step, columns), lambda j: (j, 0)),
             jax.ShapeDtypeStruct((D, columns), F32),
         )
 
@@ -806,8 +844,8 @@
     tiles = [value.reshape(6, D, T) for value in sums[:6]]
     return pl.pallas_call(
         unpack_kernel,
-        grid=(D // T,),
-        in_specs=[pl.BlockSpec((6, T, T), lambda j: (0, j, 0))] * 6
+        grid=(D // step,),
+        in_specs=[pl.BlockSpec((6, step, T), lambda j: (0, j, 0))] * 6
         + [pl.BlockSpec(sums[6].shape, lambda j: (0, 0))],
         out_specs=[o[0] for o in outs],
         out_shape=[o[1] for o in outs],
@@ -878,39 +916,38 @@
         vm((1, D), F32),
         vm((T, D), F32),
         vm((W, D), B16),
-        vm((D, 3 * D), B16),
-        vm((D, D), B16),
-        vm((D, D), B16),
-        vm((D, D), B16),
-        pltpu.SemaphoreType.DMA((4,)),
         vm((T, 2 * T), B16),
         vm((1, D), F32),
         vm((1, D), F32),
+        vm((T, D), B16),
+        vm((T, D), F32),
+        pltpu.SemaphoreType.DMA((2,)),
+        pltpu.SemaphoreType.DMA((20,)),
     ]
+    scratch += [vm(arg.shape, arg.dtype) for arg in args[1:]]
     for count, order in zip(counts, ORDERS):
         size = count
+        copies = outer - 1
         scratch.append(vm((count, T), B16))
         for name in order:
-            ways = inner if name == "z" else 2
+            ways = {"z": inner, "xyz": 4 * inner}.get(name, 2)
             size //= ways
+            copies += 2 * (ways - 1)
             scratch.append(vm((ways - 1, size, T), B16))
         scratch += [
             vm((max(outer - 1, 1), size, T), B16),
             vm((size, T), B16),
-            pltpu.SemaphoreType.DMA((6 + 2 * (inner - 1) + outer - 1,)),
-            pltpu.SemaphoreType.DMA((6 + 2 * (inner - 1) + outer - 1,)),
+            pltpu.SemaphoreType.DMA((copies,)),
+            pltpu.SemaphoreType.DMA((copies,)),
             pltpu.SemaphoreType.DMA,
         ]
-    vspec = pl.BlockSpec(memory_space=pltpu.VMEM)
     sspec = pl.BlockSpec(memory_space=pltpu.SMEM)
     aspec = pl.BlockSpec(memory_space=pl.ANY)
     return pl.pallas_call(
         compute_kernel,
         out_shape=out_shape,
-        in_specs=[
-            sspec if n == 0 else aspec if n in (6, 7, 10, 11) else vspec for n in range(len(args))
-        ],
-        out_specs=[vspec] * 2 + [pl.BlockSpec(memory_space=pl.ANY)] * 7,
+        in_specs=[sspec] + [aspec] * (len(args) - 1),
+        out_specs=[aspec] * len(out_shape),
         scratch_shapes=scratch,
         compiler_params=pltpu.CompilerParams(
             vmem_limit_bytes=60 * 1024 * 1024, collective_id=0, has_side_effects=True

time: 128 us -> 121 us (0.945)
  Pallas kernels: 126 us -> 119 us
    pallas_call x2, Pallas kernels: 126 us -> 119 us  [the longest x1 111 us: run_compute(): pl.pallas_call(compute_kernel, out_shape=out_shape, in_specs=[sspec] + [a...]
where the time goes in v4:
time: 121 us
  Pallas kernels  119 us (98%)
  local copies, waits for them, and re-layouts  1.43 us (1%)
    pallas_call x1, Pallas kernels, run_compute(): pl.pallas_call(compute_kernel, out_shape=out_shape, in_specs=[sspec] + [a...  111 us
    pallas_call x1, Pallas kernels, run_unpack(): pl.pallas_call(unpack_kernel, grid=(D // step,), in_specs=[pl.BlockSpec((...  7.87 us

profile of v4, /device:TPU:0, one launch (start us, length us, event | category | flops | bytes accessed | tf_op | source)
XLA Modules:
  0.0 121.0 jit_solution(13875174275582754717)
XLA Ops:
  0.7 111.0 %layer.1 = (bf16[128,768]{1,0:T(8,128)(2,1)}, f32[128,768]{1,0:T(8,128)}, bf16[4608,128]{1,0:T(8,128)(2,1)}, bf16[4608,128]{1,0:T(8,128)(2,1)}, bf16[4608,128]{1...) custom-call(s32[1,16]{1,0:T(1,128)} %lens_ref.1, ...), custom_call_target="tpu_custom_call" | custom-call | tf_op jit(solution)/shard_map/layer/pallas_call | solution.py:946
  111.7 0.0 copy-start.1
  111.7 0.0 copy-start
  111.7 7.9 %unpack.1 = (f32[768,2304]{1,0:T(8,128)}, f32[768,768]{1,0:T(8,128)}, f32[6,128]{1,0:T(8,128)}, f32[6,128]{1,0:T(8,128)}, f32[768,768]{1,0:T(8,128)}, /*index=5*...) custom-call(bf16[6,768,128]{2,1,0:T(8,128)(2,1)} %bitcast.27, ...), custom_call_target="tpu_custom_call" | custom-call | tf_op jit(solution)/shard_map/unpack/pallas_call | solution.py:845
  119.6 0.0 copy-done.1
  119.6 0.7 copy.39
  120.3 0.0 copy-done
  120.3 0.7 copy.40
Async XLA Ops:
  111.7 7.9 %copy-start.1 = (bf16[128,768]{1,0:T(8,128)(2,1)S(1)}, bf16[128,768]{1,0:T(8,128)(2,1)}, u32[]{:S(2)}) copy-start(bf16[128,768]{1,0:T(8,128)(2,1)} %get-tuple-element.39) | copy-start | bytes 589828
  111.7 8.6 %copy-start = (f32[128,768]{1,0:T(8,128)S(1)}, f32[128,768]{1,0:T(8,128)}, u32[]{:S(2)}) copy-start(f32[128,768]{1,0:T(8,128)} %get-tuple-element.40) | copy-start | bytes 1179652

commit v5 on v4

--- a/solution.py
+++ b/solution.py
@@ -29,9 +29,9 @@
     (1, 2, (10,)),
     (2, 1, (11, 12, 13, 14, 15)),
 )
-ORDERS = ("cxyz", "cyxz", "cyzx", "cxyz", "cxyz", "cxyz", "cyxz", "cyxz", "cxyz", "cxyz", "cyxz", "cxyz", "cxyz", "cxyz", "cyxz", "cyxz", "cyxz", "cyxz", ("c", "xyz"))
-SLOTS = {"f4": (0,), "f6": (1,), "f7": (2,), "f8": (3,), "att0": (4,), "att1": (6, 5), "att2": (7, 8), "att3": (0,), "att4": (1,), "att5": (3,), "att6": (2,), "att8": (4, 6), "gq0": (5,), "gq3": (7,), "gq4": (9,), "gq5": (0, 8, 10), "gq6": (2, 11), "gq7": (1, 3, 12), "gn1": (6, 4, 13, 5), "pair0": (7, 17, 8, 0), "pair1": (1, 3, 10, 2), "pair2": (6, 11, 14, 16), "pair3": (15, 4, 5, 9), "pair4": (17, 7, 8, 12), "pair5": (1, 11, 0, 13), "pair6": (3, 10, 6, 2), "pair7": (17, 4, 14, 16), "pair8": (1, 7, 5, 15), "pair9": (11, 6, 8, 12), "pair10": (10, 9, 14, 0), "pair11": (3, 13, 7, 2), "pair12": (11, 17, 16, 4), "pair13": (1, 10, 15, 12), "pair14": (1, 5, 0, 14), "pair15": (3, 6, 13, 8), "small": (17, 3, 9, 7)}
-TAIL = (4, 10, 0, 6, 16, 15, 18, 12, 7, 2, 5, 4, 14, 11, 2, 13, 5, 8, 9, 17, 16, 10, 8, 15, 10, 12, 14, 18, 13, 11, 9, 16, 11, 17, 15, 17, 12, 14, 12, 14, 18, 13, 16, 18, 13, 15, 9, 16, 15, 9)
+ORDERS = ("cyxz", "cxyz", "cxyz", "cyxz", "cxyz", "cyzx", "cxyz", "cxyz", "cyxz", "cxyz", "cyxz", "cyzx", "cyxz", "cxyz", "cxyz", "cyxz", "cxyz", "cxyz", ("c", "xyz"))
+SLOTS = {"f4": (0,), "f6": (1,), "f7": (2,), "f8": (3,), "att0": (4,), "att1": (5, 6), "att2": (7, 8, 0), "att3": (1,), "att4": (3,), "att5": (2,), "att6": (5,), "att7": (4,), "att9": (8, 6), "gq0": (1,), "gq2": (2,), "gq4": (5, 9, 7, 4), "gq5": (10,), "gq6": (0, 11), "gq7": (6, 12), "gq8": (1, 13, 3), "gn1": (5, 4, 7, 16), "pair0": (9, 10, 8, 15), "pair1": (1, 6, 14, 17), "pair2": (0, 2, 4, 13), "pair3": (5, 7, 3, 9), "pair4": (6, 16, 8, 11), "pair5": (0, 1, 10, 15), "pair6": (4, 2, 14, 12), "pair7": (5, 6, 7, 17), "pair8": (0, 16, 3, 13), "pair9": (1, 8, 9, 2), "pair10": (15, 1, 5, 14), "pair11": (4, 7, 10, 5), "pair12": (16, 4, 17, 13), "pair13": (6, 9, 0, 3), "pair14": (8, 6, 15, 11), "pair15": (10, 0, 2, 14), "small": (9, 16, 12, 2)}
+TAIL = (17, 7, 11, 13, 3, 18, 15, 10, 7, 3, 14, 8, 12, 16, 9, 8, 11, 17, 13, 9, 15, 12, 10, 18, 16, 14, 10, 11, 17, 16, 13, 15, 12, 13, 15, 14, 11, 18, 14, 17, 12, 11, 18, 17, 12)
 CHUNK = 8
 PAIRS = CHUNK * T
 
@@ -459,33 +459,37 @@
         off8 = off_ref[at, :]
         hop8 = hopi_ref[at, :]
         edge8 = edgei_ref[at, :]
-        for s in range(0, CHUNK, 2):
-            lanes = pl.ds(pl.multiple_of(c * PAIRS + s * T, 2 * T), 2 * T)
-            z = two(off8, s) * wide(cols_ref[0]) - wide(cols_ref[1])
-            feat = jnp.exp2(wide(cols_ref[2]) - z * z).astype(B16)
-            feat_ref[:, lanes] = feat
-            pre = mm(innert_ref[...], feat)
-            act, slope = gelu_parts(pre)
-            hidden = act.astype(B16)
-            hidden_ref[:, lanes] = hidden
-            slope_ref[:, lanes] = slope
-            hop = two(hop8, s)
-            edge = two(edge8, s)
-            low = mm(w1_ref[...], jnp.concatenate([hidden, hot(hop)], axis=0))
-            high = mm(w2_ref[...], hot(edge))
-            hop_bits = bit_masks(hop >> 7, 2)
-            edge_bits = bit_masks(edge >> 7, 4)
-            bias = jnp.concatenate(
-                [
-                    pick([low[g * HEADS + r : g * HEADS + r + 8] for g in range(4)], hop_bits)
-                    + pick([high[g * HEADS + r : g * HEADS + r + 8] for g in range(12)], edge_bits)
-                    for r in range(0, HEADS, 8)
-                ],
-                axis=0,
-            )
-            base = (c * CHUNK + s) * HEADS
-            bias_ref[pl.ds(pl.multiple_of(base, HEADS), HEADS), :] = bias[:, :T]
-            bias_ref[pl.ds(pl.multiple_of(base + HEADS, HEADS), HEADS), :] = bias[:, T:]
+        for first_pair in range(0, CHUNK, 8):
+            steps = range(first_pair, first_pair + 8, 2)
+            lanes = [pl.ds(pl.multiple_of(c * PAIRS + s * T, 2 * T), 2 * T) for s in steps]
+            highs = [mm(w2_ref[...], hot(two(edge8, s))) for s in steps]
+            pres = []
+            for s, at in zip(steps, lanes):
+                z = two(off8, s) * wide(cols_ref[0]) - wide(cols_ref[1])
+                feat = jnp.exp2(wide(cols_ref[2]) - z * z).astype(B16)
+                feat_ref[:, at] = feat
+                pres.append(mm(innert_ref[...], feat))
+            lows = []
+            for s, at, pre in zip(steps, lanes, pres):
+                act, slope = gelu_parts(pre)
+                hidden = act.astype(B16)
+                hidden_ref[:, at] = hidden
+                slope_ref[:, at] = slope
+                lows.append(mm(w1_ref[...], jnp.concatenate([hidden, hot(two(hop8, s))], axis=0)))
+            for s, low, high in zip(steps, lows, highs):
+                hop_bits = bit_masks(two(hop8, s) >> 7, 2)
+                edge_bits = bit_masks(two(edge8, s) >> 7, 4)
+                bias = jnp.concatenate(
+                    [
+                        pick([low[g * HEADS + r : g * HEADS + r + 8] for g in range(4)], hop_bits)
+                        + pick([high[g * HEADS + r : g * HEADS + r + 8] for g in range(12)], edge_bits)
+                        for r in range(0, HEADS, 8)
+                    ],
+                    axis=0,
+                )
+                base = (c * CHUNK + s) * HEADS
+                bias_ref[pl.ds(pl.multiple_of(base, HEADS), HEADS), :] = bias[:, :T]
+                bias_ref[pl.ds(pl.multiple_of(base + HEADS, HEADS), HEADS), :] = bias[:, T:]
         return 0
 
     lax.fori_loop(0, T // CHUNK, bias_step, 0)
@@ -524,12 +528,24 @@
 
     def attend(half, _):
         mixed_half = [None, None, None]
-        for tile, tiles, heads in GROUPS:
-            lanes = pl.ds(pl.multiple_of(half * W + tile * T, T), tiles * T)
+
+        def lanes_of(group):
+            tile, tiles, _ = GROUPS[group]
+            return pl.ds(pl.multiple_of(half * W + tile * T, T), tiles * T)
+
+        def raw_of(group):
+            tile, tiles, heads = GROUPS[group]
+            q = q_ref[:, lanes_of(group)]
+            qm = [q * head_mask(h, tile, tiles).astype(B16) for h in heads]
+            return mm(jnp.concatenate(qm, axis=0), k_ref[:, lanes_of(group)], NT)
+
+        raw_next = raw_of(0)
+        for group, (tile, tiles, heads) in enumerate(GROUPS):
+            lanes = lanes_of(group)
             masks = [head_mask(h, tile, tiles) for h in heads]
-            q = q_ref[:, lanes]
-            qm = jnp.concatenate([q * m.astype(B16) for m in masks], axis=0)
-            raw = mm(qm, k_ref[:, lanes], NT)
+            raw = raw_next
+            if group + 1 < len(GROUPS):
+                raw_next = raw_of(group + 1)
             probs = []
             for a, h in enumerate(heads):
                 head = half * 16 + h

time: 121 us -> 115 us (0.950)
  Pallas kernels: 119 us -> 113 us
    pallas_call x1, Pallas kernels: 111 us -> 105 us  [run_compute(): pl.pallas_call(compute_kernel, out_shape=out_shape, in_specs=[sspec] + [a...]
where the time goes in v5:
time: 115 us
  Pallas kernels  113 us (98%)
  local copies, waits for them, and re-layouts  1.43 us (1%)
    pallas_call x1, Pallas kernels, run_compute(): pl.pallas_call(compute_kernel, out_shape=out_shape, in_specs=[sspec] + [a...  105 us
    pallas_call x1, Pallas kernels, run_unpack(): pl.pallas_call(unpack_kernel, grid=(D // step,), in_specs=[pl.BlockSpec((...  7.87 us

profile of v5, /device:TPU:0, one launch (start us, length us, event | category | flops | bytes accessed | tf_op | source)
XLA Modules:
  0.0 115.1 jit_solution(6177641028648171239)
XLA Ops:
  0.7 105.1 %layer.1 = (bf16[128,768]{1,0:T(8,128)(2,1)}, f32[128,768]{1,0:T(8,128)}, bf16[4608,128]{1,0:T(8,128)(2,1)}, bf16[4608,128]{1,0:T(8,128)(2,1)}, bf16[4608,128]{1...) custom-call(s32[1,16]{1,0:T(1,128)} %lens_ref.1, ...), custom_call_target="tpu_custom_call" | custom-call | tf_op jit(solution)/shard_map/layer/pallas_call | solution.py:962
  105.7 0.0 copy-start.1
  105.7 0.0 copy-start
  105.7 7.9 %unpack.1 = (f32[768,2304]{1,0:T(8,128)}, f32[768,768]{1,0:T(8,128)}, f32[6,128]{1,0:T(8,128)}, f32[6,128]{1,0:T(8,128)}, f32[768,768]{1,0:T(8,128)}, /*index=5*...) custom-call(bf16[6,768,128]{2,1,0:T(8,128)(2,1)} %bitcast.27, ...), custom_call_target="tpu_custom_call" | custom-call | tf_op jit(solution)/shard_map/unpack/pallas_call | solution.py:861
  113.6 0.0 copy-done.1
  113.6 0.7 copy.39
  114.3 0.0 copy-done
  114.3 0.7 copy.40
Async XLA Ops:
  105.7 7.9 %copy-start.1 = (bf16[128,768]{1,0:T(8,128)(2,1)S(1)}, bf16[128,768]{1,0:T(8,128)(2,1)}, u32[]{:S(2)}) copy-start(bf16[128,768]{1,0:T(8,128)(2,1)} %get-tuple-element.39) | copy-start | bytes 589828
  105.7 8.6 %copy-start = (f32[128,768]{1,0:T(8,128)S(1)}, f32[128,768]{1,0:T(8,128)}, u32[]{:S(2)}) copy-start(f32[128,768]{1,0:T(8,128)} %get-tuple-element.40) | copy-start | bytes 1179652
